TPU v7x, 32 devices: a whole 2x2x4 slice. The times are simulated.
32 devices in a mesh: dp: 8 (over z, x), seq: 4 (over y, core).
Axes of the slice: x: 2, y: 2, z: 4, core: 2. Of those that a mesh axis runs over, the one named last changes fastest.
Arguments:
- latents: bfloat16 [16, 512, 1152], P('dp', 'seq'), may hold values from -16 to 16
- conditioning: bfloat16 [16, 1152], P('dp'), may hold values from -5 to 5
- w_mod: bfloat16 [1152, 6912], P(('dp', 'seq')), may hold values from -0.1875 to 0.1875
- b_mod: bfloat16 [6912], P(('dp', 'seq')), may hold values from -4 to 4
- w_qkv: bfloat16 [1152, 3456], P(('dp', 'seq')), may hold values from -0.1875 to 0.1875
- b_qv: bfloat16 [2304], P(('dp', 'seq')), may hold values from -1.5 to 1.5
- w_out: bfloat16 [1152, 1152], P(('dp', 'seq')), may hold values from -0.75 to 0.75
- b_out: bfloat16 [1152], P(('dp', 'seq')), may hold values from -3 to 3
- w_fc1: bfloat16 [1152, 4608], P(('dp', 'seq')), may hold values from -0.1875 to 0.1875
- b_fc1: bfloat16 [4608], P(('dp', 'seq')), may hold values from -3 to 3
- w_fc2: bfloat16 [4608, 1152], P(('dp', 'seq')), may hold values from -0.09375 to 0.09375
- b_fc2: bfloat16 [1152], P(('dp', 'seq')), may hold values from -3 to 3
- out_grad: bfloat16 [16, 512, 1152], P('dp', 'seq'), may hold values from -6 to 6
Outputs:
- output: bfloat16 [16, 512, 1152], P('dp', 'seq')
- latents_grad: bfloat16 [16, 512, 1152], P('dp', 'seq')
- conditioning_grad: bfloat16 [16, 1152], P('dp')
- w_mod_grad: float32 [1152, 6912], P(('dp', 'seq'))
- b_mod_grad: float32 [6912], P(('dp', 'seq'))
- w_qkv_grad: float32 [1152, 3456], P(('dp', 'seq'))
- b_qv_grad: float32 [2304], P(('dp', 'seq'))
- w_out_grad: float32 [1152, 1152], P(('dp', 'seq'))
- b_out_grad: float32 [1152], P(('dp', 'seq'))
- w_fc1_grad: float32 [1152, 4608], P(('dp', 'seq'))
- b_fc1_grad: float32 [4608], P(('dp', 'seq'))
- w_fc2_grad: float32 [4608, 1152], P(('dp', 'seq'))
- b_fc2_grad: float32 [1152], P(('dp', 'seq'))
All inputs are finite; a program needn't handle non-finite values.
Results may differ from a plain program's by a relative error of at most 0.015.
The roundings to bfloat16 on the way count: a program that leaves them out, or rounds other values in their place, can miss the bound.
Values may be sent and summed in bfloat16 or wider, within the bound.
A program may use at most 320 MiB of HBM per device.

v0:
```python
from functools import partial

import jax
import jax.numpy as jnp
from jax import lax
from jax.sharding import PartitionSpec as P

HEADS = 16
HEAD_DIM = 72


EPSILON = 1e-06


def layer_norm(values):
    center = values - jnp.mean(values, axis=-1, keepdims=True)
    inverse = lax.rsqrt(jnp.mean(center * center, axis=-1, keepdims=True) + EPSILON)
    return (center * inverse, inverse)


def norm_back(incoming, normed, inverse):
    return inverse * (
        incoming
        - jnp.mean(incoming, axis=-1, keepdims=True)
        - normed * jnp.mean(incoming * normed, axis=-1, keepdims=True)
    )


def split_heads(values):
    return values.reshape(values.shape[0], HEADS, HEAD_DIM)


def attend(queries, key_rows, values):
    head_q = split_heads(queries)
    head_k = split_heads(key_rows)
    head_v = split_heads(values)
    scores = jnp.einsum(
        "qhd,khd->hqk", head_q, head_k, preferred_element_type=jnp.float32
    ) * HEAD_DIM ** (-0.5)
    row_max = jnp.max(scores, axis=-1, keepdims=True)
    expon = jnp.exp(scores - row_max)
    row_total = jnp.sum(expon, axis=-1, keepdims=True)
    soft_weights = expon / row_total
    mixed_heads = jnp.einsum(
        "hqk,khd->qhd",
        soft_weights.astype(jnp.bfloat16),
        head_v,
        preferred_element_type=jnp.float32,
    )
    log_total = (row_max + jnp.log(row_total))[..., 0]
    return (mixed_heads.reshape(queries.shape[0], -1), log_total)


def attend_back(queries, key_rows, values, log_total, grad_mixed):
    head_q = split_heads(queries)
    head_k = split_heads(key_rows)
    head_v = split_heads(values)
    grad_heads = split_heads(grad_mixed)
    scale_factor = HEAD_DIM ** (-0.5)
    scores = (
        jnp.einsum("qhd,khd->hqk", head_q, head_k, preferred_element_type=jnp.float32)
        * scale_factor
    )
    soft_weights = jnp.exp(scores - log_total[..., None])
    grad_soft = jnp.einsum("qhd,khd->hqk", grad_heads, head_v, preferred_element_type=jnp.float32)
    row_delta = jnp.sum(soft_weights * grad_soft, axis=-1, keepdims=True)
    grad_scores = (soft_weights * (grad_soft - row_delta)).astype(jnp.bfloat16)
    grad_queries = (
        jnp.einsum("hqk,khd->qhd", grad_scores, head_k, preferred_element_type=jnp.float32)
        * scale_factor
    )
    grad_keys = (
        jnp.einsum("hqk,qhd->khd", grad_scores, head_q, preferred_element_type=jnp.float32)
        * scale_factor
    )
    grad_values = jnp.einsum(
        "hqk,qhd->khd",
        soft_weights.astype(jnp.bfloat16),
        grad_heads,
        preferred_element_type=jnp.float32,
    )
    return (
        grad_queries.reshape(queries.shape[0], -1),
        grad_keys.reshape(key_rows.shape[0], -1),
        grad_values.reshape(values.shape[0], -1),
    )


def flatten_rows(values):
    return values.reshape(-1, values.shape[-1])


def body(
    latents,
    conditioning,
    w_mod,
    b_mod,
    w_qkv,
    b_qv,
    w_out,
    b_out,
    w_fc1,
    b_fc1,
    w_fc2,
    b_fc2,
    out_grad,
):
    latent_count, seq_rows, model_width = latents.shape
    full_qkv, full_out, full_fc1, full_fc2, bias_qv, bias_out, bias_fc1, bias_fc2, bias_mod = (
        lax.all_gather(w_qkv, ("dp", "seq"), axis=0, tiled=True),
        lax.all_gather(w_out, ("dp", "seq"), axis=0, tiled=True),
        lax.all_gather(w_fc1, ("dp", "seq"), axis=0, tiled=True),
        lax.all_gather(w_fc2, ("dp", "seq"), axis=0, tiled=True),
        lax.all_gather(b_qv, ("dp", "seq"), axis=0, tiled=True),
        lax.all_gather(b_out, ("dp", "seq"), axis=0, tiled=True),
        lax.all_gather(b_fc1, ("dp", "seq"), axis=0, tiled=True),
        lax.all_gather(b_fc2, ("dp", "seq"), axis=0, tiled=True),
        lax.all_gather(b_mod, ("dp", "seq"), axis=0, tiled=True),
    )
    cond_act, silu_back = jax.vjp(jax.nn.silu, conditioning.astype(jnp.float32))
    cond_low = cond_act.astype(jnp.bfloat16)
    full_mod = lax.all_gather(w_mod, ("dp", "seq"), axis=0, tiled=True)
    modulation = jnp.dot(cond_low, full_mod, preferred_element_type=jnp.float32) + bias_mod.astype(
        jnp.float32
    )
    bias_qv_float = bias_qv.astype(jnp.float32)
    bias_out_float = bias_out.astype(jnp.float32)
    bias_fc1_float = bias_fc1.astype(jnp.float32)
    bias_fc2_float = bias_fc2.astype(jnp.float32)

    def micro_batch(totals, inputs):
        latent_low, grad_low, mod_row = inputs
        shift_att, scale_att, gate_att, shift_mlp, scale_mlp, gate_mlp = [
            mod_row[offset * model_width : (offset + 1) * model_width] for offset in range(6)
        ]
        tokens = latent_low.astype(jnp.float32)
        normed, inverse = layer_norm(tokens)
        modded = (normed * (1.0 + scale_att) + shift_att).astype(jnp.bfloat16)
        joined = jnp.dot(modded, full_qkv, preferred_element_type=jnp.float32)
        queries = (joined[:, :model_width] + bias_qv_float[:model_width]).astype(jnp.bfloat16)
        key_rows = joined[:, model_width : 2 * model_width].astype(jnp.bfloat16)
        values = (joined[:, 2 * model_width :] + bias_qv_float[model_width:]).astype(jnp.bfloat16)
        keys_all, values_all = (
            lax.all_gather(key_rows, "seq", axis=0, tiled=True),
            lax.all_gather(values, "seq", axis=0, tiled=True),
        )
        mixed_heads, log_total = attend(queries, keys_all, values_all)
        mixed_low = mixed_heads.astype(jnp.bfloat16)
        attended = jnp.dot(mixed_low, full_out, preferred_element_type=jnp.float32) + bias_out_float
        middle = tokens + gate_att * attended
        normed_two, inverse_two = layer_norm(middle)
        modded_two = (normed_two * (1.0 + scale_mlp) + shift_mlp).astype(jnp.bfloat16)
        hidden = jnp.dot(modded_two, full_fc1, preferred_element_type=jnp.float32) + bias_fc1_float
        active, gelu_back = jax.vjp(partial(jax.nn.gelu, approximate=True), hidden)
        active_low = active.astype(jnp.bfloat16)
        branch = jnp.dot(active_low, full_fc2, preferred_element_type=jnp.float32) + bias_fc2_float
        output = middle + gate_mlp * branch
        grad_output = grad_low.astype(jnp.float32)
        grad_gate_mlp = jnp.sum(grad_output * branch, axis=0)
        grad_branch = (gate_mlp * grad_output).astype(jnp.bfloat16)
        grad_bias_fc2 = jnp.sum(grad_branch.astype(jnp.float32), axis=0)
        grad_active = jnp.einsum(
            "td,fd->tf", grad_branch, full_fc2, preferred_element_type=jnp.float32
        )
        grad_hidden = gelu_back(grad_active)[0].astype(jnp.bfloat16)
        grad_bias_fc1 = jnp.sum(grad_hidden.astype(jnp.float32), axis=0)
        grad_modded_two = jnp.einsum(
            "tf,df->td", grad_hidden, full_fc1, preferred_element_type=jnp.float32
        )
        grad_shift_mlp = jnp.sum(grad_modded_two, axis=0)
        grad_scale_mlp = jnp.sum(grad_modded_two * normed_two, axis=0)
        grad_middle = grad_output + norm_back(
            grad_modded_two * (1.0 + scale_mlp), normed_two, inverse_two
        )
        grad_gate_att = jnp.sum(grad_middle * attended, axis=0)
        grad_attended = (gate_att * grad_middle).astype(jnp.bfloat16)
        grad_bias_out = jnp.sum(grad_attended.astype(jnp.float32), axis=0)
        grad_mixed = jnp.einsum(
            "te,de->td", grad_attended, full_out, preferred_element_type=jnp.float32
        ).astype(jnp.bfloat16)
        grad_queries, grad_keys_all, grad_values_all = attend_back(
            queries, keys_all, values_all, log_total, grad_mixed
        )
        grad_keys, grad_values = (
            lax.psum_scatter(grad_keys_all, "seq", scatter_dimension=0, tiled=True),
            lax.psum_scatter(grad_values_all, "seq", scatter_dimension=0, tiled=True),
        )
        grad_joined = jnp.concatenate(
            [
                grad_queries.astype(jnp.bfloat16),
                grad_keys.astype(jnp.bfloat16),
                grad_values.astype(jnp.bfloat16),
            ],
            axis=-1,
        )
        joined_sums = jnp.sum(grad_joined.astype(jnp.float32), axis=0)
        grad_bias_qv = jnp.concatenate([joined_sums[:model_width], joined_sums[2 * model_width :]])
        grad_modded = jnp.einsum(
            "te,de->td", grad_joined, full_qkv, preferred_element_type=jnp.float32
        )
        grad_shift_att = jnp.sum(grad_modded, axis=0)
        grad_scale_att = jnp.sum(grad_modded * normed, axis=0)
        grad_tokens = grad_middle + norm_back(grad_modded * (1.0 + scale_att), normed, inverse)
        grad_mod_part = jnp.concatenate(
            [
                grad_shift_att,
                grad_scale_att,
                grad_gate_att,
                grad_shift_mlp,
                grad_scale_mlp,
                grad_gate_mlp,
            ],
            axis=-1,
        )
        sums = (grad_bias_qv, grad_bias_out, grad_bias_fc1, grad_bias_fc2)
        totals = tuple((total + term for total, term in zip(totals, sums)))
        kept = (
            modded,
            grad_joined,
            mixed_low,
            grad_attended,
            modded_two,
            grad_hidden,
            active_low,
            grad_branch,
        )
        return (
            totals,
            (output.astype(jnp.bfloat16), grad_tokens.astype(jnp.bfloat16), grad_mod_part, kept),
        )

    starting = tuple(
        (
            jnp.zeros(shape, jnp.float32)
            for shape in (bias_qv.shape, bias_out.shape, bias_fc1.shape, bias_fc2.shape)
        )
    )
    totals, (output, grad_tokens, grad_mod_parts, kept) = lax.scan(
        micro_batch, starting, (latents, out_grad, modulation)
    )
    (
        kept_modded,
        kept_joined,
        kept_mixed,
        kept_attended,
        kept_modded_two,
        kept_hidden,
        kept_active,
        kept_branch,
    ) = [flatten_rows(item) for item in kept]
    count = lax.axis_size(("dp", "seq")) * w_qkv.shape[0]

    def columns(values):
        return lax.slice_in_dim(values, 0, count, axis=1)

    row_sums = lax.psum_scatter(
        jnp.concatenate(
            [
                jnp.einsum(
                    "td,te->de",
                    columns(kept_modded),
                    kept_joined,
                    preferred_element_type=jnp.float32,
                ),
                jnp.einsum(
                    "td,te->de",
                    columns(kept_mixed),
                    kept_attended,
                    preferred_element_type=jnp.float32,
                ),
                jnp.einsum(
                    "td,tf->df",
                    columns(kept_modded_two),
                    kept_hidden,
                    preferred_element_type=jnp.float32,
                ),
            ],
            axis=1,
        ),
        ("dp", "seq"),
        scatter_dimension=0,
        tiled=True,
    )
    sums_qkv = row_sums[:, : 3 * model_width]
    sums_out = row_sums[:, 3 * model_width : 4 * model_width]
    sums_fc1 = row_sums[:, 4 * model_width :]
    active_cols = lax.slice_in_dim(
        kept_active, 0, lax.axis_size(("dp", "seq")) * w_fc2.shape[0], axis=1
    )
    sums_fc2 = lax.psum_scatter(
        jnp.einsum("tf,td->fd", active_cols, kept_branch, preferred_element_type=jnp.float32),
        ("dp", "seq"),
        scatter_dimension=0,
        tiled=True,
    )
    grad_mod = lax.psum(grad_mod_parts, "seq").astype(jnp.bfloat16)
    leader = (lax.axis_index("seq") == 0).astype(jnp.float32)
    bias_term = jnp.sum(grad_mod.astype(jnp.float32), axis=0) * leader
    sums_bias_qv, sums_bias_out, sums_bias_fc1, sums_bias_fc2, sums_bias_mod = (
        lax.psum_scatter(totals[0], ("dp", "seq"), scatter_dimension=0, tiled=True),
        lax.psum_scatter(totals[1], ("dp", "seq"), scatter_dimension=0, tiled=True),
        lax.psum_scatter(totals[2], ("dp", "seq"), scatter_dimension=0, tiled=True),
        lax.psum_scatter(totals[3], ("dp", "seq"), scatter_dimension=0, tiled=True),
        lax.psum_scatter(bias_term, ("dp", "seq"), scatter_dimension=0, tiled=True),
    )
    grad_mod_rows = lax.psum_scatter(
        jnp.einsum("bd,be->de", cond_low, grad_mod, preferred_element_type=jnp.float32) * leader,
        ("dp", "seq"),
        scatter_dimension=0,
        tiled=True,
    )
    grad_cond_act = jnp.einsum("be,de->bd", grad_mod, full_mod, preferred_element_type=jnp.float32)
    grad_cond = silu_back(grad_cond_act)[0]
    return (
        output,
        grad_tokens,
        grad_cond.astype(jnp.bfloat16),
        grad_mod_rows,
        sums_bias_mod,
        sums_qkv,
        sums_bias_qv,
        sums_out,
        sums_bias_out,
        sums_fc1,
        sums_bias_fc1,
        sums_fc2,
        sums_bias_fc2,
    )


def solution(mesh):
    in_specs = (
        P("dp", "seq", None),
        P("dp", None),
        P(("dp", "seq"), None),
        P(("dp", "seq")),
        P(("dp", "seq"), None),
        P(("dp", "seq")),
        P(("dp", "seq"), None),
        P(("dp", "seq")),
        P(("dp", "seq"), None),
        P(("dp", "seq")),
        P(("dp", "seq"), None),
        P(("dp", "seq")),
        P("dp", "seq", None),
    )
    out_specs = (
        P("dp", "seq", None),
        P("dp", "seq", None),
        P("dp", None),
        P(("dp", "seq"), None),
        P(("dp", "seq")),
        P(("dp", "seq"), None),
        P(("dp", "seq")),
        P(("dp", "seq"), None),
        P(("dp", "seq")),
        P(("dp", "seq"), None),
        P(("dp", "seq")),
        P(("dp", "seq"), None),
        P(("dp", "seq")),
    )
    return jax.shard_map(body, mesh=mesh, in_specs=in_specs, out_specs=out_specs, check_vma=False)
```

profile of v0, /device:TPU:4, one launch (start us, length us, event | category | flops | bytes accessed | tf_op | source)
XLA Modules:
  0.0 1960.8 jit_solution(7344270771863397746)
XLA Ops:
  15.0 42.2 %all-reduce.14 = (bf16[6912]{0:T(1024)(128)(2,1)S(1)}, bf16[2304]{0:T(1024)(128)(2,1)S(1)}, bf16[1152]{0:T(1024)(128)(2,1)S(1)}, bf16[4608]{0:T(1024)(128)(2,1)S(1)}, bf16[1152]{0:T(1024)(128)(2,1)S(1)}) all-reduce(bf16[6912]{0:T(1024)(128)(2,1)S(1)} %dynamic-update-slice, ...), channel_id=1, replica_groups=mesh['dp'=8,'seq'=4] {'dp','seq'}, use_global_device_ids=true, to_apply=%add | all-reduce | flops 16128 | bytes 64512
  59.0 11.8 all-gather.18.cloned.1.call-done
  70.8 5.1 reshape.230
  76.0 75.9 %all-gather.16.cloned.1.call-done = bf16[32,36,3456]{2,1,0:T(8,128)(2,1)} async-done(((bf16[1,36,3456]{2,1,0:T(8,128)(2,1)}), bf16[32,36,3456]{2,1,0:T(8,128)(2,1)}) %all-gather.16.cloned.1.call-update) | async-done | bytes 7962640 | tf_op jit(solution)/shard_map/all_gather | solution.py:110
  151.8 12.5 reshape.228
  164.3 81.5 %all-gather.20.cloned.1.call-done = bf16[32,36,4608]{2,1,0:T(8,128)(2,1)} async-done(((bf16[1,36,4608]{2,1,0:T(8,128)(2,1)}), bf16[32,36,4608]{2,1,0:T(8,128)(2,1)}) %all-gather.20.cloned.1.call-update) | async-done | bytes 10616848 | tf_op jit(solution)/shard_map/all_gather | solution.py:112
  245.8 14.1 reshape.232
  259.9 106.4 %all-gather.14.cloned.1.call-done = bf16[32,36,6912]{2,1,0:T(8,128)(2,1)} async-done(((bf16[1,36,6912]{2,1,0:T(8,128)(2,1)}), bf16[32,36,6912]{2,1,0:T(8,128)(2,1)}) %all-gather.14.cloned.1.call-update) | async-done | bytes 15925264 | tf_op jit(solution)/shard_map/all_gather | solution.py:122
  366.2 18.4 reshape.226
  384.7 8.4 convolution_add_fusion.3
  393.1 61.4 %all-gather.12.cloned.1.call-done = bf16[4608,1152]{1,0:T(8,128)(2,1)} async-done(((bf16[144,1152]{1,0:T(8,128)(2,1)}), bf16[4608,1152]{1,0:T(8,128)(2,1)}) %all-gather.12.cloned.1.call-update) | async-done | bytes 10616848 | tf_op jit(solution)/shard_map/all_gather | solution.py:113
  454.5 346.7 %while.41 = (s32[]{:T(128)}, f32[2304]{0:T(1024)}, f32[1152]{0:T(1024)}, f32[4608]{0:T(1024)S(1)}, f32[1152]{0:T(1024)}, /*index=5*/bf16[2,128,1152]{2,1,0:T(8,1...) while((s32[]{:T(128)}, f32[2304]{0:T(1024)}, ...), condition=%wide.region_24.25_spmd.clone, body=%wide.region_0.24_spmd.clone.sunk | while | flops 9130084352 | bytes 352600960 | solution.py:238
  471.8 4.7 fusion.185
  478.4 13.8 all-gather.24.cloned.1.call-done
  497.9 13.9 all-gather.22.cloned.1.call-done
  514.4 4.0 fusion.189
  522.0 4.4 bitcast_dynamic-update-slice_fusion.9
  527.9 8.6 convert_reduce_fusion.11
  540.2 7.4 bitcast_dynamic-update-slice_fusion.10
  550.2 4.6 fusion.191
  556.1 3.9 multiply_reduce_fusion.16
  570.6 17.5 reduce-scatter.8.cloned.1.call-done
  589.2 34.7 %reduce-scatter.10.cloned.1.call-done = f32[128,1152]{0,1:T(8,128)} async-done(((f32[512,1152]{0,1:T(8,128)}), f32[128,1152]{0,1:T(8,128)}) %reduce-scatter.10.cloned.1.call-update) | async-done | bytes 589840 | tf_op jit(solution)/shard_map/while/body/eval_jaxpr/reduce_scatter | solution.py:185
  625.4 6.0 fusion.195
  635.8 4.7 fusion.185
  642.5 16.5 all-gather.24.cloned.1.call-done
  664.6 13.9 all-gather.22.cloned.1.call-done
  681.1 4.0 fusion.189
  688.8 4.4 bitcast_dynamic-update-slice_fusion.9
  694.6 8.6 convert_reduce_fusion.11
  707.0 7.4 bitcast_dynamic-update-slice_fusion.10
  717.0 4.6 fusion.191
  737.3 17.5 reduce-scatter.8.cloned.1.call-done
  755.9 34.7 %reduce-scatter.10.cloned.1.call-done = f32[128,1152]{0,1:T(8,128)} async-done(((f32[512,1152]{0,1:T(8,128)}), f32[128,1152]{0,1:T(8,128)}) %reduce-scatter.10.cloned.1.call-update) | async-done | bytes 589840 | tf_op jit(solution)/shard_map/while/body/eval_jaxpr/reduce_scatter | solution.py:185
  792.2 6.0 fusion.195
  801.3 4.7 convolution_bitcast_fusion.3
  806.0 7.8 convolution_bitcast_fusion.2
  813.8 11.7 convolution_bitcast_fusion.1
  825.5 28.7 %pad_maximum_fusion.2 = f32[1152,9216]{1,0:T(8,128)} fusion(f32[1152,4608]{1,0:T(8,128)} %convolution_bitcast_fusion.1, f32[1152,1152]{1,0:T(8,128)} %convolution_bitcast_fusion.3, f32[1152,3456]{1,0:T(8,128)} %convolution_bitcast_fusion.2), kind=kLoop, calls=%fused_computation.134 | loop fusion | flops 21233664 | bytes 84934656 | tf_op jit(solution)/shard_map/concatenate | solution.py:257
  856.0 9.6 convolution_bitcast_fusion
  866.5 13.4 psum.7
  879.9 12.9 convolution_multiply_fusion.2
  892.7 515.5 %fusion = f32[40,6912]{1,0:T(8,128)S(1)} fusion(f32[1152,6912]{1,0:T(8,128)} %convolution_multiply_fusion.2), kind=kCustom, calls=%all-reduce-scatter | all-reduce-scatter fusion | flops 8847361 | bytes 32956416
  1416.4 10.4 fusion.77
  1426.8 106.8 %all-reduce.13 = (f32[6912]{0:T(1024)S(1)}, f32[2304]{0:T(1024)S(1)}, f32[1152]{0:T(1024)S(1)}, f32[4608]{0:T(1024)S(1)}, f32[1152]{0:T(1024)S(1)}) all-reduce(f32[6912]{0:T(1024)S(1)} %broadcast_multiply_fusion.6, f32[2304]{0:T(1024)S(1)} %copy-done.33, ...), channel_id=5, replica_groups=mesh['dp'=8,'seq'=4] {'dp','seq'}, use_global_device_ids=true, to_apply=%region_28.29.clone | all-reduce | flops 16128 | bytes 129024
  1536.7 21.9 %concatenate.25 = f32[164,6912]{1,0:T(8,128)} concatenate(f32[4,6912]{1,0:T(4,128)} %collective-permute-done.3, f32[40,6912]{1,0:T(8,128)S(1)} %collective-permute-done.2, f32[40,6912]{1,0:T(8,128)S(1)} %collective-permute-done.1, f32[40,6912]{1,0:T(8,128)} %collective-permute-done, f32[40,6912]{1,0:T(8,128)S(1)} %fusion), dimensions={0} | concatenate | bytes 9068544
  1561.0 166.1 %all-reduce.17.cloned.1.call-done = f32[1152,9216]{1,0:T(8,128)} async-done(((f32[1152,9216]{1,0:T(8,128)}), f32[1152,9216]{1,0:T(8,128)}) %all-reduce.17.cloned.1.call-update) | async-done | bytes 42467344
  1733.1 220.9 %reduce-scatter.6.cloned.1.call-done = f32[144,1152]{1,0:T(8,128)} async-done(((f32[4608,1152]{1,0:T(8,128)}), f32[144,1152]{1,0:T(8,128)}) %reduce-scatter.6.cloned.1.call-update) | async-done | bytes 663568 | tf_op jit(solution)/shard_map/reduce_scatter | solution.py:290
  (383 shorter events, 114.7 us)
Async XLA Ops:
  7.2 63.6 %all-gather.18.cloned.1.call-start = ((), (), s32[]{:S(2)}) async-start(), calls=%async_computation.7 | async-start | bytes 3041280 | tf_op jit(solution)/shard_map/all_gather | solution.py:111
  7.9 143.9 %all-gather.16.cloned.1.call-start = ((), (), s32[]{:S(2)}) async-start(), calls=%async_computation.6 | async-start | bytes 9123840 | tf_op jit(solution)/shard_map/all_gather | solution.py:110
  8.7 237.1 %all-gather.20.cloned.1.call-start = ((), (), s32[]{:S(2)}) async-start(), calls=%async_computation.8 | async-start | bytes 12165120 | tf_op jit(solution)/shard_map/all_gather | solution.py:112
  9.4 356.8 %all-gather.14.cloned.1.call-start = ((), (), s32[]{:S(2)}) async-start(), calls=%async_computation.5 | async-start | bytes 18247680 | tf_op jit(solution)/shard_map/all_gather | solution.py:122
  10.0 444.6 %all-gather.12.cloned.1.call-start = ((), (), s32[]{:S(2)}) async-start(), calls=%async_computation.3 | async-start | bytes 10948608 | tf_op jit(solution)/shard_map/all_gather | solution.py:113
  259.8 124.8 %copy-start.44 = (bf16[2,1152]{1,0:T(2,128)(2,1)S(1)}, bf16[2,1152]{1,0:T(2,128)(2,1)}, u32[]{:S(2)}) copy-start(bf16[2,1152]{1,0:T(2,128)(2,1)} %param.16) | copy-start | bytes 13828
  384.7 69.9 %copy-start.6 = (bf16[2,128,1152]{2,1,0:T(8,128)(2,1)S(1)}, bf16[2,128,1152]{2,1,0:T(8,128)(2,1)}, u32[]{:S(2)}) copy-start(bf16[2,128,1152]{2,1,0:T(8,128)(2,1)} %param.15) | copy-start | bytes 1769476
  470.4 21.8 %all-gather.24.cloned.1.call-start = ((), (), s32[]{:S(2)}) async-start(), calls=%async_computation.11 | async-start | bytes 1474560 | tf_op jit(solution)/shard_map/while/body/eval_jaxpr/all_gather | solution.py:144
  477.3 34.6 %all-gather.22.cloned.1.call-start = ((), (), s32[]{:S(2)}) async-start(), calls=%async_computation.10 | async-start | bytes 1474560 | tf_op jit(solution)/shard_map/while/body/eval_jaxpr/all_gather | solution.py:145
  478.1 109.9 %reduce-scatter.8.cloned.1.call-start = ((), (), s32[]{:S(2)}) async-start(), calls=%async_computation.12 | async-start | bytes 2949120 | tf_op jit(solution)/shard_map/while/body/eval_jaxpr/reduce_scatter | solution.py:186
  478.4 16.2 copy-start.8
  511.8 10.2 slice-start
  514.4 7.6 slice-start.1
  514.4 7.6 slice-start.2
  554.9 69.0 %reduce-scatter.10.cloned.1.call-start = ((), (), s32[]{:S(2)}) async-start(), calls=%async_computation.13 | async-start | bytes 2949120 | tf_op jit(solution)/shard_map/while/body/eval_jaxpr/reduce_scatter | solution.py:185
  569.4 55.6 %copy-start.10 = (bf16[16,72,128]{2,1,0:T(8,128)(2,1)S(1)}, bf16[16,72,128]{2,1,0:T(8,128)(2,1)}, u32[]{:S(2)}) copy-start(bf16[16,72,128]{2,1,0:T(8,128)(2,1)} %fusion.192) | copy-start | bytes 884740 | tf_op jit(solution)/shard_map/while
  569.4 55.9 %copy-start.7 = (bf16[2,128,1152]{2,1,0:T(8,128)(2,1)S(1)}, bf16[2,128,1152]{2,1,0:T(8,128)(2,1)}, u32[]{:S(2)}) copy-start(bf16[2,128,1152]{2,1,0:T(8,128)(2,1)} %get-tuple-element.1060) | copy-start | bytes 1769476 | tf_op jit(solution)/shard_map/while
  569.4 55.9 %copy-start.35 = (f32[128]{0:T(128)S(1)}, f32[128]{0:T(128)}, u32[]{:S(2)}) copy-start(f32[128]{0:T(128)} %copy-done.34) | copy-start | bytes 1540 | tf_op jit(solution)/shard_map/while
  569.4 55.9 %copy-start.43 = (f32[128]{0:T(128)S(1)}, f32[128]{0:T(128)}, u32[]{:S(2)}) copy-start(f32[128]{0:T(128)} %copy-done.42) | copy-start | bytes 1540 | tf_op jit(solution)/shard_map/while
  625.4 6.2 copy-start.19
  625.4 7.6 copy-start.46
  625.4 7.8 copy-start.31
  634.5 24.5 %all-gather.24.cloned.1.call-start = ((), (), s32[]{:S(2)}) async-start(), calls=%async_computation.11 | async-start | bytes 1474560 | tf_op jit(solution)/shard_map/while/body/eval_jaxpr/all_gather | solution.py:144
  641.3 37.3 %all-gather.22.cloned.1.call-start = ((), (), s32[]{:S(2)}) async-start(), calls=%async_computation.10 | async-start | bytes 1474560 | tf_op jit(solution)/shard_map/while/body/eval_jaxpr/all_gather | solution.py:145
  642.2 112.6 %reduce-scatter.8.cloned.1.call-start = ((), (), s32[]{:S(2)}) async-start(), calls=%async_computation.12 | async-start | bytes 2949120 | tf_op jit(solution)/shard_map/while/body/eval_jaxpr/reduce_scatter | solution.py:186
  642.5 18.9 copy-start.8
  678.6 10.2 slice-start
  681.1 7.6 slice-start.1
  681.1 7.6 slice-start.2
  721.6 69.0 %reduce-scatter.10.cloned.1.call-start = ((), (), s32[]{:S(2)}) async-start(), calls=%async_computation.13 | async-start | bytes 2949120 | tf_op jit(solution)/shard_map/while/body/eval_jaxpr/reduce_scatter | solution.py:185
  736.2 55.6 %copy-start.10 = (bf16[16,72,128]{2,1,0:T(8,128)(2,1)S(1)}, bf16[16,72,128]{2,1,0:T(8,128)(2,1)}, u32[]{:S(2)}) copy-start(bf16[16,72,128]{2,1,0:T(8,128)(2,1)} %fusion.192) | copy-start | bytes 884740 | tf_op jit(solution)/shard_map/while
  736.2 55.9 %copy-start.7 = (bf16[2,128,1152]{2,1,0:T(8,128)(2,1)S(1)}, bf16[2,128,1152]{2,1,0:T(8,128)(2,1)}, u32[]{:S(2)}) copy-start(bf16[2,128,1152]{2,1,0:T(8,128)(2,1)} %get-tuple-element.1060) | copy-start | bytes 1769476 | tf_op jit(solution)/shard_map/while
  736.2 55.9 %copy-start.35 = (f32[128]{0:T(128)S(1)}, f32[128]{0:T(128)}, u32[]{:S(2)}) copy-start(f32[128]{0:T(128)} %copy-done.34) | copy-start | bytes 1540 | tf_op jit(solution)/shard_map/while
  736.2 55.9 %copy-start.43 = (f32[128]{0:T(128)S(1)}, f32[128]{0:T(128)}, u32[]{:S(2)}) copy-start(f32[128]{0:T(128)} %copy-done.42) | copy-start | bytes 1540 | tf_op jit(solution)/shard_map/while
  792.1 6.2 copy-start.19
  792.1 7.6 copy-start.46
  792.2 7.8 copy-start.31
  801.2 926.0 %all-reduce.17.cloned.1.call-start = ((), (), s32[]{:S(2)}) async-start(), calls=%async_computation.9 | async-start | bytes 84934656
  806.0 7.8 copy-start.28
  854.3 1099.7 %reduce-scatter.6.cloned.1.call-start = ((), (), s32[]{:S(2)}) async-start(), calls=%async_computation.4 | async-start | bytes 21897216 | tf_op jit(solution)/shard_map/reduce_scatter | solution.py:290
  865.7 14.2 copy-start.45
  1408.9 127.7 %collective-permute-start.2 = (f32[40,6912]{1,0:T(8,128)S(1)}, f32[40,6912]{1,0:T(8,128)S(1)}, u32[]{:S(2)}, u32[]{:S(2)}) collective-permute-start(f32[40,6912]{1,0:T(8,128)S(1)} %fusion), channel_id=1, source_target_pairs={{0,3},{1,4},{2,5},{3,6},{4,7},{5,8},{6,9},{7,10},{8,11},{9,12},{10... | collective-permute-start | bytes 3317768
  1410.3 126.4 %collective-permute-start.1 = (f32[40,6912]{1,0:T(8,128)S(1)}, f32[40,6912]{1,0:T(8,128)S(1)}, u32[]{:S(2)}, u32[]{:S(2)}) collective-permute-start(f32[40,6912]{1,0:T(8,128)S(1)} %fusion), channel_id=1, source_target_pairs={{0,2},{1,3},{2,4},{3,5},{4,6},{5,7},{6,8},{7,9},{8,10},{9,11},{10,... | collective-permute-start | bytes 3317768
  1412.2 124.4 %collective-permute-start = (f32[40,6912]{1,0:T(8,128)S(1)}, f32[40,6912]{1,0:T(8,128)}, u32[]{:S(2)}, u32[]{:S(2)}) collective-permute-start(f32[40,6912]{1,0:T(8,128)S(1)} %fusion), channel_id=1, source_target_pairs={{0,1},{1,2},{2,3},{3,4},{4,5},{5,6},{6,7},{7,8},{8,9},{9,10},{10,1... | collective-permute-start | bytes 3317768
  1414.2 122.5 %collective-permute-start.3 = (f32[4,6912]{1,0:T(4,128)}, f32[4,6912]{1,0:T(4,128)}, u32[]{:S(2)}, u32[]{:S(2)}) collective-permute-start(f32[4,6912]{1,0:T(4,128)} %slice.115), channel_id=1, source_target_pairs={{0,4},{1,5},{2,6},{3,7},{4,8},{5,9},{6,10},{7,11},{8,12},{9,13},{1... | collective-permute-start | bytes 331784
  1416.4 10.4 copy-start.33
  1416.4 10.4 copy-start.38
  1416.4 10.4 copy-start.41
  (71 other events, 201.2 us)
Sparse Core Ops, SparseCore 0:
  10.8 59.9 all-gather.17
  73.6 78.1 all-gather.15
  154.7 91.0 all-gather.19
  248.6 117.6 all-gather.13
  369.0 85.5 all-gather.11
  477.4 14.7 all-gather.23
  494.3 17.4 all-gather.21
  555.0 33.0 reduce-scatter.7
  590.8 33.0 reduce-scatter.9
  641.5 17.4 all-gather.23
  661.1 17.4 all-gather.21
  721.8 33.0 reduce-scatter.7
  757.5 33.0 reduce-scatter.9
  854.4 872.6 all-reduce.16
  1735.1 218.8 reduce-scatter.5
where the time goes:
time: 1970 us; the launch traced here: 1960 us
  waiting for transfers between devices  890 us (45%)
  blocking collectives  678 us (34%)
  matrix products  177 us (9%)
  local copies, waits for them, and re-layouts  121 us (6%)
  other arithmetic  55.6 us (3%)
    unnamed x3, blocking collectives  664 us
    reduce_scatter x1, waiting for transfers between devices, body(): lax.psum_scatter(jnp.einsum('tf,td->fd', active_cols, kept_branch, prefer...  221 us
    unnamed x12, waiting for transfers between devices  169 us
    all_gather x1, waiting for transfers between devices, body(): full_mod = lax.all_gather(w_mod, ('dp', 'seq'), axis=0, tiled=True)  106 us
    unnamed x46, local copies, waits for them, and re-layouts  84.9 us
    all_gather x1, waiting for transfers between devices, body(): lax.all_gather(w_fc1, ('dp', 'seq'), axis=0, tiled=True)  81.5 us
    all_gather x1, waiting for transfers between devices, body(): lax.all_gather(w_qkv, ('dp', 'seq'), axis=0, tiled=True)  75.9 us
    reduce_scatter x2, waiting for transfers between devices, micro_batch(): lax.psum_scatter(grad_keys_all, 'seq', scatter_dimension=0, tiled=True)  69.5 us
  transfers between devices with their start and end apart: 19, of which 15 were waited for; matrix products, arithmetic and copies ran while one was open for 35% of the time, Pallas kernels for 0%

commit v1 on v0

v1 whole, which is shorter than its diff:
```python
from functools import partial

import jax
import jax.numpy as jnp
from jax import lax
from jax.sharding import PartitionSpec as P

HEADS = 16
HEAD_DIM = 72
EPSILON = 1e-06
BF16 = jnp.bfloat16
F32 = jnp.float32


def layer_norm(values):
    center = values - jnp.mean(values, axis=-1, keepdims=True)
    inverse = lax.rsqrt(jnp.mean(center * center, axis=-1, keepdims=True) + EPSILON)
    return (center * inverse, inverse)


def norm_back(incoming, normed, inverse):
    return inverse * (
        incoming
        - jnp.mean(incoming, axis=-1, keepdims=True)
        - normed * jnp.mean(incoming * normed, axis=-1, keepdims=True)
    )


def dot(left, right):
    return jnp.dot(left, right, preferred_element_type=F32)


def dot_right_t(left, right):
    return lax.dot_general(left, right, (((1,), (1,)), ((), ())), preferred_element_type=F32)


def dot_left_t(left, right):
    return lax.dot_general(left, right, (((0,), (0,)), ((), ())), preferred_element_type=F32)


def body(
    latents,
    conditioning,
    w_mod,
    b_mod,
    w_qkv,
    b_qv,
    w_out,
    b_out,
    w_fc1,
    b_fc1,
    w_fc2,
    b_fc2,
    out_grad,
):
    count, tokens, width = latents.shape
    dp, seq = lax.axis_size("dp"), lax.axis_size("seq")
    both = ("dp", "seq")
    my_dp, my_seq = lax.axis_index("dp"), lax.axis_index("seq")
    me = my_dp * seq + my_seq
    rows, units = w_qkv.shape[0], w_fc2.shape[0]
    part = width // seq
    heads = HEADS // seq
    length = seq * tokens

    cond = conditioning.astype(F32)
    cond_act, silu_back = jax.vjp(jax.nn.silu, cond)
    cond_low = lax.all_gather(cond_act.astype(BF16), "dp", axis=0, tiled=True)
    cond_mine = lax.dynamic_slice_in_dim(cond_low, me * rows, rows, axis=1)
    mod_part = dot(cond_mine, w_mod)
    mod_sum = lax.psum(lax.psum_scatter(mod_part, "dp", scatter_dimension=0, tiled=True), "seq")
    biases = lax.all_gather(jnp.concatenate([b_mod, b_qv, b_out, b_fc1, b_fc2]), both, axis=0)
    pieces, start = [], 0
    for item in (b_mod, b_qv, b_out, b_fc1, b_fc2):
        pieces.append(biases[:, start : start + item.shape[0]].reshape(-1).astype(F32))
        start += item.shape[0]
    bias_mod, bias_qv, bias_out, bias_fc1, bias_fc2 = pieces
    bias_qv = lax.dynamic_index_in_dim(bias_qv.reshape(2, seq, part), my_seq, 1, keepdims=False)
    bias_fc1 = lax.dynamic_index_in_dim(
        bias_fc1.reshape(dp, seq, units), my_seq, 1, keepdims=False
    ).reshape(-1)
    modulation = (mod_sum + bias_mod).reshape(count, 6, 1, width)
    shift_att, scale_att, gate_att, shift_mlp, scale_mlp, gate_mlp = [
        modulation[:, index] for index in range(6)
    ]

    qkv_blocks = w_qkv.reshape(rows, 3, seq, part).transpose(2, 0, 1, 3).reshape(seq, rows, -1)
    fc1_blocks = w_fc1.reshape(rows, dp, seq, units).transpose(2, 0, 1, 3).reshape(seq, rows, -1)

    def to_columns(blocks):
        mine = lax.all_to_all(blocks, "seq", 0, 0, tiled=True).reshape(seq * rows, -1)
        return lax.all_gather(mine, "dp", axis=0, tiled=True)

    full_qkv = to_columns(qkv_blocks)
    full_out = lax.all_gather(w_out, both, axis=0, tiled=True)
    full_fc1 = to_columns(fc1_blocks)
    full_fc2 = lax.all_gather(w_fc2, "dp", axis=0, tiled=True)

    def gather_tokens(values):
        return lax.all_gather(values, "seq", axis=1, tiled=True)

    def flat(values):
        return values.reshape(-1, values.shape[-1])

    tokens_f = latents.astype(F32)
    normed, inverse = layer_norm(tokens_f)
    modded = (normed * (1.0 + scale_att) + shift_att).astype(BF16)
    modded_all = flat(gather_tokens(modded))
    joined = dot(modded_all, full_qkv).reshape(count, length, 3, heads, HEAD_DIM)
    bias_q = bias_qv[0].reshape(heads, HEAD_DIM)
    bias_v = bias_qv[1].reshape(heads, HEAD_DIM)
    queries = (joined[:, :, 0] + bias_q).astype(BF16)
    keys = joined[:, :, 1].astype(BF16)
    values = (joined[:, :, 2] + bias_v).astype(BF16)
    scores = jnp.einsum("bqhd,bkhd->bhqk", queries, keys, preferred_element_type=F32) * (
        HEAD_DIM ** (-0.5)
    )
    soft = jax.nn.softmax(scores, axis=-1)
    soft_low = soft.astype(BF16)
    mixed = jnp.einsum("bhqk,bkhd->bqhd", soft_low, values, preferred_element_type=F32)
    mixed = mixed.astype(BF16).reshape(count, length, part)
    mixed_mine = lax.all_to_all(mixed, "seq", 1, 2, tiled=True)
    attended = dot(mixed_mine, full_out) + bias_out
    middle = tokens_f + gate_att * attended
    normed_two, inverse_two = layer_norm(middle)
    modded_two = (normed_two * (1.0 + scale_mlp) + shift_mlp).astype(BF16)
    modded_two_all = flat(gather_tokens(modded_two))
    hidden = dot(modded_two_all, full_fc1) + bias_fc1
    active, gelu_back = jax.vjp(partial(jax.nn.gelu, approximate=True), hidden)
    active = active.astype(BF16)

    def sum_tokens(partial_sums):
        parts = partial_sums.astype(BF16).reshape(count, length, width)
        return lax.psum_scatter(parts, "seq", scatter_dimension=1, tiled=True).astype(F32)

    branch = sum_tokens(dot(active, full_fc2)) + bias_fc2
    output = middle + gate_mlp * branch

    grad_output = out_grad.astype(F32)
    grad_gate_mlp = jnp.sum(grad_output * branch, axis=1)
    grad_branch = (gate_mlp * grad_output).astype(BF16)
    grad_branch_all = flat(gather_tokens(grad_branch))
    grad_hidden = gelu_back(dot_right_t(grad_branch_all, full_fc2))[0].astype(BF16)
    grad_modded_two = sum_tokens(dot_right_t(grad_hidden, full_fc1))
    grad_shift_mlp = jnp.sum(grad_modded_two, axis=1)
    grad_scale_mlp = jnp.sum(grad_modded_two * normed_two, axis=1)
    grad_middle = grad_output + norm_back(
        grad_modded_two * (1.0 + scale_mlp), normed_two, inverse_two
    )
    grad_gate_att = jnp.sum(grad_middle * attended, axis=1)
    grad_attended = (gate_att * grad_middle).astype(BF16)
    grad_mixed = dot_right_t(flat(grad_attended), full_out).astype(BF16)
    grad_mixed = lax.all_to_all(grad_mixed.reshape(latents.shape), "seq", 2, 1, tiled=True)
    grad_mixed = grad_mixed.reshape(count, length, heads, HEAD_DIM)
    grad_soft = jnp.einsum("bqhd,bkhd->bhqk", grad_mixed, values, preferred_element_type=F32)
    delta = jnp.sum(soft * grad_soft, axis=-1, keepdims=True)
    grad_scores = (soft * (grad_soft - delta)).astype(BF16)
    scale = HEAD_DIM ** (-0.5)
    grad_q = jnp.einsum("bhqk,bkhd->bqhd", grad_scores, keys, preferred_element_type=F32) * scale
    grad_k = jnp.einsum("bhqk,bqhd->bkhd", grad_scores, queries, preferred_element_type=F32) * scale
    grad_v = jnp.einsum("bhqk,bqhd->bkhd", soft_low, grad_mixed, preferred_element_type=F32)
    grad_joined = jnp.concatenate(
        [item.astype(BF16).reshape(count * length, part) for item in (grad_q, grad_k, grad_v)],
        axis=1,
    )
    grad_modded = sum_tokens(dot_right_t(grad_joined, full_qkv))
    grad_shift_att = jnp.sum(grad_modded, axis=1)
    grad_scale_att = jnp.sum(grad_modded * normed, axis=1)
    grad_tokens = grad_middle + norm_back(grad_modded * (1.0 + scale_att), normed, inverse)

    def from_columns(sums, groups):
        mine = lax.psum_scatter(sums.astype(BF16), "dp", scatter_dimension=0, tiled=True)
        blocks = lax.all_to_all(mine.reshape(seq, rows, -1), "seq", 0, 0, tiled=True)
        blocks = blocks.astype(F32).reshape(seq, rows, groups, -1)
        return blocks.transpose(1, 2, 0, 3).reshape(rows, -1)

    sums_fc2 = lax.psum_scatter(
        dot_left_t(active, grad_branch_all).astype(BF16), "dp", scatter_dimension=0, tiled=True
    ).astype(F32)
    sums_fc1 = from_columns(dot_left_t(modded_two_all, grad_hidden), dp)
    sums_out = lax.psum_scatter(
        dot_left_t(flat(mixed_mine), flat(grad_attended)).astype(BF16),
        both,
        scatter_dimension=0,
        tiled=True,
    ).astype(F32)
    sums_qkv = from_columns(dot_left_t(modded_all, grad_joined), 3)

    grad_mod = jnp.concatenate(
        [
            grad_shift_att,
            grad_scale_att,
            grad_gate_att,
            grad_shift_mlp,
            grad_scale_mlp,
            grad_gate_mlp,
        ],
        axis=1,
    )
    grad_mod = lax.psum(grad_mod, "seq").astype(BF16)
    grad_mod = lax.all_gather(grad_mod, "dp", axis=0, tiled=True)
    sums_mod = dot_left_t(cond_mine, grad_mod)
    own = b_mod.shape[0]
    sums_bias_mod = jnp.sum(
        lax.dynamic_slice_in_dim(grad_mod, me * own, own, axis=1).astype(F32), axis=0
    )
    grad_cond_act = lax.all_gather(dot_right_t(grad_mod, w_mod), both, axis=0)
    grad_cond_act = lax.dynamic_slice_in_dim(grad_cond_act, my_dp * count, count, axis=1)
    grad_cond = silu_back(grad_cond_act.transpose(1, 0, 2).reshape(count, width))[0]

    def spread(values, shape):
        blank = jnp.zeros(shape, F32)
        return lax.dynamic_update_slice_in_dim(blank, values, my_seq, 1).reshape(-1)

    joined_sums = jnp.sum(grad_joined.astype(F32), axis=0)
    qv_sums = jnp.stack([joined_sums[:part], joined_sums[2 * part :]])
    fc1_sums = jnp.sum(grad_hidden.astype(F32), axis=0)
    bias_sums = [
        spread(qv_sums.reshape(2, 1, part), (2, seq, part)),
        jnp.sum(flat(grad_attended).astype(F32), axis=0),
        spread(fc1_sums.reshape(dp, 1, units), (dp, seq, units)),
        jnp.sum(flat(grad_branch).astype(F32), axis=0),
    ]
    joint = jnp.concatenate([item.reshape(dp * seq, -1) for item in bias_sums], axis=1)
    joint = lax.psum_scatter(joint, both, scatter_dimension=0, tiled=True).reshape(-1)
    cuts = [b_qv.shape[0], b_out.shape[0], b_fc1.shape[0]]
    sums_bias_qv, sums_bias_out, sums_bias_fc1, sums_bias_fc2 = jnp.split(
        joint, [cuts[0], cuts[0] + cuts[1], sum(cuts)]
    )
    return (
        output.astype(BF16),
        grad_tokens.astype(BF16),
        grad_cond.astype(BF16),
        sums_mod,
        sums_bias_mod,
        sums_qkv,
        sums_bias_qv,
        sums_out,
        sums_bias_out,
        sums_fc1,
        sums_bias_fc1,
        sums_fc2,
        sums_bias_fc2,
    )


def solution(mesh):
    both = P(("dp", "seq"))
    wide = P(("dp", "seq"), None)
    tokens = P("dp", "seq", None)
    in_specs = (
        tokens,
        P("dp", None),
        wide,
        both,
        wide,
        both,
        wide,
        both,
        wide,
        both,
        wide,
        both,
        tokens,
    )
    out_specs = (tokens, tokens, P("dp", None)) + (wide, both) * 5
    return jax.shard_map(body, mesh=mesh, in_specs=in_specs, out_specs=out_specs, check_vma=False)
```

time: 1970 us -> 887 us (0.45)
  waiting for transfers between devices: 890 us -> 295 us
  blocking collectives: 678 us -> 319 us
  matrix products: 177 us -> 99.2 us
  local copies, waits for them, and re-layouts: 121 us -> 72.9 us
  starting transfers between devices: 7.95 us -> 42.6 us
  other arithmetic: 55.6 us -> 30 us
    unnamed x3, blocking collectives: 664 us -> 175 us
    reduce_scatter x5 -> x6, waiting for transfers between devices: 325 us -> 43.1 us  [the longest x3 43.1 us: sum_tokens(): lax.psum_scatter(parts, 'seq', scatter_dimension=1, tiled=True).astype(F32)]
    all_gather x9 -> x7, waiting for transfers between devices: 395 us -> 207 us  [the longest x2 69.7 us: to_columns(): return lax.all_gather(mine, 'dp', axis=0, tiled=True)]
    unnamed x12 -> x23, waiting for transfers between devices: 169 us -> 33.5 us
    all_gather x0 -> x3, blocking collectives: none -> 100 us  [the longest x1 38.1 us: body(): grad_cond_act = lax.all_gather(dot_right_t(grad_mod, w_mod), both, axis=0)]
    dot_general x35 -> x21, matrix products: 177 us -> 99.2 us  [the longest x5 29.1 us: dot(): return jnp.dot(left, right, preferred_element_type=F32)]
    unnamed x46 -> x128, local copies, waits for them, and re-layouts: 84.9 us -> 37.7 us
    concatenate x1, other arithmetic: 28.7 us -> 0.1 us  [body(): jnp.concatenate([item.reshape(dp * seq, -1) for item in bias_sums], axis=1)]
  transfers between devices with their start and end apart: 19 -> 26, of which waited for: 15 -> 14; matrix products, arithmetic and copies ran while one was open for 35% -> 29% of each run, Pallas kernels for 0% -> 0%
where the time goes in v1:
time: 887 us; the launch traced here: 874 us
  blocking collectives  319 us (36%)
  waiting for transfers between devices  295 us (33%)
  matrix products  99.2 us (11%)
  local copies, waits for them, and re-layouts  72.9 us (8%)
  starting transfers between devices  42.6 us (5%)
  other arithmetic  30 us (3%)
  between operations  16 us (2%)
    unnamed x3, blocking collectives  175 us
    all_gather x2, waiting for transfers between devices, to_columns(): return lax.all_gather(mine, 'dp', axis=0, tiled=True)  69.7 us
    all_gather x1, waiting for transfers between devices, body(): full_fc2 = lax.all_gather(w_fc2, 'dp', axis=0, tiled=True)  58.5 us
    all_gather x3, waiting for transfers between devices, gather_tokens(): return lax.all_gather(values, 'seq', axis=1, tiled=True)  57.2 us
    reduce_scatter x3, waiting for transfers between devices, sum_tokens(): lax.psum_scatter(parts, 'seq', scatter_dimension=1, tiled=True).astype(F32)  43.1 us
    all_gather x1, blocking collectives, body(): grad_cond_act = lax.all_gather(dot_right_t(grad_mod, w_mod), both, axis=0)  38.1 us
    unnamed x128, local copies, waits for them, and re-layouts  37.7 us
    unnamed x23, waiting for transfers between devices  33.5 us
  transfers between devices with their start and end apart: 26, of which 14 were waited for; matrix products, arithmetic and copies ran while one was open for 29% of the time, Pallas kernels for 0%

profile of v1, /device:TPU:4, one launch (start us, length us, event | category | flops | bytes accessed | tf_op | source)
XLA Modules:
  0.0 874.4 jit_solution(14390168292395758996)
XLA Ops:
  9.9 3.4 all-to-all-start
  13.4 31.3 %all-gather.2 = bf16[8,2,1152]{2,1,0:T(2,128)(2,1)S(1)} all-gather(bf16[1,2,1152]{2,1,0:T(2,128)(2,1)S(1)} %fusion.79), channel_id=1, replica_groups=mesh['dp'=8,'seq'=4] {'dp'}, dimensions={0}, use_global_device_ids=true | all-gather | bytes 41472 | tf_op jit(solution)/shard_map/all_gather | solution.py:68
  46.5 40.4 %all-reduce = bf16[16128]{0:T(1024)(128)(2,1)S(1)} all-reduce(bf16[16128]{0:T(1024)(128)(2,1)S(1)} %dynamic-update-slice), channel_id=2, replica_groups=mesh['dp'=8,'seq'=4] {'dp','seq'}, use_global_device_ids=true, to_apply=%add | all-reduce | flops 16128 | bytes 64512
  89.7 29.1 %all-reduce.7.cloned.1.call-done = f32[16,6912]{1,0:T(8,128)} async-done(((f32[16,6912]{1,0:T(8,128)}), f32[16,6912]{1,0:T(8,128)}) %all-reduce.7.cloned.1.call-update) | async-done | bytes 442384
  119.7 11.0 %psum.14 = f32[2,6912]{1,0:T(2,128)S(1)} all-reduce(f32[2,6912]{1,0:T(2,128)S(1)} %constant_dynamic-slice_fusion), channel_id=1, replica_groups=mesh['dp'=8,'seq'=4] {'seq'}, use_global_device_ids=true, to_apply=%region_1.2 | all-reduce | flops 13824 | bytes 110592 | tf_op jit(solution)/shard_map/psum | solution.py:71
  136.8 8.8 %all_to_all.53 = bf16[4,36,1152]{2,1,0:T(8,128)(2,1)S(1)} all-to-all(bf16[4,36,1152]{2,1,0:T(8,128)(2,1)S(1)} %copy.85), channel_id=1, replica_groups=mesh['dp'=8,'seq'=4] {'seq'}, dimensions={0} | all-to-all | bytes 663552 | tf_op jit(solution)/shard_map/all_to_all | solution.py:91
  148.7 21.2 %all-gather.15.cloned.1.call-done = bf16[1152,864]{1,0:T(8,128)(2,1)} async-done(((bf16[144,864]{1,0:T(8,128)(2,1)}), bf16[1152,864]{1,0:T(8,128)(2,1)}) %all-gather.15.cloned.1.call-update) | async-done | bytes 1990672 | tf_op jit(solution)/shard_map/all_gather | solution.py:92
  169.9 2.9 copy.78
  172.8 20.7 %all-gather.13.cloned.1.call-done = bf16[2,512,1152]{2,1,0:T(8,128)(2,1)} async-done(((bf16[2,128,1152]{2,1,0:T(8,128)(2,1)}), bf16[2,512,1152]{2,1,0:T(8,128)(2,1)}) %all-gather.13.cloned.1.call-update) | async-done | bytes 2359312 | tf_op jit(solution)/shard_map/all_gather | solution.py:100
  193.5 4.2 fusion.13
  200.8 5.0 fusion.100
  206.7 9.2 %fusion.31 = bf16[2,4,72,512]{3,2,1,0:T(8,128)(2,1)S(1)} fusion(f32[2,512,3,4,72]{1,4,3,2,0:T(8,128)} %copy-done.3, f32[4,72]{1,0:T(4,128)S(1)} %add.191, f32[2,4,512]{2,1,0:T(4,128)S(1)} %get-tuple-element.48, f32[2,4,512,512]{2,3,1,0:T(8,128)} %copy-done.1), kind=kOutput, calls=%fused_computation.62 | convolution fusion | flops 313364992 | bytes 18564224 | tf_op jit(solution)/shard_map/bhqk,bkhd->bqhd/dot_general | solution.py:120
  217.7 5.2 all-to-all-start.1
  223.4 10.1 %all-to-all-done.1 = bf16[2,512,288]{2,0,1:T(2,128)(2,1)S(1)} async-done(((bf16[2,512,288]{2,0,1:T(2,128)(2,1)}), bf16[2,512,288]{2,0,1:T(2,128)(2,1)S(1)}, u32[]{:S(2)}, u32[]{:S(2)}) %all-to-all-start.1) | async-done | bytes 589856 | tf_op jit(solution)/shard_map/all_to_all | solution.py:122
  235.1 21.8 %all-gather.25.cloned.1.call-done = bf16[32,36,1152]{2,1,0:T(8,128)(2,1)} async-done(((bf16[1,36,1152]{2,1,0:T(8,128)(2,1)}), bf16[32,36,1152]{2,1,0:T(8,128)(2,1)}) %all-gather.25.cloned.1.call-update) | async-done | bytes 2654224 | tf_op jit(solution)/shard_map/all_gather | solution.py:95
  256.8 5.2 reshape.313
  262.0 3.9 fusion.97
  267.9 12.7 %all-gather.23.cloned.1.call-done = bf16[2,512,1152]{2,1,0:T(8,128)(2,1)} async-done(((bf16[2,128,1152]{2,1,0:T(8,128)(2,1)}), bf16[2,512,1152]{2,1,0:T(8,128)(2,1)}) %all-gather.23.cloned.1.call-update) | async-done | bytes 2359312 | tf_op jit(solution)/shard_map/all_gather | solution.py:100
  280.6 58.5 %all-gather.21.cloned.1.call-done = bf16[1152,1152]{1,0:T(8,128)(2,1)} async-done(((bf16[144,1152]{1,0:T(8,128)(2,1)}), bf16[1152,1152]{1,0:T(8,128)(2,1)}) %all-gather.21.cloned.1.call-update) | async-done | bytes 2654224 | tf_op jit(solution)/shard_map/all_gather | solution.py:97
  339.1 8.1 fusion.101
  347.2 48.5 %all-gather.19.cloned.1.call-done = bf16[1152,1152]{1,0:T(8,128)(2,1)} async-done(((bf16[144,1152]{1,0:T(8,128)(2,1)}), bf16[1152,1152]{1,0:T(8,128)(2,1)}) %all-gather.19.cloned.1.call-update) | async-done | bytes 2654224 | tf_op jit(solution)/shard_map/all_gather | solution.py:92
  395.7 23.7 %all-gather.17.cloned.1.call-done = bf16[2,512,1152]{2,1,0:T(8,128)(2,1)} async-done(((bf16[2,128,1152]{2,1,0:T(8,128)(2,1)}), bf16[2,512,1152]{2,1,0:T(8,128)(2,1)}) %all-gather.17.cloned.1.call-update) | async-done | bytes 2359312 | tf_op jit(solution)/shard_map/all_gather | solution.py:100
  419.5 11.1 %convert_reduce_fusion = (f32[1152]{0:T(1024)}, bf16[1024,1152]{1,0:T(8,128)(2,1)S(1)}, f32[1024,1152]{1,0:T(8,128)}) fusion(f32[1024,1152]{1,0:T(8,128)} %fusion.101, f32[1152]{0:T(1024)S(1)} %add.206, bf16[1024,1152]{1,0:T(8,128)(2,1)} %bitcast.193, bf16[1152,1152]{1,0:T(8,128)(2,1)} %all-gather.19.cloned.1.call-done), kind=kOutput, calls=%fused_computation.18 | convolution fusion | flops 2745039872 | bytes 16819200 | tf_op jit(solution)/shard_map/dot_general | solution.py:30
  430.6 4.8 convolution_convert_fusion.4
  435.4 8.8 %convolution_convert_fusion.5 = bf16[1024,1152]{1,0:T(8,128)(2,1)} fusion(bf16[1152,1152]{1,0:T(8,128)(2,1)} %all-gather.21.cloned.1.call-done, f32[1024,1152]{1,0:T(8,128)} %get-tuple-element.51), kind=kOutput, calls=%fused_computation.25 | convolution fusion | flops 2729705472 | bytes 9732096 | tf_op jit(solution)/shard_map/dot_general | solution.py:30
  445.0 5.2 reshape.308
  450.2 7.2 convolution_convert_fusion.2
  457.5 11.1 %reduce-scatter.11.cloned.1.call-done = bf16[2,128,1152]{2,1,0:T(8,128)(2,1)} async-done(((bf16[2,512,1152]{2,1,0:T(8,128)(2,1)}), bf16[2,128,1152]{2,1,0:T(8,128)(2,1)}) %reduce-scatter.11.cloned.1.call-update) | async-done | bytes 589840 | tf_op jit(solution)/shard_map/reduce_scatter | solution.py:134
  472.1 32.0 %reduce-scatter.9.cloned.1.call-done = bf16[2,128,1152]{2,1,0:T(8,128)(2,1)} async-done(((bf16[2,512,1152]{2,1,0:T(8,128)(2,1)}), bf16[2,128,1152]{2,1,0:T(8,128)(2,1)}) %reduce-scatter.9.cloned.1.call-update) | async-done | bytes 589840 | tf_op jit(solution)/shard_map/reduce_scatter | solution.py:134
  504.1 4.3 convert_reduce_fusion.6
  510.1 12.1 %all_to_all.54 = bf16[2,128,1152]{1,0,2:T(2,128)(2,1)S(1)} all-to-all(bf16[2,128,1152]{1,0,2:T(2,128)(2,1)S(1)} %copy.86), channel_id=1, replica_groups=mesh['dp'=8,'seq'=4] {'seq'}, dimensions={2} | all-to-all | bytes 1179648 | tf_op jit(solution)/shard_map/all_to_all | solution.py:153
  522.8 7.5 fusion.39
  531.1 5.1 multiply_reduce_fusion
  537.6 2.4 multiply_convert_fusion
  546.0 3.9 convolution_convert_fusion.6
  550.2 8.4 convolution_convert_fusion.1
  558.7 6.5 convolution_convert_fusion.3
  566.2 2.5 convolution_convert_fusion
  568.7 84.4 %fusion = bf16[48,1152]{1,0:T(8,128)(2,1)S(1)} fusion(bf16[1152,1152]{1,0:T(8,128)(2,1)} %convolution_convert_fusion), kind=kCustom, calls=%all-reduce-scatter | all-reduce-scatter fusion | flops 1769473 | bytes 2764800
  660.0 14.3 %collective-permute-start.2 = (bf16[48,1152]{1,0:T(8,128)(2,1)S(1)}, bf16[48,1152]{1,0:T(8,128)(2,1)}, u32[]{:S(2)}, u32[]{:S(2)}) collective-permute-start(bf16[48,1152]{1,0:T(8,128)(2,1)S(1)} %fusion), channel_id=1, source_target_pairs={{0,3},{1,4},{2,5},{3,6},{4,7},{5,8},{6,9},{7,10},{8,11},{9,12},{10... | collective-permute-start | bytes 331784
  682.4 13.8 %concatenate.16 = bf16[420,1152]{1,0:T(8,128)(2,1)} concatenate(bf16[36,1152]{1,0:T(8,128)(2,1)} %copy-done.17, bf16[48,1152]{1,0:T(8,128)(2,1)S(1)} %collective-permute-done.6, bf16[48,1152]{1,0:T(8,128)(2,1)S(1)} %collective-permute-done.5, bf16[48,1152]{1,0:T(8,128)(2,1)S(1)} %collective-permute-done.4, bf16[48,1152]{1,0:T(8,128)(2,1)S(1)} %collective-permute-done.3, ...), dimensions={0} | concatenate | bytes 1935360
  699.9 3.4 all-to-all-start.5
  703.7 49.6 %all-reduce.2 = f32[32,288]{1,0:T(8,128)S(1)} all-reduce(f32[32,288]{1,0:T(8,128)S(1)} %pad_maximum_fusion), channel_id=9, replica_groups=mesh['dp'=8,'seq'=4] {'dp','seq'}, use_global_device_ids=true, to_apply=%region_29.30.clone | all-reduce | flops 9216 | bytes 73728
  755.7 4.3 all-to-all-start.4
  777.8 2.5 multiply_reduce_fusion.2
  782.7 12.1 %psum.15 = bf16[2,6912]{1,0:T(2,128)(2,1)S(1)} all-reduce(f32[2,6912]{1,0:T(2,128)} %constant_dynamic-update-slice_fusion.3), channel_id=1, replica_groups=mesh['dp'=8,'seq'=4] {'seq'}, use_global_device_ids=true, to_apply=%region_22.23 | all-reduce | flops 13824 | bytes 82944 | tf_op jit(solution)/shard_map/psum | solution.py:200
  794.9 30.8 %all-gather.4 = bf16[8,2,6912]{2,1,0:T(2,128)(2,1)S(1)} all-gather(bf16[1,2,6912]{2,1,0:T(2,128)(2,1)S(1)} %bitcast.183), channel_id=1, replica_groups=mesh['dp'=8,'seq'=4] {'dp'}, dimensions={0}, use_global_device_ids=true | all-gather | bytes 248832 | tf_op jit(solution)/shard_map/all_gather | solution.py:201
  828.7 38.1 %all-gather.1 = f32[512,36]{1,0:T(8,128)S(1)} all-gather(f32[16,36]{1,0:T(8,128)S(1)} %fusion.102), channel_id=3, replica_groups=mesh['dp'=8,'seq'=4] {'dp','seq'}, dimensions={0}, use_global_device_ids=true | all-gather | bytes 76032 | tf_op jit(solution)/shard_map/all_gather | solution.py:207
  (278 shorter events, 87.3 us)
Async XLA Ops:
  7.2 37.6 %copy-start = (bf16[36,6912]{1,0:T(8,128)(2,1)S(1)}, bf16[36,6912]{1,0:T(8,128)(2,1)}, u32[]{:S(2)}) copy-start(bf16[36,6912]{1,0:T(8,128)(2,1)} %param.15) | copy-start | bytes 1492996
  7.2 38.8 %copy-start.2 = (bf16[2,128,1152]{2,1,0:T(8,128)(2,1)S(1)}, bf16[2,128,1152]{2,1,0:T(8,128)(2,1)}, u32[]{:S(2)}) copy-start(bf16[2,128,1152]{2,1,0:T(8,128)(2,1)} %param.13) | copy-start | bytes 1769476
  8.5 37.6 %copy-start.41 = (bf16[216]{0:T(256)(128)(2,1)S(1)}, bf16[216]{0:T(256)(128)(2,1)}, u32[]{:S(2)}) copy-start(bf16[216]{0:T(256)(128)(2,1)} %param.16) | copy-start | bytes 1300
  8.5 37.6 %copy-start.42 = (bf16[72]{0:T(256)(128)(2,1)S(1)}, bf16[72]{0:T(256)(128)(2,1)}, u32[]{:S(2)}) copy-start(bf16[72]{0:T(256)(128)(2,1)} %param.18) | copy-start | bytes 436
  8.5 37.6 %copy-start.43 = (bf16[36]{0:T(256)(128)(2,1)S(1)}, bf16[36]{0:T(256)(128)(2,1)}, u32[]{:S(2)}) copy-start(bf16[36]{0:T(256)(128)(2,1)} %param.20) | copy-start | bytes 220
  8.6 37.6 %copy-start.44 = (bf16[144]{0:T(256)(128)(2,1)S(1)}, bf16[144]{0:T(256)(128)(2,1)}, u32[]{:S(2)}) copy-start(bf16[144]{0:T(256)(128)(2,1)} %param.22) | copy-start | bytes 868
  8.6 37.6 %copy-start.45 = (bf16[36]{0:T(256)(128)(2,1)S(1)}, bf16[36]{0:T(256)(128)(2,1)}, u32[]{:S(2)}) copy-start(bf16[36]{0:T(256)(128)(2,1)} %param.24) | copy-start | bytes 220
  8.6 78.7 %copy-start.48 = (u32[32]{0:T(128)S(1)}, u32[32]{0:T(128)}, u32[]{:S(2)}) copy-start(u32[32]{0:T(128)} %constant.89) | copy-start | bytes 388
  9.9 78.9 %all-to-all-start = ((bf16[4,36,864]{2,1,0:T(8,128)(2,1)}), bf16[4,36,864]{2,1,0:T(8,128)(2,1)S(1)}, u32[]{:S(2)}, u32[]{:S(2)}) async-start(bf16[4,36,864]{2,1,0:T(8,128)(2,1)} %copy.77), calls=%async_computation | async-start | bytes 573440 | tf_op jit(solution)/shard_map/all_to_all | solution.py:91
  13.3 105.4 %all-reduce.7.cloned.1.call-start = ((), (), s32[]{:S(2)}) async-start(), calls=%async_computation.25 | async-start | bytes 884736
  45.9 124.0 %all-gather.15.cloned.1.call-start = ((), (), s32[]{:S(2)}) async-start(), calls=%async_computation.13 | async-start | bytes 2322432 | tf_op jit(solution)/shard_map/all_gather | solution.py:92
  46.0 86.7 %copy-start.10 = (bf16[2,128,1152]{2,1,0:T(8,128)(2,1)S(1)}, bf16[2,128,1152]{2,1,0:T(8,128)(2,1)}, u32[]{:S(2)}) copy-start(bf16[2,128,1152]{2,1,0:T(8,128)(2,1)} %param.25) | copy-start | bytes 1769476
  87.1 47.1 %copy-start.31 = (f32[2,128]{1,0:T(2,128)}, f32[2,128]{1,0:T(2,128)S(1)}, u32[]{:S(2)}) copy-start(f32[2,128]{1,0:T(2,128)S(1)} %broadcast_multiply_fusion.5) | copy-start | bytes 3076
  88.8 45.4 %copy-start.35 = (f32[2,128]{1,0:T(2,128)}, f32[2,128]{1,0:T(2,128)S(1)}, u32[]{:S(2)}) copy-start(f32[2,128]{1,0:T(2,128)S(1)} %add_rsqrt_fusion.1) | copy-start | bytes 3076
  89.6 45.2 %copy-start.14 = (bf16[36,4608]{1,0:T(8,128)(2,1)S(1)}, bf16[36,4608]{1,0:T(8,128)(2,1)}, u32[]{:S(2)}) copy-start(bf16[36,4608]{1,0:T(8,128)(2,1)} %param.21) | copy-start | bytes 995332
  89.6 103.9 %all-gather.13.cloned.1.call-start = ((), (), s32[]{:S(2)}) async-start(), calls=%async_computation.12 | async-start | bytes 2949120 | tf_op jit(solution)/shard_map/all_gather | solution.py:100
  132.0 124.8 %all-gather.25.cloned.1.call-start = ((), (), s32[]{:S(2)}) async-start(), calls=%async_computation.24 | async-start | bytes 3041280 | tf_op jit(solution)/shard_map/all_gather | solution.py:95
  132.5 148.0 %all-gather.23.cloned.1.call-start = ((), (), s32[]{:S(2)}) async-start(), calls=%async_computation.18 | async-start | bytes 2949120 | tf_op jit(solution)/shard_map/all_gather | solution.py:100
  134.2 204.9 %all-gather.21.cloned.1.call-start = ((), (), s32[]{:S(2)}) async-start(), calls=%async_computation.16 | async-start | bytes 2985984 | tf_op jit(solution)/shard_map/all_gather | solution.py:97
  134.8 260.9 %all-gather.19.cloned.1.call-start = ((), (), s32[]{:S(2)}) async-start(), calls=%async_computation.15 | async-start | bytes 2985984 | tf_op jit(solution)/shard_map/all_gather | solution.py:92
  146.7 60.0 %copy-start.39 = (f32[4,72]{1,0:T(4,128)}, f32[4,72]{1,0:T(4,128)S(1)}, u32[]{:S(2)}) copy-start(f32[4,72]{1,0:T(4,128)S(1)} %add.191) | copy-start | bytes 3460
  217.7 15.8 %all-to-all-start.1 = ((bf16[2,512,288]{2,0,1:T(2,128)(2,1)}), bf16[2,512,288]{2,0,1:T(2,128)(2,1)S(1)}, u32[]{:S(2)}, u32[]{:S(2)}) async-start(bf16[2,512,288]{2,0,1:T(2,128)(2,1)} %copy.80), calls=%async_computation.1 | async-start | bytes 1572864 | tf_op jit(solution)/shard_map/all_to_all | solution.py:122
  222.8 196.6 %all-gather.17.cloned.1.call-start = ((), (), s32[]{:S(2)}) async-start(), calls=%async_computation.14 | async-start | bytes 2949120 | tf_op jit(solution)/shard_map/all_gather | solution.py:100
  267.4 201.2 %reduce-scatter.11.cloned.1.call-start = ((), (), s32[]{:S(2)}) async-start(), calls=%async_computation.19 | async-start | bytes 2949120 | tf_op jit(solution)/shard_map/reduce_scatter | solution.py:134
  435.4 68.7 %reduce-scatter.9.cloned.1.call-start = ((), (), s32[]{:S(2)}) async-start(), calls=%async_computation.17 | async-start | bytes 2949120 | tf_op jit(solution)/shard_map/reduce_scatter | solution.py:134
  444.2 253.8 %reduce-scatter.17.cloned.1.call-start = ((), (), s32[]{:S(2)}) async-start(), calls=%async_computation.22 | async-start | bytes 2985984 | tf_op jit(solution)/shard_map/reduce_scatter | solution.py:172
  457.4 46.6 %copy-start.11 = (bf16[2,128,1152]{2,1,0:T(8,128)(2,1)S(1)}, bf16[2,128,1152]{2,1,0:T(8,128)(2,1)}, u32[]{:S(2)}) copy-start(bf16[2,128,1152]{2,1,0:T(8,128)(2,1)} %param.25) | copy-start | bytes 1769476
  457.4 46.6 %copy-start.18 = (f32[2,1,1,1152]{3,0,1,2:T(2,128)S(1)}, f32[2,1,1,1152]{3,0,1,2:T(2,128)}, u32[]{:S(2)}) copy-start(f32[2,1,1,1152]{3,0,1,2:T(2,128)} %copy.133) | copy-start | bytes 27652
  457.5 296.5 %reduce-scatter.15.cloned.1.call-start = ((), (), s32[]{:S(2)}) async-start(), calls=%async_computation.21 | async-start | bytes 2322432 | tf_op jit(solution)/shard_map/reduce_scatter | solution.py:172
  550.0 211.2 %reduce-scatter.19.cloned.1.call-start = ((), (), s32[]{:S(2)}) async-start(), calls=%async_computation.23 | async-start | bytes 2985984 | tf_op jit(solution)/shard_map/reduce_scatter | solution.py:177
  558.6 216.1 %reduce-scatter.13.cloned.1.call-start = ((), (), s32[]{:S(2)}) async-start(), calls=%async_computation.20 | async-start | bytes 2949120 | tf_op jit(solution)/shard_map/reduce_scatter | solution.py:134
  568.7 109.5 %copy-start.29 = (f32[1152]{0:T(1024)S(1)}, f32[1152]{0:T(1024)}, u32[]{:S(2)}) copy-start(f32[1152]{0:T(1024)} %get-tuple-element.28) | copy-start | bytes 13828
  568.7 110.2 %copy-start.38 = (f32[1152]{0:T(1024)S(1)}, f32[1152]{0:T(1024)}, u32[]{:S(2)}) copy-start(f32[1152]{0:T(1024)} %get-tuple-element.26) | copy-start | bytes 13828
  568.7 110.4 %copy-start.30 = (f32[1152]{0:T(1024)S(1)}, f32[1152]{0:T(1024)}, u32[]{:S(2)}) copy-start(f32[1152]{0:T(1024)} %get-tuple-element.23) | copy-start | bytes 13828
  568.7 129.1 %copy-start.8 = (bf16[1024,864]{0,1:T(8,128)(2,1)S(1)}, bf16[1024,864]{0,1:T(8,128)(2,1)}, u32[]{:S(2)}) copy-start(bf16[1024,864]{0,1:T(8,128)(2,1)} %copy-done.7) | copy-start | bytes 5308420
  653.1 21.1 %collective-permute-start.6 = (bf16[48,1152]{1,0:T(8,128)(2,1)S(1)}, bf16[48,1152]{1,0:T(8,128)(2,1)S(1)}, u32[]{:S(2)}, u32[]{:S(2)}) collective-permute-start(bf16[48,1152]{1,0:T(8,128)(2,1)S(1)} %fusion), channel_id=1, source_target_pairs={{0,7},{1,8},{2,9},{3,10},{4,11},{5,12},{6,13},{7,14},{8,15},{9,16}... | collective-permute-start | bytes 331784
  654.4 21.8 %collective-permute-start.5 = (bf16[48,1152]{1,0:T(8,128)(2,1)S(1)}, bf16[48,1152]{1,0:T(8,128)(2,1)S(1)}, u32[]{:S(2)}, u32[]{:S(2)}) collective-permute-start(bf16[48,1152]{1,0:T(8,128)(2,1)S(1)} %fusion), channel_id=1, source_target_pairs={{0,6},{1,7},{2,8},{3,9},{4,10},{5,11},{6,12},{7,13},{8,14},{9,15},... | collective-permute-start | bytes 331784
  655.8 4.2 collective-permute-start.7
  657.1 22.1 %collective-permute-start.4 = (bf16[48,1152]{1,0:T(8,128)(2,1)S(1)}, bf16[48,1152]{1,0:T(8,128)(2,1)S(1)}, u32[]{:S(2)}, u32[]{:S(2)}) collective-permute-start(bf16[48,1152]{1,0:T(8,128)(2,1)S(1)} %fusion), channel_id=1, source_target_pairs={{0,5},{1,6},{2,7},{3,8},{4,9},{5,10},{6,11},{7,12},{8,13},{9,14},{... | collective-permute-start | bytes 331784
  658.4 20.8 %collective-permute-start.3 = (bf16[48,1152]{1,0:T(8,128)(2,1)S(1)}, bf16[48,1152]{1,0:T(8,128)(2,1)S(1)}, u32[]{:S(2)}, u32[]{:S(2)}) collective-permute-start(bf16[48,1152]{1,0:T(8,128)(2,1)S(1)} %fusion), channel_id=1, source_target_pairs={{0,4},{1,5},{2,6},{3,7},{4,8},{5,9},{6,10},{7,11},{8,12},{9,13},{1... | collective-permute-start | bytes 331784
  660.0 16.2 %copy-start.17 = (bf16[36,1152]{1,0:T(8,128)(2,1)}, bf16[36,1152]{1,0:T(8,128)(2,1)S(1)}, u32[]{:S(2)}) copy-start(bf16[36,1152]{1,0:T(8,128)(2,1)S(1)} %collective-permute-done.7) | copy-start | bytes 248836
  660.0 19.2 %collective-permute-start.2 = (bf16[48,1152]{1,0:T(8,128)(2,1)S(1)}, bf16[48,1152]{1,0:T(8,128)(2,1)}, u32[]{:S(2)}, u32[]{:S(2)}) collective-permute-start(bf16[48,1152]{1,0:T(8,128)(2,1)S(1)} %fusion), channel_id=1, source_target_pairs={{0,3},{1,4},{2,5},{3,6},{4,7},{5,8},{6,9},{7,10},{8,11},{9,12},{10... | collective-permute-start | bytes 331784
  674.3 6.7 collective-permute-start.1
  676.2 6.2 collective-permute-start
  679.1 24.4 %copy-start.23 = (f32[32,36]{1,0:T(8,128)S(1)}, f32[32,36]{1,0:T(8,128)}, u32[]{:S(2)}) copy-start(f32[32,36]{1,0:T(8,128)} %reshape.280) | copy-start | bytes 13828
  699.9 55.8 %all-to-all-start.5 = ((bf16[4,36,1152]{2,1,0:T(8,128)(2,1)}), bf16[4,36,1152]{2,1,0:T(8,128)(2,1)S(1)}, u32[]{:S(2)}, u32[]{:S(2)}) async-start(bf16[4,36,1152]{2,1,0:T(8,128)(2,1)} %reshape.282), calls=%async_computation.10 | async-start | bytes 737280 | tf_op jit(solution)/shard_map/all_to_all | solution.py:173
  755.7 12.0 %all-to-all-start.4 = ((bf16[4,36,864]{2,1,0:T(8,128)(2,1)}), bf16[4,36,864]{2,1,0:T(8,128)(2,1)}, u32[]{:S(2)}, u32[]{:S(2)}) async-start(bf16[4,36,864]{2,1,0:T(8,128)(2,1)} %reshape.273), calls=%async_computation.8 | async-start | bytes 573440 | tf_op jit(solution)/shard_map/all_to_all | solution.py:173
  780.3 86.7 %copy-start.34 = (bf16[2,1152]{1,0:T(2,128)(2,1)S(1)}, bf16[2,1152]{1,0:T(2,128)(2,1)}, u32[]{:S(2)}) copy-start(bf16[2,1152]{1,0:T(2,128)(2,1)} %param.14) | copy-start | bytes 13828
  (30 other events, 148.4 us)
Sparse Core Ops, SparseCore 0:
  46.0 72.6 all-reduce.6
  121.7 48.1 all-gather.14
  172.1 21.3 all-gather.12
  196.6 60.1 all-gather.24
  258.9 21.6 all-gather.22
  282.8 56.2 all-gather.20
  342.1 53.5 all-gather.18
  397.9 21.4 all-gather.16
  435.5 33.0 reduce-scatter.10
  471.0 33.0 reduce-scatter.8
  508.2 71.6 reduce-scatter.16
  583.3 69.7 reduce-scatter.14
  656.7 76.7 reduce-scatter.18
  736.1 34.1 reduce-scatter.12

commit v2 on v1

v2 whole, which is shorter than its diff:
```python
from functools import partial
from types import SimpleNamespace
from typing import NamedTuple

import jax
import jax.numpy as jnp
from jax import lax
from jax.experimental import pallas as pl
from jax.experimental.pallas import tpu as pltpu
from jax.sharding import PartitionSpec as P

HEADS = 16
HEAD_DIM = 72
EPSILON = 1e-06
BF16 = jnp.bfloat16
F32 = jnp.float32


def layer_norm(values):
    center = values - jnp.mean(values, axis=-1, keepdims=True)
    inverse = lax.rsqrt(jnp.mean(center * center, axis=-1, keepdims=True) + EPSILON)
    return (center * inverse, inverse)


def norm_back(incoming, normed, inverse):
    return inverse * (
        incoming
        - jnp.mean(incoming, axis=-1, keepdims=True)
        - normed * jnp.mean(incoming * normed, axis=-1, keepdims=True)
    )


def dot(left, right):
    return jnp.dot(left, right, preferred_element_type=F32)


def dot_right_t(left, right):
    return lax.dot_general(left, right, (((1,), (1,)), ((), ())), preferred_element_type=F32)


def dot_left_t(left, right):
    return lax.dot_general(left, right, (((0,), (0,)), ((), ())), preferred_element_type=F32)


MESH = pl.DeviceIdType.MESH
ROOT = HEAD_DIM ** (-0.5)
LANES = 128
ROWS = 32


class Sizes:
    def __init__(self, dp, seq, latents, w_qkv, w_fc2):
        self.dp, self.seq, self.line = dp, seq, dp // 2
        self.count, self.tokens, self.width = latents.shape
        self.rows, self.units = w_qkv.shape[0], w_fc2.shape[0]
        self.chunk = seq * self.rows
        self.hidden = dp * self.units
        self.heads = HEADS // seq
        self.part = self.width // seq
        self.length = seq * self.tokens
        self.total = self.count * self.length
        self.own = self.count * self.tokens
        self.padded_rows = -(-self.rows // 16) * 16
        self.joined = -(-3 * self.part // LANES) * LANES
        self.mod_part = -(-6 * self.width // (seq * LANES)) * LANES

    def fits(self):
        return (
            self.seq == 4
            and self.dp % 2 == 0
            and self.dp == 8
            and self.count == 2
            and self.width == self.dp * self.chunk
            and self.chunk % 16 == 0
            and self.units % 16 == 0
            and self.tokens % 128 == 0
            and self.width % LANES == 0
            and self.hidden == self.width
            and self.chunk == self.units
        )


def column_cuts(width, most=512):
    cuts, start = [], 0
    while start < width:
        size = min(most, width - start)
        cuts.append((start, size))
        start += size
    return cuts


def one_hot(rows, columns, group, padded, flip):
    shape = (columns, rows) if flip else (rows, columns)
    tight = lax.broadcasted_iota(jnp.int32, shape, 1 if flip else 0)
    loose = lax.broadcasted_iota(jnp.int32, shape, 0 if flip else 1)
    hit = jnp.zeros(shape, F32)
    for index in range(rows // group):
        inside = (tight >= index * group) & (tight < (index + 1) * group)
        match = loose == tight + index * (padded - group)
        hit = jnp.where(inside & match, 1.0, hit)
    return hit.astype(BF16)


def block_kernel(sz, *refs):
    names = Inputs._fields + Outputs._fields + tuple(kernel_scratch(sz))
    r = SimpleNamespace(**dict(zip(names, refs)))
    dp_me, s_me = lax.axis_index("dp"), lax.axis_index("seq")
    z_me, x_me = dp_me // 2, dp_me % 2
    y_me, c_me = s_me // 2, s_me % 2
    count, tokens, width = sz.count, sz.tokens, sz.width
    line, seq = sz.line, sz.seq

    def seq_peer(mask):
        flip_y, flip_c = mask // 2, mask % 2
        y = 1 - y_me if flip_y else y_me
        c = 1 - c_me if flip_c else c_me
        return y * 2 + c

    def z_peer(step):
        return lax.rem(z_me + step, line)

    def device_seq(mask):
        return (dp_me, seq_peer(mask))

    def device_z(step):
        return (z_peer(step) * 2 + x_me, s_me)

    device_x = (z_me * 2 + (1 - x_me), s_me)
    used = [0, 0]

    def send(src, dst, device):
        index = used[0]
        used[0] += 1
        copy = pltpu.make_async_remote_copy(
            src_ref=src,
            dst_ref=dst,
            send_sem=r.send_sems.at[index],
            recv_sem=r.recv_sems.at[index],
            device_id=device,
            device_id_type=MESH,
        )
        copy.start()
        return copy

    def local(src, dst):
        index = used[1]
        used[1] += 1
        copy = pltpu.make_async_copy(src, dst, r.local_sems.at[index])
        copy.start()
        return copy

    def rows_of(ref, start, size):
        return ref.at[pl.ds(start, size)]

    peers = [device_seq(mask) for mask in (1, 2, 3)]
    peers += [device_z(step) for step in range(1, line)] + [device_x]
    barrier = pltpu.get_barrier_semaphore()
    for peer in peers:
        pl.semaphore_signal(barrier, inc=1, device_id=peer, device_id_type=MESH)
    pl.semaphore_wait(barrier, len(peers))

    pending = []
    far_moves = []
    sum_own = r.attended

    def release(copy):
        copy.wait_send()
        pending[:] = [item for item in pending if item is not copy]

    def token_rows(ref, latent, position):
        return rows_of(ref, (latent * seq + position) * tokens, tokens)

    class GatherTokens:
        def __init__(self, ref, latent, source=None):
            self.ref, self.latent = ref, latent
            slot = token_rows(ref, latent, s_me)
            mine = slot if source is None else source
            self.core = send(mine, slot, device_seq(1))
            self.chip = send(mine, slot, device_seq(2))

        def forward(self):
            self.chip.wait_recv()
            slot = token_rows(self.ref, self.latent, seq_peer(2))
            self.last = send(slot, slot, device_seq(1))

        def finish(self):
            self.core.wait_recv()
            self.last.wait_recv()
            for copy in (self.core, self.chip, self.last):
                pending.append(copy)

    class SumTokens:
        def __init__(self, part, slot, latent):
            self.part, self.slot, self.latent = part, slot, latent
            self.first = [
                send(
                    token_rows(part, latent, y * 2 + 1 - c_me),
                    r.sum_core.at[slot, y, latent],
                    device_seq(1),
                )
                for y in range(2)
            ]

        def forward(self):
            for copy in self.first:
                copy.wait_recv()
            other = 1 - y_me
            total = token_rows(self.part, self.latent, other * 2 + c_me)[...].astype(F32)
            total = total + r.sum_core[self.slot, other, self.latent].astype(F32)
            r.sum_send[self.slot, self.latent] = total.astype(BF16)
            self.last = send(
                r.sum_send.at[self.slot, self.latent],
                r.sum_chip.at[self.slot, self.latent],
                device_seq(2),
            )

        def finish(self):
            self.last.wait_recv()
            for copy in self.first + [self.last]:
                copy.wait_send()

        def rows(self, start):
            place = pl.ds((self.latent * seq + s_me) * tokens + start, ROWS)
            here = pl.ds(start, ROWS)
            total = self.part[place, :].astype(F32)
            total = total + r.sum_core[self.slot, y_me, self.latent, here, :].astype(F32)
            return total + r.sum_chip[self.slot, self.latent, here, :].astype(F32)

    def exchange(pick, place):
        return [send(pick(seq_peer(mask)), place(s_me), device_seq(mask)) for mask in (1, 2, 3)]

    def settle(copies):
        for copy in copies:
            copy.wait_recv()
        pending.extend(copies)

    class GatherWeights:
        def __init__(self, ref, chunk):
            self.ref, self.chunk = ref, chunk

        def slot(self, dp):
            return rows_of(self.ref, dp * self.chunk, self.chunk)

        def push(self, source=None):
            own = self.slot(dp_me)
            mine = own if source is None else source
            self.along = [send(mine, own, device_z(step)) for step in range(1, line)]
            self.across = [send(mine, own, device_x)]

        def forward(self):
            for step, copy in zip(range(1, line), self.along):
                copy.wait_recv()
                came = lax.rem(z_me + line - step, line) * 2 + x_me
                self.across.append(send(self.slot(came), self.slot(came), device_x))

        def finish(self):
            for copy in self.across:
                copy.wait_recv()

        def drain(self):
            for copy in self.along + self.across:
                copy.wait_send()

    class SumWeights:
        def __init__(self, ref, chunk, across_ref, along_ref, columns):
            self.ref, self.chunk, self.columns = ref, chunk, columns
            self.across_ref, self.along_ref = across_ref, along_ref

        def view(self, ref, index):
            return ref.at[index, :, pl.ds(0, self.columns)]

        def slot(self, dp):
            return rows_of(self.ref, dp * self.chunk, self.chunk)

        def push(self):
            self.across = []
            for step in range(line):
                z = lax.rem(z_me + step, line)
                self.across.append(
                    send(self.slot(z * 2 + 1 - x_me), self.view(self.across_ref, step), device_x)
                )

        def forward(self):
            self.along = []
            for step in list(range(1, line)) + [0]:
                self.across[step].wait_recv()
                z = lax.rem(z_me + step, line)
                slot = self.slot(z * 2 + x_me)
                total = slot[...].astype(F32) + self.view(self.across_ref, step)[...].astype(F32)
                if step:
                    slot[...] = total.astype(BF16)
                    self.along.append(send(slot, self.view(self.along_ref, step), device_z(step)))
                else:
                    sum_own[pl.ds(0, self.chunk), pl.ds(0, self.columns)] = total

        def finish(self):
            total = sum_own[pl.ds(0, self.chunk), pl.ds(0, self.columns)]
            for copy, step in zip(self.along, range(1, line)):
                copy.wait_recv()
                total = total + self.view(self.along_ref, step)[...].astype(F32)
            for copy in self.along + self.across:
                copy.wait_send()
            return total

    pad = sz.padded_rows
    qkv_blocks, fc1_blocks = r.qkv_blocks, r.fc1_blocks
    out_wide = sz.dp * pad
    out_mine = rows_of(r.out_blocks, s_me * out_wide, out_wide)

    cond = r.conditioning[...].astype(F32)
    gate_cond = 1.0 / (1.0 + jnp.exp(-cond))
    low_rows = jnp.concatenate([cond * gate_cond, jnp.zeros((16 - count, width), F32)], axis=0)
    rows_of(r.cond_all, dp_me * 16, 16)[...] = low_rows.astype(BF16)
    gather_cond = GatherWeights(r.cond_all, 16)
    gather_cond.push()
    qkv_moves = exchange(
        lambda peer: r.qkv_src.at[peer], lambda me: rows_of(qkv_blocks, me * pad, pad)
    )
    qkv_local = local(r.qkv_src.at[s_me], rows_of(qkv_blocks, s_me * pad, pad))
    lat_local, og_local = [
        [local(source.at[latent], token_rows(target, latent, s_me)) for latent in range(count)]
        for source, target in ((r.latents, r.lat_all), (r.out_grad, r.grad_branch))
    ]
    lat_moves = [
        GatherTokens(r.lat_all, latent, r.latents.at[latent]) for latent in range(count)
    ]
    fc1_local = local(r.fc1_src.at[s_me], rows_of(fc1_blocks, s_me * pad, pad))
    out_local = local(r.out_src, rows_of(out_mine, dp_me * pad, pad))
    fc2_local = local(r.fc2_src, rows_of(r.fc2, dp_me * sz.units, sz.units))

    def place(values, start, size):
        blank = jnp.zeros((1, size - values.shape[1]), F32)
        row = jnp.concatenate([values.astype(F32), blank], axis=1)
        return pltpu.roll(jnp.broadcast_to(row, (8, size)), start, 1)[0:1, :]

    def when(hit, values):
        return jnp.where(hit, values, jnp.zeros_like(values))

    me = dp_me * seq + s_me
    lengths = (6 * sz.rows, 2 * sz.rows, sz.rows, sz.units, sz.rows)
    starts = [sum(lengths[:index]) for index in range(len(lengths))]
    own_mod, own_qv, own_out, own_fc1, own_fc2 = [
        r.bias[:, start : start + size] for start, size in zip(starts, lengths)
    ]
    devices = sz.dp * seq
    half_way = devices // 2
    qv_row = place(own_qv, lax.rem(me, half_way) * (2 * sz.rows), width)
    fc1_row = place(own_fc1, dp_me * sz.units, width)
    bias_rows = [
        place(own_out, me * sz.rows, width),
        place(own_fc2, me * sz.rows, width),
        when(me < half_way, qv_row),
        when(me >= half_way, qv_row),
    ] + [when(s_me == position, fc1_row) for position in range(seq)]
    bias_rows.append(jnp.zeros((16 - len(bias_rows), width), F32))
    bias_mine = rows_of(r.bias_blocks, s_me * 16, 16)
    bias_mine[...] = jnp.concatenate(bias_rows, axis=0).astype(BF16)
    bias_moves = exchange(lambda peer: bias_mine, lambda me: rows_of(r.bias_blocks, me * 16, 16))

    tighten = one_hot(sz.chunk, seq * pad, sz.rows, pad, False)
    loosen = one_hot(sz.chunk, seq * pad, sz.rows, pad, True)
    gather_out = GatherWeights(out_mine, pad)
    gather_qkv = GatherWeights(r.qkv, sz.chunk)
    gather_fc1 = GatherWeights(r.fc1, sz.chunk)
    gather_fc2 = GatherWeights(r.fc2, sz.units)
    qkv_local.wait()
    settle(qkv_moves)
    rows_of(r.qkv, dp_me * sz.chunk, sz.chunk)[...] = dot(tighten, qkv_blocks[...]).astype(BF16)
    gather_qkv.push()

    gather_cond.forward()
    gather_cond.finish()
    iota = partial(lax.broadcasted_iota, jnp.int32)
    hit = iota((width, LANES), 0) == iota((width, LANES), 1) + me * sz.rows
    hit = hit & (iota((width, LANES), 1) < sz.rows)
    cond_mine = dot(r.cond_all[...], jnp.where(hit, 1.0, 0.0).astype(BF16)).astype(BF16)
    r.cond_mine[...] = cond_mine
    order = iota((16, sz.dp * 16), 0)
    across, along, which = order >> 3, (order >> 1) & (line - 1), order & 1
    hit = iota((16, sz.dp * 16), 1) == (along * 2 + across) * 16 + which
    cond_rows = dot(jnp.where(hit, 1.0, 0.0).astype(BF16), cond_mine).astype(BF16)
    cond_rows = cond_rows[:, : sz.rows]
    mod_wide = sz.mod_part * seq
    own_row = place(own_mod, me * (6 * sz.rows), mod_wide)
    for comp in range(6):
        here = slice(comp * width, (comp + 1) * width)
        r.mod_sums[:, here] = dot(cond_rows, r.w_mod[:, here]) + own_row[:, here]
    r.mod_sums[:, 6 * width :] = jnp.zeros((16, mod_wide - 6 * width), F32)

    def mod_part(position):
        return r.mod_sums.at[:, pl.ds(pl.multiple_of(position * sz.mod_part, LANES), sz.mod_part)]

    mod_core = [
        send(mod_part(y * 2 + 1 - c_me), r.mod_core.at[y], device_seq(1)) for y in range(2)
    ]
    for move in lat_moves:
        move.forward()
    fc1_moves = exchange(
        lambda peer: r.fc1_src.at[peer], lambda me: rows_of(fc1_blocks, me * pad, pad)
    )
    for copy in mod_core:
        copy.wait_recv()
    r.mod_send[...] = mod_part((1 - y_me) * 2 + c_me)[...] + r.mod_core[1 - y_me]
    mod_chip = send(r.mod_send, r.mod_chip, device_seq(2))
    settle(bias_moves)
    bias_sum = sum(
        r.bias_blocks[position * 16 : (position + 1) * 16, :].astype(F32) for position in range(seq)
    )
    rows_of(r.bias_all, dp_me * 16, 16)[...] = bias_sum.astype(BF16)
    gather_bias = GatherWeights(r.bias_all, 16)
    gather_bias.push()
    mod_chip.wait_recv()
    r.mod_sum[...] = mod_part(s_me)[...] + r.mod_core[y_me] + r.mod_chip[...]
    mod_x = send(rows_of(r.mod_sum, (1 - x_me) * 8, 8), r.mod_x, device_x)
    fc1_local.wait()
    settle(fc1_moves)
    rows_of(r.fc1, dp_me * sz.chunk, sz.chunk)[...] = dot(tighten, fc1_blocks[...]).astype(BF16)
    mod_x.wait_recv()
    r.mod_half[...] = rows_of(r.mod_sum, x_me * 8, 8)[...] + r.mod_x[...]
    mod_z = [send(r.mod_half, r.mod_z.at[step], device_z(step)) for step in range(1, line)]
    gather_bias.forward()
    gather_qkv.forward()
    gather_out.push(r.out_src)
    mod_total = r.mod_half[...]
    for copy, step in zip(mod_z, range(1, line)):
        copy.wait_recv()
        mod_total = mod_total + r.mod_z[step]
    hit = iota((8, sz.mod_part), 0)
    picked = [
        jnp.sum(jnp.where(hit == z_me * count + latent, mod_total, 0.0), axis=0, keepdims=True)
        for latent in range(count)
    ]
    picked.append(jnp.zeros((8 - count, sz.mod_part), F32))
    mod_slot = r.mod_all.at[s_me]
    mod_slot[...] = jnp.concatenate(picked, axis=0)
    mod_moves = [send(mod_slot, mod_slot, device_seq(mask)) for mask in (1, 2)]
    gather_out.forward()
    gather_fc1.push()
    og_moves = [
        GatherTokens(r.grad_branch, latent, r.out_grad.at[latent]) for latent in range(count)
    ]
    mod_moves[1].wait_recv()
    mod_slot = r.mod_all.at[seq_peer(2)]
    mod_moves.append(send(mod_slot, mod_slot, device_seq(1)))
    gather_bias.finish()
    bias = jnp.sum(r.bias_all[...].astype(F32).reshape(sz.dp, 16, width), axis=0)
    bias_out, bias_fc2 = bias[0:1, :], bias[1:2, :]
    part = sz.part

    def own_part(row):
        return sum(
            when(s_me == position, row[:, position * part : (position + 1) * part])
            for position in range(seq)
        )

    r.bias_joined[...] = jnp.concatenate(
        [
            own_part(bias[2:3, :]),
            jnp.zeros((1, part), F32),
            own_part(bias[3:4, :]),
            jnp.zeros((1, sz.joined - 3 * part), F32),
        ],
        axis=1,
    )
    r.bias_fc1[...] = sum(
        when(s_me == position, bias[4 + position : 5 + position, :]) for position in range(seq)
    )
    r.bias_out[...] = bias_out
    r.bias_fc2[...] = bias_fc2
    mod_moves[0].wait_recv()
    mod_moves[2].wait_recv()
    wide = jnp.concatenate([r.mod_all[position] for position in range(seq)], axis=1)
    mod = r.modulation
    for latent in range(count):
        for comp in range(6):
            mod[latent, comp : comp + 1, :] = wide[
                latent : latent + 1, comp * width : (comp + 1) * width
            ]
    pending.extend(mod_core + [mod_chip, mod_x] + mod_z + mod_moves)

    for copy in lat_local:
        copy.wait()
    for move in lat_moves:
        move.finish()

    heads, length = sz.heads, sz.length

    def modulate_tokens(step, carry):
        latent = step // (length // ROWS)
        here = pl.ds(pl.multiple_of(step * ROWS, ROWS), ROWS)
        normed, _ = layer_norm(r.lat_all[here, :].astype(F32))
        shift, scale = mod[latent, 0:1, :], mod[latent, 1:2, :]
        r.modded[here, :] = (normed * (1.0 + scale) + shift).astype(BF16)
        return carry

    lax.fori_loop(0, count * length // ROWS, modulate_tokens, 0)

    out_local.wait()
    gather_out.finish()
    out_core = send(out_mine, out_mine, device_seq(1))
    out_chip = send(out_mine, out_mine, device_seq(2))

    gather_qkv.finish()
    tile = 2 * tokens
    per_latent = length // tile

    def pad_head(values):
        return jnp.concatenate(
            [values, jnp.zeros((values.shape[0], LANES - HEAD_DIM), values.dtype)], axis=1
        )

    def project(step, carry):
        start = pl.multiple_of(step * tile, tile)
        latent = step // per_latent
        row = pl.multiple_of((step % per_latent) * tile, tile)
        joined = dot(r.modded[pl.ds(start, tile), :], r.qkv[...]) + r.bias_joined[...]
        for kind, target in enumerate((r.q_heads, r.k_heads, r.v_heads)):
            for head in range(heads):
                column = kind * part + head * HEAD_DIM
                piece = pad_head(joined[:, column : column + HEAD_DIM]).astype(BF16)
                target[latent * heads + head, pl.ds(row, tile), :] = piece
        return carry

    lax.fori_loop(0, count * per_latent, project, 0)

    half = length // 2

    def attend(index, carry):
        keys, values = r.k_heads[index], r.v_heads[index]

        def rows(step, carry):
            here = pl.ds(pl.multiple_of(step * half, half), half)
            scores = dot_right_t(r.q_heads[index, here, :], keys) * ROOT
            expon = jnp.exp(scores - jnp.max(scores, axis=-1, keepdims=True))
            soft = (expon * (1.0 / jnp.sum(expon, axis=-1, keepdims=True))).astype(BF16)
            r.soft[index, here, :] = soft
            r.o_heads[index, here, :] = dot(soft, values).astype(BF16)
            return carry

        return lax.fori_loop(0, 2, rows, carry)

    mixed_moves = []
    for latent in range(count):
        lax.fori_loop(latent * heads, (latent + 1) * heads, attend, 0)

        def assemble(block, carry, latent=latent):
            row = pl.multiple_of(block * tokens, tokens)
            pieces = [
                r.o_heads[latent * heads + head, pl.ds(row, tokens), :][:, :HEAD_DIM]
                for head in range(heads)
            ]
            r.mixed_send[block, latent] = jnp.concatenate(pieces, axis=1)
            return carry

        lax.fori_loop(0, seq, assemble, 0)
        own = local(r.mixed_send.at[s_me, latent], r.mixed_recv.at[s_me, latent])
        mixed_moves.append(
            (
                own,
                exchange(
                    lambda peer, latent=latent: r.mixed_send.at[peer, latent],
                    lambda me, latent=latent: r.mixed_recv.at[me, latent],
                ),
            )
        )
        if latent == 0:
            out_chip.wait_recv()
            other = rows_of(r.out_blocks, seq_peer(2) * out_wide, out_wide)
            out_last = send(other, other, device_seq(1))
            for move in og_moves:
                move.forward()
    gather_fc1.forward()
    fc2_local.wait()
    gather_fc2.push()

    for copy in og_local:
        copy.wait()
    for move in og_moves:
        move.finish()
    for move in lat_moves + og_moves:
        release(move.last)

    def gate_grads(step, carry):
        here = pl.ds(pl.multiple_of(step * ROWS, ROWS), ROWS)
        gate = mod[step // (length // ROWS), 5:6, :]
        r.grad_branch[here, :] = (r.grad_branch[here, :].astype(F32) * gate).astype(BF16)
        return carry

    lax.fori_loop(0, count * length // ROWS, gate_grads, 0)

    out_core.wait_recv()
    out_last.wait_recv()
    pending.extend([out_core, out_chip, out_last])

    def tighten_out(step, carry):
        blocks = [
            r.out_blocks[pl.ds(pl.multiple_of(block * out_wide + step * pad, 16), pad), :]
            for block in range(seq)
        ]
        start = pl.multiple_of(step * sz.chunk, 16)
        packed = dot(tighten, jnp.concatenate(blocks, axis=0))
        r.out[pl.ds(start, sz.chunk), :] = packed.astype(BF16)
        return carry

    lax.fori_loop(0, sz.dp, tighten_out, 0)

    gather_fc1.finish()
    m2_moves = []
    for latent in range(count):
        own, moves = mixed_moves[latent]
        own.wait()
        settle(moves)
        pieces = [r.mixed_recv[block, latent] for block in range(seq)]
        mixed = jnp.concatenate(pieces, axis=1)
        here = pl.ds(latent * tokens, tokens)
        r.mixed[here, :] = mixed
        r.attended[here, :] = dot(mixed, r.out[...]) + r.bias_out[...]

        def second_norm(step, carry, latent=latent):
            start = pl.multiple_of(step * ROWS, ROWS)
            here = pl.ds(latent * tokens + start, ROWS)
            tokens_in = r.latents[latent, pl.ds(start, ROWS), :].astype(F32)
            middle = tokens_in + mod[latent, 2:3, :] * r.attended[here, :]
            r.middle[here, :] = middle
            normed, _ = layer_norm(middle)
            modded = normed * (1.0 + mod[latent, 4:5, :]) + mod[latent, 3:4, :]
            place = pl.multiple_of((latent * seq + s_me) * tokens + start, ROWS)
            r.modded_two[pl.ds(place, ROWS), :] = modded.astype(BF16)
            return carry

        lax.fori_loop(0, tokens // ROWS, second_norm, 0)
        m2_moves.append(GatherTokens(r.modded_two, latent))

    gather_fc2.forward()
    for move in m2_moves:
        move.forward()
    gather_fc2.finish()

    cuts = column_cuts(sz.hidden, 256)
    r.fc1_sums[...] = jnp.zeros_like(r.fc1_sums)
    grad_moves = []
    for latent in range(count):
        m2_moves[latent].finish()

        def mlp(step, carry, latent=latent):
            start = pl.multiple_of(latent * length + step * tile, tile)
            rows = r.modded_two[pl.ds(start, tile), :]
            incoming = r.grad_branch[pl.ds(start, tile), :]
            for column, size in cuts:
                here = slice(column, column + size)
                hidden = dot(rows, r.fc1[:, here]) + r.bias_fc1[:, here]
                square = hidden * hidden
                inner = 0.7978845608028654 * (hidden + 0.044715 * square * hidden)
                bent = jnp.tanh(inner)
                r.lat_all[pl.ds(start, tile), here] = (0.5 * hidden * (1.0 + bent)).astype(BF16)
                slope = 0.5 * (1.0 + bent) + 0.5 * hidden * (1.0 - bent * bent) * (
                    0.7978845608028654 * (1.0 + 3 * 0.044715 * square)
                )
                grads = (dot_right_t(incoming, r.fc2[here, :]) * slope).astype(BF16)
                r.grad_hidden[pl.ds(start, tile), here] = grads
                r.fc1_sums[:, here] += jnp.sum(grads.astype(F32), axis=0, keepdims=True)
            return carry

        lax.fori_loop(0, per_latent, mlp, 0)

        def back_fc1(step, carry, latent=latent):
            start = pl.multiple_of(latent * length + step * tile, tile)
            rows = r.grad_hidden[pl.ds(start, tile), :]
            for column, size in column_cuts(width):
                here = slice(column, column + size)
                sums = dot_right_t(rows, r.fc1[here, :])
                r.part_a[pl.ds(start, tile), here] = sums.astype(BF16)
            return carry

        lax.fori_loop(0, per_latent, back_fc1, 0)
        grad_moves.append(SumTokens(r.part_a, 0, latent))

    for copy in (out_core, out_chip, out_last):
        release(copy)
    gather_out.drain()
    for latent in range(count):

        def branch_out(step, carry, latent=latent):
            start = pl.multiple_of(latent * length + step * tile, tile)
            sums = dot(r.lat_all[pl.ds(start, tile), :], r.fc2[...])
            r.out_blocks[pl.ds(start, tile), :] = sums.astype(BF16)
            return carry

        lax.fori_loop(0, per_latent, branch_out, 0)
        grad_moves[latent].forward()

    gather_fc2.drain()

    def weight_grad(left, right, target):
        size = 384 if width % 384 == 0 else LANES

        def tiles(step, carry):
            start = pl.multiple_of(step * size, LANES)
            sums = dot_left_t(left[:, pl.ds(start, size)], right[...])
            target[pl.ds(start, size), :] = sums.astype(BF16)
            return carry

        lax.fori_loop(0, left.shape[1] // size, tiles, 0)

    weight_grad(r.lat_all, r.grad_branch, r.fc2)
    sum_fc2 = SumWeights(r.fc2, sz.units, r.across_b, r.along_b, width)
    sum_fc2.push()

    grad_mod = r.grad_mod
    grad_mod[...] = jnp.zeros_like(grad_mod)

    def total_rows(values):
        return jnp.sum(values, axis=0, keepdims=True)

    r.bias_sums[...] = jnp.zeros_like(r.bias_sums)
    mix_moves = []
    for latent in range(count):
        grad_moves[latent].finish()

        def second_back(step, carry, latent=latent):
            start = pl.multiple_of(step * ROWS, ROWS)
            here = pl.ds(latent * tokens + start, ROWS)
            incoming = grad_moves[latent].rows(start)
            normed, inverse = layer_norm(r.middle[here, :])
            grad_mod[latent, 3:4, :] += total_rows(incoming)
            grad_mod[latent, 4:5, :] += total_rows(incoming * normed)
            grad_middle = r.out_grad[latent, pl.ds(start, ROWS), :].astype(F32) + norm_back(
                incoming * (1.0 + mod[latent, 4:5, :]), normed, inverse
            )
            r.grad_middle[here, :] = grad_middle
            grad_mod[latent, 2:3, :] += total_rows(grad_middle * r.attended[here, :])
            grad_attended = (mod[latent, 2:3, :] * grad_middle).astype(BF16)
            r.grad_attended[here, :] = grad_attended
            r.bias_sums[0:1, :] += total_rows(grad_attended.astype(F32))
            return carry

        lax.fori_loop(0, tokens // ROWS, second_back, 0)
        here = pl.ds(latent * tokens, tokens)
        grad_mixed = dot_right_t(r.grad_attended[here, :], r.out[...])
        for copy in mixed_moves[latent][1]:
            release(copy)
        for block in range(seq):
            piece = grad_mixed[:, block * part : (block + 1) * part].astype(BF16)
            r.mixed_send[block, latent] = piece
        own = local(r.mixed_send.at[s_me, latent], r.mixed_recv.at[s_me, latent])
        mix_moves.append(
            (
                own,
                exchange(
                    lambda peer, latent=latent: r.mixed_send.at[peer, latent],
                    lambda me, latent=latent: r.mixed_recv.at[me, latent],
                ),
            )
        )

    branch_moves = [SumTokens(r.out_blocks, 1, latent) for latent in range(count)]

    gather_fc1.drain()
    weight_grad(r.modded_two, r.grad_hidden, r.fc1)
    sum_fc1 = SumWeights(r.fc1, sz.chunk, r.across_a, r.along_a, sz.hidden)
    sum_fc2.forward()
    sum_fc1.push()
    for move in branch_moves:
        move.forward()

    def attend_back(index, carry):
        queries, keys, values = r.q_heads[index], r.k_heads[index], r.v_heads[index]
        incoming = r.o_heads[index]
        r.v_heads[index] = dot_left_t(r.soft[index], incoming).astype(BF16)

        def rows(step, carry):
            here = pl.ds(pl.multiple_of(step * half, half), half)
            soft = r.soft[index, here, :].astype(F32)
            grad_soft = dot_right_t(r.o_heads[index, here, :], values)
            delta = jnp.sum(soft * grad_soft, axis=-1, keepdims=True)
            r.soft[index, here, :] = (soft * (grad_soft - delta)).astype(BF16)
            return carry

        lax.fori_loop(0, 2, rows, 0)
        r.q_heads[index] = (dot(r.soft[index], keys) * ROOT).astype(BF16)
        r.k_heads[index] = (dot_left_t(r.soft[index], queries) * ROOT).astype(BF16)
        return carry

    joined_sums = r.joined_sums
    grad_joined = r.grad_hidden.at[:, pl.ds(0, sz.joined)]
    joined_sums[...] = jnp.zeros_like(joined_sums)
    token_moves = []
    for latent in range(count):
        own, moves = mix_moves[latent]
        own.wait()
        settle(moves)

        def unpack(block, carry, latent=latent):
            row = pl.multiple_of(block * tokens, tokens)
            values = r.mixed_recv[block, latent]
            for head in range(heads):
                piece = pad_head(values[:, head * HEAD_DIM : (head + 1) * HEAD_DIM])
                r.o_heads[latent * heads + head, pl.ds(row, tokens), :] = piece
            return carry

        lax.fori_loop(0, seq, unpack, 0)
        lax.fori_loop(latent * heads, (latent + 1) * heads, attend_back, 0)

        def join(block, carry, latent=latent):
            row = pl.multiple_of(block * tokens, tokens)
            start = pl.multiple_of(latent * length + block * tokens, tokens)
            pieces = [
                source[latent * heads + head, pl.ds(row, tokens), :][:, :HEAD_DIM]
                for source in (r.q_heads, r.k_heads, r.v_heads)
                for head in range(heads)
            ]
            if sz.joined > 3 * part:
                pieces.append(jnp.zeros((tokens, sz.joined - 3 * part), BF16))
            values = jnp.concatenate(pieces, axis=1)
            joined_sums[...] += total_rows(values.astype(F32))
            grad_joined[pl.ds(start, tokens), :] = values
            return carry

        lax.fori_loop(0, seq, join, 0)

        def back_qkv(step, carry, latent=latent):
            start = pl.multiple_of(latent * length + step * tile, tile)
            rows = grad_joined[pl.ds(start, tile), :]
            for column, size in column_cuts(width):
                here = slice(column, column + size)
                sums = dot_right_t(rows, r.qkv[here, :])
                r.part_a[pl.ds(start, tile), here] = sums.astype(BF16)
            return carry

        lax.fori_loop(0, per_latent, back_qkv, 0)
        token_moves.append(SumTokens(r.part_a, 0, latent))
        if latent == 0:
            fc2_rows = rows_of(sum_own, 0, sz.units)
            fc2_rows[...] = sum_fc2.finish()
            local(fc2_rows, r.fc2_out).wait()
            sum_fc1.forward()

    gather_qkv.drain()
    weight_grad(r.modded, grad_joined, r.qkv)
    for move in token_moves:
        move.forward()

    sum_qkv = SumWeights(r.qkv, sz.chunk, r.across_b, r.along_b, sz.joined)
    sum_qkv.push()

    for move in m2_moves:
        for copy in (move.core, move.chip, move.last):
            release(copy)
    for latent in range(count):
        branch_moves[latent].finish()

        def final_output(step, carry, latent=latent):
            start = pl.multiple_of(step * ROWS, ROWS)
            here = pl.ds(latent * tokens + start, ROWS)
            branch = branch_moves[latent].rows(start) + r.bias_fc2[...]
            grad_output = r.out_grad[latent, pl.ds(start, ROWS), :].astype(F32)
            gate = mod[latent, 5:6, :]
            r.modded_two[here, :] = (r.middle[here, :] + gate * branch).astype(BF16)
            grad_mod[latent, 5:6, :] += total_rows(grad_output * branch)
            r.bias_sums[1:2, :] += total_rows((gate * grad_output).astype(BF16).astype(F32))
            return carry

        lax.fori_loop(0, tokens // ROWS, final_output, 0)
        slot = rows_of(r.modded_two, latent * tokens, tokens)
        far_moves.append(local(slot, r.output.at[latent]))
    for latent in range(count):
        token_moves[latent].finish()

        def final_grads(step, carry, latent=latent):
            start = pl.multiple_of(step * ROWS, ROWS)
            here = pl.ds(latent * tokens + start, ROWS)
            incoming = token_moves[latent].rows(start)
            normed, inverse = layer_norm(r.latents[latent, pl.ds(start, ROWS), :].astype(F32))
            grad_mod[latent, 0:1, :] += total_rows(incoming)
            grad_mod[latent, 1:2, :] += total_rows(incoming * normed)
            grads = r.grad_middle[here, :] + norm_back(
                incoming * (1.0 + mod[latent, 1:2, :]), normed, inverse
            )
            place = pl.ds((count + latent) * tokens + start, ROWS)
            r.modded_two[place, :] = grads.astype(BF16)
            return carry

        lax.fori_loop(0, tokens // ROWS, final_grads, 0)
        slot = rows_of(r.modded_two, (count + latent) * tokens, tokens)
        far_moves.append(local(slot, r.latents_grad.at[latent]))

    weight_grad(r.mixed, r.grad_attended, r.out)

    def loosen_out(step, carry):
        start = pl.multiple_of(step * sz.chunk, 16)
        spread = dot(loosen, r.out[pl.ds(start, sz.chunk), :]).astype(BF16)
        for block in range(seq):
            place = pl.multiple_of(block * out_wide + step * pad, 16)
            r.out_blocks[pl.ds(place, pad), :] = spread[block * pad : (block + 1) * pad, :]
        return carry

    lax.fori_loop(0, sz.dp, loosen_out, 0)
    out_first = [
        send(
            rows_of(r.out_blocks, (y * 2 + 1 - c_me) * out_wide, out_wide),
            rows_of(r.lat_all, y * out_wide, out_wide),
            device_seq(1),
        )
        for y in range(2)
    ]

    def return_rows(total, send_ref, recv_ref):
        send_ref[...] = dot(loosen, total.astype(BF16)).astype(BF16)
        mine = rows_of(send_ref, s_me * pad, pad)
        own = local(mine, rows_of(recv_ref, s_me * pad, pad))
        moves = exchange(
            lambda peer: rows_of(send_ref, peer * pad, pad),
            lambda me: rows_of(recv_ref, me * pad, pad),
        )
        return own, moves

    def small(values):
        return values.reshape(count * 8, width)

    r.grad_core_send[...] = small(grad_mod[...])
    mod_core = send(r.grad_core_send, r.grad_core, device_seq(1))

    def own_place(sums, column):
        return place(sums[:, column : column + part], s_me * part, width)

    sums = joined_sums[...]
    r.bias_sums[2:3, :] = own_place(sums, 0)
    r.bias_sums[3:4, :] = own_place(sums, 2 * part)
    for position in range(seq):
        r.bias_sums[4 + position : 5 + position, :] = when(s_me == position, r.fc1_sums[...])
    bias_x = send(r.bias_sums, r.bias_x, device_x)
    mod_core.wait_recv()
    r.grad_chip_send[...] = r.grad_core_send[...] + r.grad_core[...]
    mod_chip = send(r.grad_chip_send, r.grad_chip, device_seq(2))
    bias_x.wait_recv()
    r.bias_half[...] = r.bias_sums[...] + r.bias_x[...]
    bias_z = [send(r.bias_half, r.bias_z.at[step], device_z(step)) for step in range(1, line)]
    mod_chip.wait_recv()
    rows_of(r.grad_all, dp_me * 16, 16)[...] = (r.grad_chip_send[...] + r.grad_chip[...]).astype(
        BF16
    )
    gather_grad = GatherWeights(r.grad_all, 16)
    gather_grad.push()
    pending.extend([mod_core, bias_x, mod_chip] + bias_z)

    for copy in out_first:
        copy.wait_recv()

    def out_from_core(y):
        return rows_of(r.lat_all, y * out_wide, out_wide)[...].astype(F32)

    other = rows_of(r.out_blocks, ((1 - y_me) * 2 + c_me) * out_wide, out_wide)
    other[...] = (other[...].astype(F32) + out_from_core(1 - y_me)).astype(BF16)
    out_chip_sum = rows_of(r.grad_branch, 0, out_wide)
    out_second = send(other, out_chip_sum, device_seq(2))

    for copy in fc1_moves:
        release(copy)
    fc1_own, fc1_back = return_rows(sum_fc1.finish(), r.fc1_blocks, r.fc1_rows)
    sum_qkv.forward()
    gather_grad.forward()
    bias_total = r.bias_half[...]
    for copy, step in zip(bias_z, range(1, line)):
        copy.wait_recv()
        bias_total = bias_total + r.bias_z[step]
    r.bias_line[...] = bias_total
    bias_core = send(r.bias_line, r.bias_core, device_seq(1))

    out_second.wait_recv()
    mine = out_mine[...].astype(F32) + out_from_core(y_me)
    out_mine[...] = (mine + out_chip_sum[...].astype(F32)).astype(BF16)
    pending.extend(out_first + [out_second])
    sum_out = SumWeights(out_mine, pad, r.across_out, r.along_out, width)
    sum_out.push()

    gather_grad.finish()
    all_grads = r.grad_all[...]
    rows = sz.dp * 16
    comp_of = iota((rows, rows), 0) & 7
    source = (iota((rows, rows), 0) & ~15) + ((iota((rows, rows), 0) >> 3) & 1)
    spread = jnp.where(iota((rows, rows), 1) == source, 1.0, 0.0).astype(BF16)
    cond_spread = dot(spread, r.cond_mine[...])
    comp_of = iota((rows, LANES), 0) & 7
    cond_grads = jnp.zeros((rows, sz.rows), F32)
    mod_rows = r.mod_out.shape[0]
    for comp in range(6):
        here = slice(comp * width, (comp + 1) * width)
        chosen = jnp.where(comp_of == comp, cond_spread, 0.0).astype(BF16)
        place_rows = rows_of(r.grad_middle, comp * mod_rows, mod_rows)
        place_rows[...] = dot_left_t(chosen, all_grads)[:mod_rows, :]
        far_moves.append(local(place_rows, r.mod_out.at[:, pl.ds(comp * width, width)]))
        back = dot_right_t(all_grads, r.w_mod[:, here])
        cond_grads = cond_grads + jnp.where(comp_of[:, : sz.rows] == comp, back, 0.0)
    cond_grads = jnp.sum(cond_grads.reshape(rows // 8, 8, sz.rows), axis=1)
    blank = jnp.zeros((16, width - sz.rows), F32)
    cond_grads = pltpu.roll(jnp.concatenate([cond_grads, blank], axis=1), me * sz.rows, 1)
    keep = iota((8, 16), 0)
    hits = []
    for side in range(2):
        hits.append(
            sum(
                when(
                    iota((8, width), 0) == along * count + latent,
                    jnp.broadcast_to(
                        cond_grads[
                            (along * 2 + side) * count + latent : (along * 2 + side) * count
                            + latent
                            + 1,
                            :,
                        ],
                        (8, width),
                    ),
                )
                for along in range(line)
                for latent in range(count)
            )
        )
    r.cond_sides[0] = hits[0]
    r.cond_sides[1] = hits[1]
    cond_x = send(r.cond_sides.at[1 - x_me], r.cond_x, device_x)
    bias_core.wait_recv()
    r.bias_pair[...] = r.bias_line[...] + r.bias_core[...]
    bias_chip = send(r.bias_pair, r.bias_chip, device_seq(2))
    comp_rows = iota((8, rows), 0) == (iota((8, rows), 1) & 7)
    mod_bias = dot(jnp.where(comp_rows, 1.0, 0.0).astype(BF16), all_grads)
    cond_x.wait_recv()
    r.cond_half[...] = r.cond_sides[x_me] + r.cond_x[...]
    cond_z = [send(r.cond_half, r.cond_z.at[step], device_z(step)) for step in range(1, line)]
    bias_chip.wait_recv()
    bias_full = r.bias_pair[...] + r.bias_chip[...]

    def own_lanes(row, start):
        size = row.shape[1]
        turned = pltpu.roll(jnp.broadcast_to(row, (8, size)), lax.rem(size - start, size), 1)
        return turned[0:1, : 2 * LANES]

    qv_total = when(me < half_way, bias_full[2:3, :]) + when(me >= half_way, bias_full[3:4, :])
    fc1_total = sum(
        when(s_me == position, bias_full[4 + position : 5 + position, :])
        for position in range(seq)
    )
    first = me * (6 * sz.rows) // width
    comp_row = iota((8, width), 0)
    pair = [
        jnp.sum(jnp.where(comp_row == first + more, mod_bias, 0.0), axis=0, keepdims=True)
        for more in range(2)
    ]
    r.small_out[...] = jnp.concatenate(
        [
            own_lanes(bias_full[0:1, :], me * sz.rows),
            own_lanes(bias_full[1:2, :], me * sz.rows),
            own_lanes(qv_total, lax.rem(me, half_way) * (2 * sz.rows)),
            own_lanes(fc1_total, dp_me * sz.units),
            own_lanes(jnp.concatenate(pair, axis=1), me * (6 * sz.rows) - first * width),
            jnp.zeros((3, 2 * LANES), F32),
        ],
        axis=0,
    )
    for copy in qkv_moves:
        release(copy)
    qkv_own, qkv_back = return_rows(sum_qkv.finish(), r.qkv_blocks, r.qkv_rows)
    sum_out.forward()
    cond_total = r.cond_half[...]
    for copy, step in zip(cond_z, range(1, line)):
        copy.wait_recv()
        cond_total = cond_total + r.cond_z[step]
    r.cond_line[...] = cond_total
    cond_core = send(r.cond_line, r.cond_core, device_seq(1))
    r.out_out[...] = sum_out.finish()
    cond_core.wait_recv()
    r.cond_pair[...] = r.cond_line[...] + r.cond_core[...]
    cond_chip = send(r.cond_pair, r.cond_chip, device_seq(2))
    gather_grad.drain()
    gather_bias.drain()
    gather_cond.drain()
    cond_chip.wait_recv()
    cond_full = r.cond_pair[...] + r.cond_chip[...]
    picked = [
        jnp.sum(
            jnp.where(comp_row == z_me * count + latent, cond_full, 0.0), axis=0, keepdims=True
        )
        for latent in range(count)
    ]
    slope = gate_cond * (1.0 + cond * (1.0 - gate_cond))
    r.cond_grad[...] = (jnp.concatenate(picked, axis=0) * slope).astype(BF16)
    pending.extend([bias_core, bias_chip, cond_x, cond_core, cond_chip] + cond_z)
    for own, moves in ((fc1_own, fc1_back), (qkv_own, qkv_back)):
        own.wait()
        settle(moves)
    far_moves.append(local(r.fc1_rows, r.fc1_out))
    far_moves.append(local(r.qkv_rows, r.qkv_out))
    for copy in far_moves:
        copy.wait()
    for copy in pending:
        copy.wait_send()


class Inputs(NamedTuple):
    latents: object
    out_grad: object
    conditioning: object
    bias: object
    w_mod: object
    qkv_src: object
    fc1_src: object
    out_src: object
    fc2_src: object


class Outputs(NamedTuple):
    output: object
    latents_grad: object
    cond_grad: object
    mod_out: object
    small_out: object
    qkv_out: object
    out_out: object
    fc1_out: object
    fc2_out: object


def kernel_scratch(sz):
    low = lambda *shape: pltpu.VMEM(shape, BF16)
    full = lambda *shape: pltpu.VMEM(shape, F32)
    count, tokens, width, seq = sz.count, sz.tokens, sz.width, sz.seq
    pad, groups = sz.padded_rows, sz.count * sz.heads
    tall = sz.chunk if sz.chunk > sz.units else sz.units
    wide = max(sz.joined, sz.hidden, width)
    return dict(
        lat_all=low(sz.total, max(width, sz.hidden)),
        grad_branch=low(sz.total, width),
        modded=low(sz.total, width),
        q_heads=low(groups, sz.length, LANES),
        k_heads=low(groups, sz.length, LANES),
        v_heads=low(groups, sz.length, LANES),
        o_heads=low(groups, sz.length, LANES),
        soft=low(groups, sz.length, sz.length),
        mixed_send=low(seq, count, tokens, sz.part),
        mixed_recv=low(seq, count, tokens, sz.part),
        mixed=low(sz.own, width),
        attended=full(sz.own, width),
        middle=full(sz.own, width),
        grad_middle=full(sz.own, width),
        grad_attended=low(sz.own, width),
        modded_two=low(sz.total, width),
        grad_hidden=low(sz.total, sz.hidden),
        part_a=low(sz.total, width),
        sum_core=low(2, 2, count, tokens, width),
        sum_send=low(2, count, tokens, width),
        sum_chip=low(2, count, tokens, width),
        qkv_blocks=low(seq * pad, sz.joined),
        fc1_blocks=low(seq * pad, sz.hidden),
        qkv_rows=low(seq * pad, sz.joined),
        fc1_rows=low(seq * pad, sz.hidden),
        out_blocks=low(seq * sz.dp * pad, width),
        qkv=low(width, sz.joined),
        fc1=low(width, sz.hidden),
        fc2=low(sz.hidden, width),
        out=low(width, width),
        across_a=low(sz.line, sz.chunk, wide),
        along_a=low(sz.line, sz.chunk, wide),
        across_b=low(sz.line, tall, wide),
        along_b=low(sz.line, tall, wide),
        across_out=low(sz.line, pad, width),
        along_out=low(sz.line, pad, width),
        cond_all=low(sz.dp * 16, width),
        cond_mine=low(sz.dp * 16, LANES),
        bias_blocks=low(seq * 16, width),
        bias_all=low(sz.dp * 16, width),
        mod_sums=full(16, sz.mod_part * seq),
        mod_core=full(2, 16, sz.mod_part),
        mod_send=full(16, sz.mod_part),
        mod_chip=full(16, sz.mod_part),
        mod_sum=full(16, sz.mod_part),
        mod_x=full(8, sz.mod_part),
        mod_half=full(8, sz.mod_part),
        mod_z=full(sz.line, 8, sz.mod_part),
        mod_all=full(seq, 8, sz.mod_part),
        modulation=full(count, 8, width),
        bias_joined=full(1, sz.joined),
        bias_out=full(1, width),
        bias_fc1=full(1, width),
        bias_fc2=full(1, width),
        joined_sums=full(1, sz.joined),
        fc1_sums=full(1, sz.hidden),
        grad_mod=full(count, 8, width),
        grad_core_send=full(16, width),
        grad_core=full(16, width),
        grad_chip_send=full(16, width),
        grad_chip=full(16, width),
        grad_all=low(sz.dp * 16, width),
        bias_sums=full(8, width),
        bias_x=full(8, width),
        bias_half=full(8, width),
        bias_z=full(sz.line, 8, width),
        bias_line=full(8, width),
        bias_core=full(8, width),
        bias_pair=full(8, width),
        bias_chip=full(8, width),
        cond_sides=full(2, 8, width),
        cond_x=full(8, width),
        cond_half=full(8, width),
        cond_z=full(sz.line, 8, width),
        cond_line=full(8, width),
        cond_core=full(8, width),
        cond_pair=full(8, width),
        cond_chip=full(8, width),
        send_sems=pltpu.SemaphoreType.DMA((200,)),
        recv_sems=pltpu.SemaphoreType.DMA((200,)),
        local_sems=pltpu.SemaphoreType.DMA((40,)),
    )


def kernel_outputs(sz):
    low = lambda *shape: jax.ShapeDtypeStruct(shape, BF16)
    full = lambda *shape: jax.ShapeDtypeStruct(shape, F32)
    count, tokens, width, pad = sz.count, sz.tokens, sz.width, sz.padded_rows
    return [
        low(count, tokens, width),
        low(count, tokens, width),
        low(count, width),
        full(-(-sz.rows // 8) * 8, 6 * width),
        full(8, 2 * LANES),
        low(sz.seq * pad, sz.joined),
        full(pad, width),
        low(sz.seq * pad, sz.hidden),
        full(sz.units, width),
    ]


def run_kernel(sz, *operands):
    vmem = pl.BlockSpec(memory_space=pltpu.VMEM)
    far = pl.BlockSpec(memory_space=pl.ANY)
    outputs = kernel_outputs(sz)
    return pl.pallas_call(
        partial(block_kernel, sz),
        out_shape=outputs,
        in_specs=[vmem] * 5 + [far] * 4,
        out_specs=[far, far, vmem, far, vmem, far, vmem, far, far],
        scratch_shapes=list(kernel_scratch(sz).values()),
        compiler_params=pltpu.CompilerParams(
            collective_id=0, has_side_effects=True, vmem_limit_bytes=66584576
        ),
    )(*operands)


def general_path(
    latents, out_grad, modulation, blocks, w_out, w_fc2, bias_qv, bias_out, bias_fc1, bias_fc2
):
    count, tokens, width = latents.shape
    dp, seq = lax.axis_size("dp"), lax.axis_size("seq")
    both = ("dp", "seq")
    qkv_blocks, fc1_blocks = blocks
    rows = qkv_blocks.shape[1]
    part, heads, length = width // seq, HEADS // seq, seq * tokens
    shift_att, scale_att, gate_att, shift_mlp, scale_mlp, gate_mlp = [
        modulation[:, index : index + 1] for index in range(6)
    ]

    def to_columns(blocks):
        mine = lax.all_to_all(blocks, "seq", 0, 0, tiled=True).reshape(seq * rows, -1)
        return lax.all_gather(mine, "dp", axis=0, tiled=True)

    full_qkv = to_columns(qkv_blocks)
    full_out = lax.all_gather(w_out, both, axis=0, tiled=True)
    full_fc1 = to_columns(fc1_blocks)
    full_fc2 = lax.all_gather(w_fc2, "dp", axis=0, tiled=True)

    def gather_tokens(values):
        return lax.all_gather(values, "seq", axis=1, tiled=True)

    def flat(values):
        return values.reshape(-1, values.shape[-1])

    tokens_f = latents.astype(F32)
    normed, inverse = layer_norm(tokens_f)
    modded = (normed * (1.0 + scale_att) + shift_att).astype(BF16)
    modded_all = flat(gather_tokens(modded))
    joined = dot(modded_all, full_qkv).reshape(count, length, 3, heads, HEAD_DIM)
    bias_q = bias_qv[0].reshape(heads, HEAD_DIM)
    bias_v = bias_qv[1].reshape(heads, HEAD_DIM)
    queries = (joined[:, :, 0] + bias_q).astype(BF16)
    keys = joined[:, :, 1].astype(BF16)
    values = (joined[:, :, 2] + bias_v).astype(BF16)
    scores = jnp.einsum("bqhd,bkhd->bhqk", queries, keys, preferred_element_type=F32) * (
        HEAD_DIM ** (-0.5)
    )
    soft = jax.nn.softmax(scores, axis=-1)
    soft_low = soft.astype(BF16)
    mixed = jnp.einsum("bhqk,bkhd->bqhd", soft_low, values, preferred_element_type=F32)
    mixed = mixed.astype(BF16).reshape(count, length, part)
    mixed_mine = lax.all_to_all(mixed, "seq", 1, 2, tiled=True)
    attended = dot(mixed_mine, full_out) + bias_out
    middle = tokens_f + gate_att * attended
    normed_two, inverse_two = layer_norm(middle)
    modded_two = (normed_two * (1.0 + scale_mlp) + shift_mlp).astype(BF16)
    modded_two_all = flat(gather_tokens(modded_two))
    hidden = dot(modded_two_all, full_fc1) + bias_fc1
    active, gelu_back = jax.vjp(partial(jax.nn.gelu, approximate=True), hidden)
    active = active.astype(BF16)

    def sum_tokens(partial_sums):
        parts = partial_sums.astype(BF16).reshape(count, length, width)
        return lax.psum_scatter(parts, "seq", scatter_dimension=1, tiled=True).astype(F32)

    branch = sum_tokens(dot(active, full_fc2)) + bias_fc2
    output = middle + gate_mlp * branch

    grad_output = out_grad.astype(F32)
    grad_gate_mlp = jnp.sum(grad_output * branch, axis=1)
    grad_branch = (gate_mlp * grad_output).astype(BF16)
    grad_branch_all = flat(gather_tokens(grad_branch))
    grad_hidden = gelu_back(dot_right_t(grad_branch_all, full_fc2))[0].astype(BF16)
    grad_modded_two = sum_tokens(dot_right_t(grad_hidden, full_fc1))
    grad_shift_mlp = jnp.sum(grad_modded_two, axis=1)
    grad_scale_mlp = jnp.sum(grad_modded_two * normed_two, axis=1)
    grad_middle = grad_output + norm_back(
        grad_modded_two * (1.0 + scale_mlp), normed_two, inverse_two
    )
    grad_gate_att = jnp.sum(grad_middle * attended, axis=1)
    grad_attended = (gate_att * grad_middle).astype(BF16)
    grad_mixed = dot_right_t(flat(grad_attended), full_out).astype(BF16)
    grad_mixed = lax.all_to_all(grad_mixed.reshape(latents.shape), "seq", 2, 1, tiled=True)
    grad_mixed = grad_mixed.reshape(count, length, heads, HEAD_DIM)
    grad_soft = jnp.einsum("bqhd,bkhd->bhqk", grad_mixed, values, preferred_element_type=F32)
    delta = jnp.sum(soft * grad_soft, axis=-1, keepdims=True)
    grad_scores = (soft * (grad_soft - delta)).astype(BF16)
    scale = HEAD_DIM ** (-0.5)
    grad_q = jnp.einsum("bhqk,bkhd->bqhd", grad_scores, keys, preferred_element_type=F32) * scale
    grad_k = jnp.einsum("bhqk,bqhd->bkhd", grad_scores, queries, preferred_element_type=F32) * scale
    grad_v = jnp.einsum("bhqk,bqhd->bkhd", soft_low, grad_mixed, preferred_element_type=F32)
    grad_joined = jnp.concatenate(
        [item.astype(BF16).reshape(count * length, part) for item in (grad_q, grad_k, grad_v)],
        axis=1,
    )
    grad_modded = sum_tokens(dot_right_t(grad_joined, full_qkv))
    grad_shift_att = jnp.sum(grad_modded, axis=1)
    grad_scale_att = jnp.sum(grad_modded * normed, axis=1)
    grad_tokens = grad_middle + norm_back(grad_modded * (1.0 + scale_att), normed, inverse)

    def from_columns(sums, groups):
        mine = lax.psum_scatter(sums.astype(BF16), "dp", scatter_dimension=0, tiled=True)
        blocks = lax.all_to_all(mine.reshape(seq, rows, -1), "seq", 0, 0, tiled=True)
        blocks = blocks.astype(F32).reshape(seq, rows, groups, -1)
        return blocks.transpose(1, 2, 0, 3).reshape(rows, -1)

    sums_fc2 = lax.psum_scatter(
        dot_left_t(active, grad_branch_all).astype(BF16), "dp", scatter_dimension=0, tiled=True
    ).astype(F32)
    sums_fc1 = from_columns(dot_left_t(modded_two_all, grad_hidden), dp)
    sums_out = lax.psum_scatter(
        dot_left_t(flat(mixed_mine), flat(grad_attended)).astype(BF16),
        both,
        scatter_dimension=0,
        tiled=True,
    ).astype(F32)
    sums_qkv = from_columns(dot_left_t(modded_all, grad_joined), 3)

    grad_mod = jnp.stack(
        [
            grad_shift_att,
            grad_scale_att,
            grad_gate_att,
            grad_shift_mlp,
            grad_scale_mlp,
            grad_gate_mlp,
        ],
        axis=1,
    )
    bias_sums = [
        jnp.sum(item.astype(F32), axis=0)
        for item in (grad_joined, flat(grad_attended), grad_hidden, flat(grad_branch))
    ]
    weight_sums = [sums_qkv, sums_out, sums_fc1, sums_fc2]
    return output.astype(BF16), grad_tokens.astype(BF16), grad_mod, bias_sums, weight_sums


def kernel_path(sz, latents, conditioning, w_mod, w_qkv, w_out, w_fc1, w_fc2, biases, out_grad):
    more = sz.padded_rows - sz.rows
    gap = sz.joined - 3 * sz.part
    part, seq, pad, rows = sz.part, sz.seq, sz.padded_rows, sz.rows
    qkv_blocks, fc1_blocks = column_blocks(seq, sz.dp, w_qkv, w_fc1, sz.units)
    output, grad_tokens, grad_cond, sums_mod, small, sums_qkv, sums_out, sums_fc1, sums_fc2 = (
        run_kernel(
            sz,
            latents,
            out_grad,
            conditioning,
            jnp.concatenate(biases).reshape(1, -1),
            w_mod,
            jnp.pad(qkv_blocks, ((0, 0), (0, more), (0, gap))),
            jnp.pad(fc1_blocks, ((0, 0), (0, more), (0, 0))),
            jnp.pad(w_out, ((0, more), (0, 0))),
            w_fc2,
        )
    )

    def spread(sums, columns, groups):
        sums = sums.reshape(seq, pad, -1)[:, :rows, :columns].astype(F32)
        return sums.reshape(seq, rows, groups, -1).transpose(1, 2, 0, 3).reshape(rows, -1)

    return (
        output,
        grad_tokens,
        grad_cond,
        sums_mod[:rows],
        small[4, : 6 * rows],
        spread(sums_qkv, 3 * part, 3),
        small[2, : 2 * rows],
        sums_out[:rows],
        small[0, :rows],
        spread(sums_fc1, sz.hidden, sz.dp),
        small[3, : sz.units],
        sums_fc2,
        small[1, :rows],
    )


def column_blocks(seq, dp, w_qkv, w_fc1, units):
    rows = w_qkv.shape[0]
    qkv_blocks = w_qkv.reshape(rows, 3, seq, -1).transpose(2, 0, 1, 3).reshape(seq, rows, -1)
    fc1_blocks = w_fc1.reshape(rows, dp, seq, units).transpose(2, 0, 1, 3).reshape(seq, rows, -1)
    return qkv_blocks, fc1_blocks


def body(
    latents,
    conditioning,
    w_mod,
    b_mod,
    w_qkv,
    b_qv,
    w_out,
    b_out,
    w_fc1,
    b_fc1,
    w_fc2,
    b_fc2,
    out_grad,
):
    count, tokens, width = latents.shape
    dp, seq = lax.axis_size("dp"), lax.axis_size("seq")
    sz = Sizes(dp, seq, latents, w_qkv, w_fc2)
    if sz.fits():
        biases = (b_mod, b_qv, b_out, b_fc1, b_fc2)
        return kernel_path(
            sz, latents, conditioning, w_mod, w_qkv, w_out, w_fc1, w_fc2, biases, out_grad
        )
    both = ("dp", "seq")
    my_dp, my_seq = lax.axis_index("dp"), lax.axis_index("seq")
    me = my_dp * seq + my_seq
    rows, units = w_qkv.shape[0], w_fc2.shape[0]
    part = width // seq

    cond = conditioning.astype(F32)
    cond_act, silu_back = jax.vjp(jax.nn.silu, cond)
    cond_low = lax.all_gather(cond_act.astype(BF16), "dp", axis=0, tiled=True)
    cond_mine = lax.dynamic_slice_in_dim(cond_low, me * rows, rows, axis=1)
    mod_part = dot(cond_mine, w_mod)
    mod_sum = lax.psum(lax.psum_scatter(mod_part, "dp", scatter_dimension=0, tiled=True), "seq")
    biases = lax.all_gather(jnp.concatenate([b_mod, b_qv, b_out, b_fc1, b_fc2]), both, axis=0)
    pieces, start = [], 0
    for item in (b_mod, b_qv, b_out, b_fc1, b_fc2):
        pieces.append(biases[:, start : start + item.shape[0]].reshape(-1).astype(F32))
        start += item.shape[0]
    bias_mod, bias_qv, bias_out, bias_fc1, bias_fc2 = pieces
    bias_qv = lax.dynamic_index_in_dim(bias_qv.reshape(2, seq, part), my_seq, 1, keepdims=False)
    bias_fc1 = lax.dynamic_index_in_dim(
        bias_fc1.reshape(dp, seq, units), my_seq, 1, keepdims=False
    ).reshape(-1)
    modulation = (mod_sum + bias_mod).reshape(count, 6, width)

    blocks = column_blocks(seq, dp, w_qkv, w_fc1, units)
    output, grad_tokens, grad_mod, bias_sums, weight_sums = general_path(
        latents,
        out_grad,
        modulation,
        blocks,
        w_out,
        w_fc2,
        bias_qv,
        bias_out,
        bias_fc1,
        bias_fc2,
    )
    sums_qkv, sums_out, sums_fc1, sums_fc2 = weight_sums

    grad_mod = grad_mod.reshape(count, -1)
    grad_mod = lax.psum(grad_mod, "seq").astype(BF16)
    grad_mod = lax.all_gather(grad_mod, "dp", axis=0, tiled=True)
    sums_mod = dot_left_t(cond_mine, grad_mod)
    own = b_mod.shape[0]
    sums_bias_mod = jnp.sum(
        lax.dynamic_slice_in_dim(grad_mod, me * own, own, axis=1).astype(F32), axis=0
    )
    grad_cond_act = lax.all_gather(dot_right_t(grad_mod, w_mod), both, axis=0)
    grad_cond_act = lax.dynamic_slice_in_dim(grad_cond_act, my_dp * count, count, axis=1)
    grad_cond = silu_back(grad_cond_act.transpose(1, 0, 2).reshape(count, width))[0]

    def spread(values, shape):
        blank = jnp.zeros(shape, F32)
        return lax.dynamic_update_slice_in_dim(blank, values, my_seq, 1).reshape(-1)

    joined_sums, out_sums, fc1_sums, fc2_sums = bias_sums
    qv_sums = jnp.stack([joined_sums[:part], joined_sums[2 * part : 3 * part]])
    bias_sums = [
        spread(qv_sums.reshape(2, 1, part), (2, seq, part)),
        out_sums,
        spread(fc1_sums.reshape(dp, 1, units), (dp, seq, units)),
        fc2_sums,
    ]
    joint = jnp.concatenate([item.reshape(dp * seq, -1) for item in bias_sums], axis=1)
    joint = lax.psum_scatter(joint, both, scatter_dimension=0, tiled=True).reshape(-1)
    cuts = [b_qv.shape[0], b_out.shape[0], b_fc1.shape[0]]
    sums_bias_qv, sums_bias_out, sums_bias_fc1, sums_bias_fc2 = jnp.split(
        joint, [cuts[0], cuts[0] + cuts[1], sum(cuts)]
    )
    return (
        output,
        grad_tokens,
        grad_cond.astype(BF16),
        sums_mod,
        sums_bias_mod,
        sums_qkv,
        sums_bias_qv,
        sums_out,
        sums_bias_out,
        sums_fc1,
        sums_bias_fc1,
        sums_fc2,
        sums_bias_fc2,
    )


def solution(mesh):
    both = P(("dp", "seq"))
    wide = P(("dp", "seq"), None)
    tokens = P("dp", "seq", None)
    in_specs = (
        tokens,
        P("dp", None),
        wide,
        both,
        wide,
        both,
        wide,
        both,
        wide,
        both,
        wide,
        both,
        tokens,
    )
    out_specs = (tokens, tokens, P("dp", None)) + (wide, both) * 5
    return jax.shard_map(body, mesh=mesh, in_specs=in_specs, out_specs=out_specs, check_vma=False)
```

time: 887 us -> 338 us (0.38); the launches traced: 874 us -> 336 us
  blocking collectives: 319 us -> 0 us
  Pallas kernels: 0 us -> 312 us
  waiting for transfers between devices: 295 us -> 0 us
  matrix products: 99.2 us -> 0 us
  local copies, waits for them, and re-layouts: 72.9 us -> 21.8 us
  starting transfers between devices: 42.6 us -> 0 us
  other arithmetic: 30 us -> 1.08 us
  between operations: 16 us -> 0.87 us
    pallas_call x0 -> x1, Pallas kernels: none -> 312 us  [run_kernel(): pl.pallas_call(partial(block_kernel, sz), out_shape=outputs, in_specs=[vm...]
    all_gather x7 -> x0, waiting for transfers between devices: 207 us -> none  [the longest x2 69.7 us: to_columns(): return lax.all_gather(mine, 'dp', axis=0, tiled=True)]
    unnamed x3 -> x0, blocking collectives: 175 us -> none
    all_gather x3 -> x0, blocking collectives: 100 us -> none  [the longest x1 38.1 us: body(): grad_cond_act = lax.all_gather(dot_right_t(grad_mod, w_mod), both, axis=0)]
    dot_general x21 -> x0, matrix products: 99.2 us -> none  [the longest x5 29.1 us: dot(): return jnp.dot(left, right, preferred_element_type=F32)]
    reduce_scatter x6 -> x0, waiting for transfers between devices: 43.1 us -> none  [the longest x3 43.1 us: sum_tokens(): lax.psum_scatter(parts, 'seq', scatter_dimension=1, tiled=True).astype(F32)]
    unnamed x23 -> x0, waiting for transfers between devices: 33.5 us -> none
    unnamed x128 -> x35, local copies, waits for them, and re-layouts: 37.7 us -> 4.43 us
  transfers between devices with their start and end apart: 26 -> 0, of which waited for: 14 -> 0; matrix products, arithmetic and copies ran while one was open for 29% -> 0% of each run, Pallas kernels for 0% -> 0%
where the time goes in v2:
time: 338 us; the launch traced here: 336 us
  Pallas kernels  312 us (92%)
  local copies, waits for them, and re-layouts  21.8 us (6%)
    pallas_call x1, Pallas kernels, run_kernel(): pl.pallas_call(partial(block_kernel, sz), out_shape=outputs, in_specs=[vm...  312 us

profile of v2, /device:TPU:4, one launch (start us, length us, event | category | flops | bytes accessed | tf_op | source)
XLA Modules:
  0.0 335.9 jit_solution(5047138951470409998)
XLA Ops:
  0.6 2.0 reshape.70
  2.6 0.1 copy.50
  2.7 0.0 copy-start.4
  2.7 0.7 reshape.71
  3.5 0.8 pad.13.refs_6_
  4.3 0.0 copy-done.4
  4.3 0.2 reshape.68
  4.5 0.0 copy-start.7
  4.5 0.2 copy.51
  4.7 0.0 copy-start.9
  4.7 0.0 copy-start.10
  4.8 0.0 copy-start.11
  4.8 0.0 copy-start.12
  4.8 0.0 copy-start.13
  4.8 0.3 reshape.69
  5.2 0.8 pad.12.refs_5_
  5.9 0.0 copy-done.7
  5.9 0.7 pad.14.refs_7_
  6.6 0.0 copy-done.9
  6.6 0.0 copy-done.10
  6.6 0.0 copy-done.11
  6.6 0.0 copy-done.12
  6.6 0.0 copy-done.13
  6.6 0.1 concatenate.3
  6.7 0.6 reshape.67.refs_3_
  7.3 312.1 %shard_map.228 = (bf16[2,128,1152]{2,1,0:T(8,128)(2,1)}, bf16[2,128,1152]{2,1,0:T(8,128)(2,1)}, bf16[2,1152]{1,0:T(2,128)(2,1)}, f32[40,6912]{1,0:T(8,128)}, f32...) custom-call(bf16[2,128,1152]{2,1,0:T(8,128)(2,1)} %refs_0_.1, ...), custom_call_target="tpu_custom_call" | custom-call | tf_op jit(solution)/shard_map/pallas_call | solution.py:1235
  319.5 1.3 slice_bitcast_fusion
  320.7 1.3 slice.28
  322.0 1.3 slice.34
  323.2 1.2 slice_bitcast_fusion.2
  324.4 1.0 slice_convert_fusion
  325.5 0.2 copy.47
  325.7 0.8 reshape.89
  326.5 0.5 copy.43
  327.0 0.0 copy-start.5
  327.0 2.0 reshape.83
  329.0 0.0 copy-done.5
  329.0 0.1 copy.46
  329.2 0.6 reshape.87
  329.7 0.2 copy.41
  329.9 1.2 reshape.81
  331.1 0.0 copy-done.6
  331.1 0.7 slice.31
  331.8 0.8 copy.57
  332.6 0.8 copy.58
  333.4 0.6 copy.59
  334.0 1.0 copy.60
  335.0 0.8 copy.61
  (14 shorter events, 0.1 us)
Async XLA Ops:
  2.7 1.6 copy-start.4
  4.5 1.4 copy-start.7
  4.7 1.9 copy-start.9
  4.7 1.9 copy-start.10
  4.8 1.8 copy-start.11
  4.8 1.8 copy-start.12
  4.8 1.8 copy-start.13
  327.0 2.0 copy-start.5
  329.7 1.4 copy-start.6
  329.9 1.9 copy-start.3
  329.9 2.7 copy-start.2
  331.8 1.6 copy-start.8
  331.8 2.2 copy-start
  333.4 1.6 copy-start.1

commit v3 on v2

--- a/solution.py
+++ b/solution.py
@@ -125,20 +125,32 @@
     def device_z(step):
         return (z_peer(step) * 2 + x_me, s_me)
 
+    inner = z_me % 3 != 0
+    outer = z_me % 3 == 0
+
+    def z_flip(mask):
+        return (z_me, z_me + 1 - 2 * (z_me % 2), lax.rem(z_me + 2, line), line - 1 - z_me)[mask]
+
+    def device_flip(mask):
+        return (z_flip(mask) * 2 + x_me, s_me)
+
     device_x = (z_me * 2 + (1 - x_me), s_me)
     used = [0, 0]
 
-    def send(src, dst, device):
+    def copy_to(src, dst, device, arrival=None):
         index = used[0]
         used[0] += 1
-        copy = pltpu.make_async_remote_copy(
+        return pltpu.make_async_remote_copy(
             src_ref=src,
             dst_ref=dst,
             send_sem=r.send_sems.at[index],
-            recv_sem=r.recv_sems.at[index],
+            recv_sem=r.recv_sems.at[index] if arrival is None else arrival,
             device_id=device,
             device_id_type=MESH,
         )
+
+    def send(src, dst, device, arrival=None):
+        copy = copy_to(src, dst, device, arrival)
         copy.start()
         return copy
 
@@ -161,7 +173,6 @@
 
     pending = []
     far_moves = []
-    sum_own = r.attended
 
     def release(copy):
         copy.wait_send()
@@ -241,17 +252,33 @@
         def slot(self, dp):
             return rows_of(self.ref, dp * self.chunk, self.chunk)
 
-        def push(self, source=None):
+        def push_along(self, source=None):
             own = self.slot(dp_me)
             mine = own if source is None else source
-            self.along = [send(mine, own, device_z(step)) for step in range(1, line)]
-            self.across = [send(mine, own, device_x)]
-
-        def forward(self):
-            for step, copy in zip(range(1, line), self.along):
-                copy.wait_recv()
-                came = lax.rem(z_me + line - step, line) * 2 + x_me
-                self.across.append(send(self.slot(came), self.slot(came), device_x))
+            self.along = [send(mine, own, device_flip(mask)) for mask in (2, 1)]
+            self.arrival = r.recv_sems.at[used[0]]
+            self.last = copy_to(mine, own, device_flip(3))
+            pl.when(inner)(self.last.start)
+            self.across, self.passed = [], 0
+
+        def push_across(self, source=None):
+            own = self.slot(dp_me)
+            mine = own if source is None else source
+            self.across.append(send(mine, own, device_x))
+
+        def push(self, source=None):
+            self.push_along(source)
+            self.push_across(source)
+
+        def forward(self, limit=3):
+            for mask in (2, 1, 3)[self.passed :][:limit]:
+                (self.along + [self.last])[self.passed].wait_recv()
+                self.passed += 1
+                came = self.slot(z_flip(mask) * 2 + x_me)
+                if mask == 2:
+                    self.relay = copy_to(came, came, device_flip(1), self.arrival)
+                    pl.when(inner)(self.relay.start)
+                self.across.append(send(came, came, device_x))
 
         def finish(self):
             for copy in self.across:
@@ -260,11 +287,17 @@
         def drain(self):
             for copy in self.along + self.across:
                 copy.wait_send()
+
+            @pl.when(inner)
+            def _():
+                self.last.wait_send()
+                self.relay.wait_send()
 
     class SumWeights:
         def __init__(self, ref, chunk, across_ref, along_ref, columns):
             self.ref, self.chunk, self.columns = ref, chunk, columns
             self.across_ref, self.along_ref = across_ref, along_ref
+            self.across = {}
 
         def view(self, ref, index):
             return ref.at[index, :, pl.ds(0, self.columns)]
@@ -272,35 +305,70 @@
         def slot(self, dp):
             return rows_of(self.ref, dp * self.chunk, self.chunk)
 
-        def push(self):
-            self.across = []
-            for step in range(line):
-                z = lax.rem(z_me + step, line)
-                self.across.append(
-                    send(self.slot(z * 2 + 1 - x_me), self.view(self.across_ref, step), device_x)
+        def push(self, masks=(3, 2, 1, 0)):
+            if not self.across:
+                self.across, self.passed = {}, []
+            for mask in masks:
+                self.across[mask] = send(
+                    self.slot(z_flip(mask) * 2 + 1 - x_me),
+                    self.view(self.across_ref, mask),
+                    device_x,
                 )
 
-        def forward(self):
-            self.along = []
-            for step in list(range(1, line)) + [0]:
-                self.across[step].wait_recv()
-                z = lax.rem(z_me + step, line)
-                slot = self.slot(z * 2 + x_me)
-                total = slot[...].astype(F32) + self.view(self.across_ref, step)[...].astype(F32)
-                if step:
-                    slot[...] = total.astype(BF16)
-                    self.along.append(send(slot, self.view(self.along_ref, step), device_z(step)))
+        def forward(self, limit=3):
+            for mask in (3, 2, 1)[len(self.passed) :][:limit]:
+                self.passed.append(mask)
+                self.across[mask].wait_recv()
+                slot = self.slot(z_flip(mask) * 2 + x_me)
+                came = self.view(self.across_ref, mask)
+
+                def total():
+                    return slot[...].astype(F32) + came[...].astype(F32)
+
+                extra = self.view(self.along_ref, 0)
+                if mask == 3:
+                    slot[...] = total().astype(BF16)
+                    self.direct = copy_to(slot, self.view(self.along_ref, 3), device_flip(3))
+                    self.relay = copy_to(slot, extra, device_flip(1))
+                    pl.when(inner)(self.direct.start)
+                    pl.when(outer)(self.relay.start)
+                elif mask == 2:
+
+                    @pl.when(inner)
+                    def _():
+                        self.relay.wait_recv()
+                        slot[...] = (total() + extra[...].astype(F32)).astype(BF16)
+
+                    @pl.when(outer)
+                    def _():
+                        slot[...] = total().astype(BF16)
+
+                    self.two = send(slot, self.view(self.along_ref, 2), device_flip(2))
                 else:
-                    sum_own[pl.ds(0, self.chunk), pl.ds(0, self.columns)] = total
-
-        def finish(self):
-            total = sum_own[pl.ds(0, self.chunk), pl.ds(0, self.columns)]
-            for copy, step in zip(self.along, range(1, line)):
+                    slot[...] = total().astype(BF16)
+                    self.one = send(slot, self.view(self.along_ref, 1), device_flip(1))
+
+        def finish(self, target):
+            self.across[0].wait_recv()
+            total = self.slot(dp_me)[...].astype(F32)
+            total = total + self.view(self.across_ref, 0)[...].astype(F32)
+            for copy, mask in ((self.one, 1), (self.two, 2)):
                 copy.wait_recv()
-                total = total + self.view(self.along_ref, step)[...].astype(F32)
-            for copy in self.along + self.across:
+                total = total + self.view(self.along_ref, mask)[...].astype(F32)
+            target[...] = total
+
+            @pl.when(inner)
+            def _():
+                self.direct.wait_recv()
+                target[...] += self.view(self.along_ref, 3)[...].astype(F32)
+                self.direct.wait_send()
+
+            @pl.when(outer)
+            def _():
+                self.relay.wait_send()
+
+            for copy in [self.one, self.two] + list(self.across.values()):
                 copy.wait_send()
-            return total
 
     pad = sz.padded_rows
     qkv_blocks, fc1_blocks = r.qkv_blocks, r.fc1_blocks
@@ -313,18 +381,14 @@
     rows_of(r.cond_all, dp_me * 16, 16)[...] = low_rows.astype(BF16)
     gather_cond = GatherWeights(r.cond_all, 16)
     gather_cond.push()
-    qkv_moves = exchange(
-        lambda peer: r.qkv_src.at[peer], lambda me: rows_of(qkv_blocks, me * pad, pad)
-    )
+    gather_out = GatherWeights(out_mine, pad)
+    gather_out.push(r.out_src)
     qkv_local = local(r.qkv_src.at[s_me], rows_of(qkv_blocks, s_me * pad, pad))
+    fc1_local = local(r.fc1_src.at[s_me], rows_of(fc1_blocks, s_me * pad, pad))
     lat_local, og_local = [
         [local(source.at[latent], token_rows(target, latent, s_me)) for latent in range(count)]
         for source, target in ((r.latents, r.lat_all), (r.out_grad, r.grad_branch))
     ]
-    lat_moves = [
-        GatherTokens(r.lat_all, latent, r.latents.at[latent]) for latent in range(count)
-    ]
-    fc1_local = local(r.fc1_src.at[s_me], rows_of(fc1_blocks, s_me * pad, pad))
     out_local = local(r.out_src, rows_of(out_mine, dp_me * pad, pad))
     fc2_local = local(r.fc2_src, rows_of(r.fc2, dp_me * sz.units, sz.units))
 
@@ -356,20 +420,35 @@
     bias_mine = rows_of(r.bias_blocks, s_me * 16, 16)
     bias_mine[...] = jnp.concatenate(bias_rows, axis=0).astype(BF16)
     bias_moves = exchange(lambda peer: bias_mine, lambda me: rows_of(r.bias_blocks, me * 16, 16))
+    qkv_moves = exchange(
+        lambda peer: r.qkv_src.at[peer], lambda me: rows_of(qkv_blocks, me * pad, pad)
+    )
+    fc1_moves = exchange(
+        lambda peer: r.fc1_src.at[peer], lambda me: rows_of(fc1_blocks, me * pad, pad)
+    )
+    lat_moves = [GatherTokens(r.lat_all, 0, r.latents.at[0])]
 
     tighten = one_hot(sz.chunk, seq * pad, sz.rows, pad, False)
     loosen = one_hot(sz.chunk, seq * pad, sz.rows, pad, True)
-    gather_out = GatherWeights(out_mine, pad)
     gather_qkv = GatherWeights(r.qkv, sz.chunk)
     gather_fc1 = GatherWeights(r.fc1, sz.chunk)
     gather_fc2 = GatherWeights(r.fc2, sz.units)
+    settle(bias_moves)
+    bias_sum = sum(
+        r.bias_blocks[position * 16 : (position + 1) * 16, :].astype(F32) for position in range(seq)
+    )
+    rows_of(r.bias_all, dp_me * 16, 16)[...] = bias_sum.astype(BF16)
+    gather_bias = GatherWeights(r.bias_all, 16)
+    gather_bias.push()
+    gather_cond.forward()
+    gather_out.forward(1)
     qkv_local.wait()
     settle(qkv_moves)
     rows_of(r.qkv, dp_me * sz.chunk, sz.chunk)[...] = dot(tighten, qkv_blocks[...]).astype(BF16)
-    gather_qkv.push()
-
-    gather_cond.forward()
+    gather_qkv.push_along()
+
     gather_cond.finish()
+    gather_qkv.push_across()
     iota = partial(lax.broadcasted_iota, jnp.int32)
     hit = iota((width, LANES), 0) == iota((width, LANES), 1) + me * sz.rows
     hit = hit & (iota((width, LANES), 1) < sz.rows)
@@ -393,34 +472,34 @@
     mod_core = [
         send(mod_part(y * 2 + 1 - c_me), r.mod_core.at[y], device_seq(1)) for y in range(2)
     ]
-    for move in lat_moves:
-        move.forward()
-    fc1_moves = exchange(
-        lambda peer: r.fc1_src.at[peer], lambda me: rows_of(fc1_blocks, me * pad, pad)
-    )
+    gather_out.forward()
+    fc1_local.wait()
+    settle(fc1_moves)
+    rows_of(r.fc1, dp_me * sz.chunk, sz.chunk)[...] = dot(tighten, fc1_blocks[...]).astype(BF16)
     for copy in mod_core:
         copy.wait_recv()
     r.mod_send[...] = mod_part((1 - y_me) * 2 + c_me)[...] + r.mod_core[1 - y_me]
     mod_chip = send(r.mod_send, r.mod_chip, device_seq(2))
-    settle(bias_moves)
-    bias_sum = sum(
-        r.bias_blocks[position * 16 : (position + 1) * 16, :].astype(F32) for position in range(seq)
-    )
-    rows_of(r.bias_all, dp_me * 16, 16)[...] = bias_sum.astype(BF16)
-    gather_bias = GatherWeights(r.bias_all, 16)
-    gather_bias.push()
+    for latent in range(1, count):
+        lat_moves.append(GatherTokens(r.lat_all, latent, r.latents.at[latent]))
     mod_chip.wait_recv()
     r.mod_sum[...] = mod_part(s_me)[...] + r.mod_core[y_me] + r.mod_chip[...]
     mod_x = send(rows_of(r.mod_sum, (1 - x_me) * 8, 8), r.mod_x, device_x)
-    fc1_local.wait()
-    settle(fc1_moves)
-    rows_of(r.fc1, dp_me * sz.chunk, sz.chunk)[...] = dot(tighten, fc1_blocks[...]).astype(BF16)
+    lat_moves[0].forward()
+    gather_bias.forward(1)
+    gather_qkv.forward(1)
     mod_x.wait_recv()
     r.mod_half[...] = rows_of(r.mod_sum, x_me * 8, 8)[...] + r.mod_x[...]
     mod_z = [send(r.mod_half, r.mod_z.at[step], device_z(step)) for step in range(1, line)]
+    gather_fc1.push_along()
     gather_bias.forward()
+    og_moves = [GatherTokens(r.grad_branch, 0, r.out_grad.at[0])]
+    gather_fc1.push_across()
     gather_qkv.forward()
-    gather_out.push(r.out_src)
+    for move in lat_moves[1:]:
+        move.forward()
+    out_local.wait()
+    gather_out.finish()
     mod_total = r.mod_half[...]
     for copy, step in zip(mod_z, range(1, line)):
         copy.wait_recv()
@@ -434,11 +513,8 @@
     mod_slot = r.mod_all.at[s_me]
     mod_slot[...] = jnp.concatenate(picked, axis=0)
     mod_moves = [send(mod_slot, mod_slot, device_seq(mask)) for mask in (1, 2)]
-    gather_out.forward()
-    gather_fc1.push()
-    og_moves = [
-        GatherTokens(r.grad_branch, latent, r.out_grad.at[latent]) for latent in range(count)
-    ]
+    out_core = send(out_mine, out_mine, device_seq(1))
+    out_chip = send(out_mine, out_mine, device_seq(2))
     mod_moves[1].wait_recv()
     mod_slot = r.mod_all.at[seq_peer(2)]
     mod_moves.append(send(mod_slot, mod_slot, device_seq(1)))
@@ -477,6 +553,9 @@
                 latent : latent + 1, comp * width : (comp + 1) * width
             ]
     pending.extend(mod_core + [mod_chip, mod_x] + mod_z + mod_moves)
+    gather_fc1.forward(1)
+    fc2_local.wait()
+    gather_fc2.push()
 
     for copy in lat_local:
         copy.wait()
@@ -494,11 +573,6 @@
         return carry
 
     lax.fori_loop(0, count * length // ROWS, modulate_tokens, 0)
-
-    out_local.wait()
-    gather_out.finish()
-    out_core = send(out_mine, out_mine, device_seq(1))
-    out_chip = send(out_mine, out_mine, device_seq(2))
 
     gather_qkv.finish()
     tile = 2 * tokens
@@ -522,6 +596,7 @@
         return carry
 
     lax.fori_loop(0, count * per_latent, project, 0)
+    gather_fc1.forward(1)
 
     half = length // 2
 
@@ -564,29 +639,12 @@
             )
         )
         if latent == 0:
+            gather_fc1.forward()
             out_chip.wait_recv()
             other = rows_of(r.out_blocks, seq_peer(2) * out_wide, out_wide)
             out_last = send(other, other, device_seq(1))
-            for move in og_moves:
-                move.forward()
-    gather_fc1.forward()
-    fc2_local.wait()
-    gather_fc2.push()
-
-    for copy in og_local:
-        copy.wait()
-    for move in og_moves:
-        move.finish()
-    for move in lat_moves + og_moves:
-        release(move.last)
-
-    def gate_grads(step, carry):
-        here = pl.ds(pl.multiple_of(step * ROWS, ROWS), ROWS)
-        gate = mod[step // (length // ROWS), 5:6, :]
-        r.grad_branch[here, :] = (r.grad_branch[here, :].astype(F32) * gate).astype(BF16)
-        return carry
-
-    lax.fori_loop(0, count * length // ROWS, gate_grads, 0)
+    og_moves[0].forward()
+    gather_fc2.forward(1)
 
     out_core.wait_recv()
     out_last.wait_recv()
@@ -604,7 +662,6 @@
 
     lax.fori_loop(0, sz.dp, tighten_out, 0)
 
-    gather_fc1.finish()
     m2_moves = []
     for latent in range(count):
         own, moves = mixed_moves[latent]
@@ -631,21 +688,38 @@
         lax.fori_loop(0, tokens // ROWS, second_norm, 0)
         m2_moves.append(GatherTokens(r.modded_two, latent))
 
+    for latent in range(1, count):
+        og_moves.append(GatherTokens(r.grad_branch, latent, r.out_grad.at[latent]))
+    gather_fc2.forward(1)
+    for copy in og_local:
+        copy.wait()
+    for move in lat_moves:
+        release(move.last)
+
+    def gate_grads(step, carry):
+        here = pl.ds(pl.multiple_of(step * ROWS, ROWS), ROWS)
+        gate = mod[step // (length // ROWS), 5:6, :]
+        r.grad_branch[here, :] = (r.grad_branch[here, :].astype(F32) * gate).astype(BF16)
+        return carry
+
+    def gate_latent(latent):
+        og_moves[latent].finish()
+        release(og_moves[latent].last)
+        steps = length // ROWS
+        lax.fori_loop(latent * steps, (latent + 1) * steps, gate_grads, 0)
+
+    gate_latent(0)
+    m2_moves[0].forward()
     gather_fc2.forward()
-    for move in m2_moves:
-        move.forward()
-    gather_fc2.finish()
 
     cuts = column_cuts(sz.hidden, 256)
-    r.fc1_sums[...] = jnp.zeros_like(r.fc1_sums)
-    grad_moves = []
+    gather_fc1.finish()
     for latent in range(count):
         m2_moves[latent].finish()
 
         def mlp(step, carry, latent=latent):
             start = pl.multiple_of(latent * length + step * tile, tile)
             rows = r.modded_two[pl.ds(start, tile), :]
-            incoming = r.grad_branch[pl.ds(start, tile), :]
             for column, size in cuts:
                 here = slice(column, column + size)
                 hidden = dot(rows, r.fc1[:, here]) + r.bias_fc1[:, here]
@@ -656,12 +730,54 @@
                 slope = 0.5 * (1.0 + bent) + 0.5 * hidden * (1.0 - bent * bent) * (
                     0.7978845608028654 * (1.0 + 3 * 0.044715 * square)
                 )
+                r.part_a[pl.ds(start, tile), here] = slope.astype(BF16)
+            return carry
+
+        lax.fori_loop(0, per_latent, mlp, 0)
+        if latent + 1 < count:
+            m2_moves[latent + 1].forward()
+
+    for copy in (out_core, out_chip, out_last):
+        release(copy)
+    gather_out.drain()
+
+    def weight_grad(left, right, target):
+        size = 384 if width % 384 == 0 else LANES
+
+        def tiles(step, carry):
+            start = pl.multiple_of(step * size, LANES)
+            sums = dot_left_t(left[:, pl.ds(start, size)], right[...])
+            target[pl.ds(start, size), :] = sums.astype(BF16)
+            return carry
+
+        lax.fori_loop(0, left.shape[1] // size, tiles, 0)
+
+    for latent in range(1, count):
+        og_moves[latent].forward()
+        gate_latent(latent)
+    weight_grad(r.lat_all, r.grad_branch, r.out_blocks)
+    sum_fc2 = SumWeights(r.out_blocks, sz.units, r.across_b, r.along_b, width)
+    sum_fc2.push()
+
+    gather_fc2.finish()
+    r.fc1_sums[...] = jnp.zeros_like(r.fc1_sums)
+    grad_moves = []
+    for latent in range(count):
+
+        def mlp_back(step, carry, latent=latent):
+            start = pl.multiple_of(latent * length + step * tile, tile)
+            incoming = r.grad_branch[pl.ds(start, tile), :]
+            for column, size in cuts:
+                here = slice(column, column + size)
+                slope = r.part_a[pl.ds(start, tile), here].astype(F32)
                 grads = (dot_right_t(incoming, r.fc2[here, :]) * slope).astype(BF16)
                 r.grad_hidden[pl.ds(start, tile), here] = grads
                 r.fc1_sums[:, here] += jnp.sum(grads.astype(F32), axis=0, keepdims=True)
             return carry
 
-        lax.fori_loop(0, per_latent, mlp, 0)
+        lax.fori_loop(0, per_latent, mlp_back, 0)
+        if latent:
+            grad_moves[latent - 1].forward()
 
         def back_fc1(step, carry, latent=latent):
             start = pl.multiple_of(latent * length + step * tile, tile)
@@ -675,36 +791,14 @@
         lax.fori_loop(0, per_latent, back_fc1, 0)
         grad_moves.append(SumTokens(r.part_a, 0, latent))
 
-    for copy in (out_core, out_chip, out_last):
-        release(copy)
-    gather_out.drain()
-    for latent in range(count):
-
-        def branch_out(step, carry, latent=latent):
-            start = pl.multiple_of(latent * length + step * tile, tile)
-            sums = dot(r.lat_all[pl.ds(start, tile), :], r.fc2[...])
-            r.out_blocks[pl.ds(start, tile), :] = sums.astype(BF16)
-            return carry
-
-        lax.fori_loop(0, per_latent, branch_out, 0)
-        grad_moves[latent].forward()
-
-    gather_fc2.drain()
-
-    def weight_grad(left, right, target):
-        size = 384 if width % 384 == 0 else LANES
-
-        def tiles(step, carry):
-            start = pl.multiple_of(step * size, LANES)
-            sums = dot_left_t(left[:, pl.ds(start, size)], right[...])
-            target[pl.ds(start, size), :] = sums.astype(BF16)
-            return carry
-
-        lax.fori_loop(0, left.shape[1] // size, tiles, 0)
-
-    weight_grad(r.lat_all, r.grad_branch, r.fc2)
-    sum_fc2 = SumWeights(r.fc2, sz.units, r.across_b, r.along_b, width)
-    sum_fc2.push()
+    for move in m2_moves:
+        for copy in (move.core, move.chip, move.last):
+            release(copy)
+    gather_fc1.drain()
+    grad_moves[-1].forward()
+    weight_grad(r.modded_two, r.grad_hidden, r.fc1)
+    sum_fc1 = SumWeights(r.fc1, sz.chunk, r.across_a, r.along_a, sz.hidden)
+    sum_fc1.push()
 
     grad_mod = r.grad_mod
     grad_mod[...] = jnp.zeros_like(grad_mod)
@@ -735,6 +829,7 @@
             return carry
 
         lax.fori_loop(0, tokens // ROWS, second_back, 0)
+        sum_fc2.forward(1)
         here = pl.ds(latent * tokens, tokens)
         grad_mixed = dot_right_t(r.grad_attended[here, :], r.out[...])
         for copy in mixed_moves[latent][1]:
@@ -753,13 +848,20 @@
             )
         )
 
-    branch_moves = [SumTokens(r.out_blocks, 1, latent) for latent in range(count)]
-
-    gather_fc1.drain()
-    weight_grad(r.modded_two, r.grad_hidden, r.fc1)
-    sum_fc1 = SumWeights(r.fc1, sz.chunk, r.across_a, r.along_a, sz.hidden)
+    gather_fc2.drain()
+    branch_moves = []
+    for latent in range(count):
+
+        def branch_out(step, carry, latent=latent):
+            start = pl.multiple_of(latent * length + step * tile, tile)
+            sums = dot(r.lat_all[pl.ds(start, tile), :], r.fc2[...])
+            r.lat_all[pl.ds(start, tile), :] = sums.astype(BF16)
+            return carry
+
+        lax.fori_loop(0, per_latent, branch_out, 0)
+        branch_moves.append(SumTokens(r.lat_all, 1, latent))
     sum_fc2.forward()
-    sum_fc1.push()
+
     for move in branch_moves:
         move.forward()
 
@@ -781,6 +883,7 @@
         r.k_heads[index] = (dot_left_t(r.soft[index], queries) * ROOT).astype(BF16)
         return carry
 
+    fc_rows = rows_of(r.attended, 0, sz.units)
     joined_sums = r.joined_sums
     grad_joined = r.grad_hidden.at[:, pl.ds(0, sz.joined)]
     joined_sums[...] = jnp.zeros_like(joined_sums)
@@ -799,7 +902,21 @@
             return carry
 
         lax.fori_loop(0, seq, unpack, 0)
-        lax.fori_loop(latent * heads, (latent + 1) * heads, attend_back, 0)
+        middle_head = latent * heads + heads // 2
+        lax.fori_loop(latent * heads, middle_head, attend_back, 0)
+        if latent == 0:
+            sum_fc2.finish(fc_rows)
+            fc2_move = local(fc_rows, r.fc2_out)
+            pl.semaphore_signal(r.free_x, inc=1, device_id=device_x, device_id_type=MESH)
+            for step in range(1, line):
+                pl.semaphore_signal(
+                    r.free_z, inc=1, device_id=device_z(step), device_id_type=MESH
+                )
+        else:
+            token_moves[latent - 1].forward()
+            sum_fc1.forward(1)
+        lax.fori_loop(middle_head, (latent + 1) * heads, attend_back, 0)
+        sum_fc1.forward(1)
 
         def join(block, carry, latent=latent):
             row = pl.multiple_of(block * tokens, tokens)
@@ -829,23 +946,46 @@
 
         lax.fori_loop(0, per_latent, back_qkv, 0)
         token_moves.append(SumTokens(r.part_a, 0, latent))
-        if latent == 0:
-            fc2_rows = rows_of(sum_own, 0, sz.units)
-            fc2_rows[...] = sum_fc2.finish()
-            local(fc2_rows, r.fc2_out).wait()
-            sum_fc1.forward()
-
+
+    token_moves[-1].forward()
     gather_qkv.drain()
     weight_grad(r.modded, grad_joined, r.qkv)
-    for move in token_moves:
-        move.forward()
-
     sum_qkv = SumWeights(r.qkv, sz.chunk, r.across_b, r.along_b, sz.joined)
-    sum_qkv.push()
-
-    for move in m2_moves:
-        for copy in (move.core, move.chip, move.last):
-            release(copy)
+    pl.semaphore_wait(r.free_x, 1)
+    sum_qkv.push((3,))
+    sum_fc1.forward()
+
+
+    weight_grad(r.mixed, r.grad_attended, r.out)
+
+    def loosen_out(step, carry):
+        start = pl.multiple_of(step * sz.chunk, 16)
+        spread = dot(loosen, r.out[pl.ds(start, sz.chunk), :]).astype(BF16)
+        for block in range(seq):
+            place = pl.multiple_of(block * out_wide + step * pad, 16)
+            r.out_blocks[pl.ds(place, pad), :] = spread[block * pad : (block + 1) * pad, :]
+        return carry
+
+    lax.fori_loop(0, sz.dp, loosen_out, 0)
+    out_first = [
+        send(
+            rows_of(r.out_blocks, (y * 2 + 1 - c_me) * out_wide, out_wide),
+            rows_of(r.grad_branch, y * out_wide, out_wide),
+            device_seq(1),
+        )
+        for y in range(2)
+    ]
+
+    def out_from_core(y):
+        return rows_of(r.grad_branch, y * out_wide, out_wide)[...].astype(F32)
+
+    other = rows_of(r.out_blocks, ((1 - y_me) * 2 + c_me) * out_wide, out_wide)
+    out_chip_sum = rows_of(r.modded_two, 2 * count * tokens, out_wide)
+
+    def out_half(index):
+        start, size = index * (out_wide // 2), out_wide // 2
+        return send(rows_of(other, start, size), rows_of(out_chip_sum, start, size), device_seq(2))
+
     for latent in range(count):
         branch_moves[latent].finish()
 
@@ -863,6 +1003,10 @@
         lax.fori_loop(0, tokens // ROWS, final_output, 0)
         slot = rows_of(r.modded_two, latent * tokens, tokens)
         far_moves.append(local(slot, r.output.at[latent]))
+    for copy in out_first:
+        copy.wait_recv()
+    other[...] = (other[...].astype(F32) + out_from_core(1 - y_me)).astype(BF16)
+    out_second = [out_half(0)]
     for latent in range(count):
         token_moves[latent].finish()
 
@@ -884,26 +1028,6 @@
         slot = rows_of(r.modded_two, (count + latent) * tokens, tokens)
         far_moves.append(local(slot, r.latents_grad.at[latent]))
 
-    weight_grad(r.mixed, r.grad_attended, r.out)
-
-    def loosen_out(step, carry):
-        start = pl.multiple_of(step * sz.chunk, 16)
-        spread = dot(loosen, r.out[pl.ds(start, sz.chunk), :]).astype(BF16)
-        for block in range(seq):
-            place = pl.multiple_of(block * out_wide + step * pad, 16)
-            r.out_blocks[pl.ds(place, pad), :] = spread[block * pad : (block + 1) * pad, :]
-        return carry
-
-    lax.fori_loop(0, sz.dp, loosen_out, 0)
-    out_first = [
-        send(
-            rows_of(r.out_blocks, (y * 2 + 1 - c_me) * out_wide, out_wide),
-            rows_of(r.lat_all, y * out_wide, out_wide),
-            device_seq(1),
-        )
-        for y in range(2)
-    ]
-
     def return_rows(total, send_ref, recv_ref):
         send_ref[...] = dot(loosen, total.astype(BF16)).astype(BF16)
         mine = rows_of(send_ref, s_me * pad, pad)
@@ -929,49 +1053,36 @@
     for position in range(seq):
         r.bias_sums[4 + position : 5 + position, :] = when(s_me == position, r.fc1_sums[...])
     bias_x = send(r.bias_sums, r.bias_x, device_x)
+    sum_qkv.push((2,))
     mod_core.wait_recv()
     r.grad_chip_send[...] = r.grad_core_send[...] + r.grad_core[...]
     mod_chip = send(r.grad_chip_send, r.grad_chip, device_seq(2))
+    out_second.append(out_half(1))
+    for copy in fc1_moves:
+        release(copy)
+    fc2_move.wait()
+    sum_fc1.finish(fc_rows)
+    fc1_own, fc1_back = return_rows(fc_rows[...], r.fc1_blocks, r.fc1_rows)
     bias_x.wait_recv()
     r.bias_half[...] = r.bias_sums[...] + r.bias_x[...]
-    bias_z = [send(r.bias_half, r.bias_z.at[step], device_z(step)) for step in range(1, line)]
     mod_chip.wait_recv()
     rows_of(r.grad_all, dp_me * 16, 16)[...] = (r.grad_chip_send[...] + r.grad_chip[...]).astype(
         BF16
     )
     gather_grad = GatherWeights(r.grad_all, 16)
     gather_grad.push()
+    bias_z = [send(r.bias_half, r.bias_z.at[step], device_z(step)) for step in range(1, line)]
+    pl.semaphore_wait(r.free_z, line - 1)
+    sum_qkv.forward(1)
+    gather_grad.forward()
+    sum_qkv.push((1,))
     pending.extend([mod_core, bias_x, mod_chip] + bias_z)
-
-    for copy in out_first:
-        copy.wait_recv()
-
-    def out_from_core(y):
-        return rows_of(r.lat_all, y * out_wide, out_wide)[...].astype(F32)
-
-    other = rows_of(r.out_blocks, ((1 - y_me) * 2 + c_me) * out_wide, out_wide)
-    other[...] = (other[...].astype(F32) + out_from_core(1 - y_me)).astype(BF16)
-    out_chip_sum = rows_of(r.grad_branch, 0, out_wide)
-    out_second = send(other, out_chip_sum, device_seq(2))
-
-    for copy in fc1_moves:
-        release(copy)
-    fc1_own, fc1_back = return_rows(sum_fc1.finish(), r.fc1_blocks, r.fc1_rows)
-    sum_qkv.forward()
-    gather_grad.forward()
     bias_total = r.bias_half[...]
     for copy, step in zip(bias_z, range(1, line)):
         copy.wait_recv()
         bias_total = bias_total + r.bias_z[step]
     r.bias_line[...] = bias_total
     bias_core = send(r.bias_line, r.bias_core, device_seq(1))
-
-    out_second.wait_recv()
-    mine = out_mine[...].astype(F32) + out_from_core(y_me)
-    out_mine[...] = (mine + out_chip_sum[...].astype(F32)).astype(BF16)
-    pending.extend(out_first + [out_second])
-    sum_out = SumWeights(out_mine, pad, r.across_out, r.along_out, width)
-    sum_out.push()
 
     gather_grad.finish()
     all_grads = r.grad_all[...]
@@ -984,12 +1095,7 @@
     cond_grads = jnp.zeros((rows, sz.rows), F32)
     mod_rows = r.mod_out.shape[0]
     for comp in range(6):
-        here = slice(comp * width, (comp + 1) * width)
-        chosen = jnp.where(comp_of == comp, cond_spread, 0.0).astype(BF16)
-        place_rows = rows_of(r.grad_middle, comp * mod_rows, mod_rows)
-        place_rows[...] = dot_left_t(chosen, all_grads)[:mod_rows, :]
-        far_moves.append(local(place_rows, r.mod_out.at[:, pl.ds(comp * width, width)]))
-        back = dot_right_t(all_grads, r.w_mod[:, here])
+        back = dot_right_t(all_grads, r.w_mod[:, comp * width : (comp + 1) * width])
         cond_grads = cond_grads + jnp.where(comp_of[:, : sz.rows] == comp, back, 0.0)
     cond_grads = jnp.sum(cond_grads.reshape(rows // 8, 8, sz.rows), axis=1)
     blank = jnp.zeros((16, width - sz.rows), F32)
@@ -1018,6 +1124,7 @@
     r.cond_sides[0] = hits[0]
     r.cond_sides[1] = hits[1]
     cond_x = send(r.cond_sides.at[1 - x_me], r.cond_x, device_x)
+    sum_qkv.push((0,))
     bias_core.wait_recv()
     r.bias_pair[...] = r.bias_line[...] + r.bias_core[...]
     bias_chip = send(r.bias_pair, r.bias_chip, device_seq(2))
@@ -1026,6 +1133,30 @@
     cond_x.wait_recv()
     r.cond_half[...] = r.cond_sides[x_me] + r.cond_x[...]
     cond_z = [send(r.cond_half, r.cond_z.at[step], device_z(step)) for step in range(1, line)]
+    sum_qkv.forward(1)
+    for copy in out_second:
+        copy.wait_recv()
+    mine = out_mine[...].astype(F32) + out_from_core(y_me)
+    out_mine[...] = (mine + out_chip_sum[...].astype(F32)).astype(BF16)
+    pending.extend(out_first + out_second)
+    sum_out = SumWeights(out_mine, pad, r.across_out, r.along_out, width)
+    sum_out.push()
+    cond_total = r.cond_half[...]
+    for copy, step in zip(cond_z, range(1, line)):
+        copy.wait_recv()
+        cond_total = cond_total + r.cond_z[step]
+    r.cond_line[...] = cond_total
+    cond_core = send(r.cond_line, r.cond_core, device_seq(1))
+    sum_qkv.forward()
+    cond_core.wait_recv()
+    r.cond_pair[...] = r.cond_line[...] + r.cond_core[...]
+    cond_chip = send(r.cond_pair, r.cond_chip, device_seq(2))
+    for comp in range(6):
+        chosen = jnp.where(comp_of == comp, cond_spread, 0.0).astype(BF16)
+        place_rows = rows_of(r.grad_middle, comp * mod_rows, mod_rows)
+        place_rows[...] = dot_left_t(chosen, all_grads)[:mod_rows, :]
+        far_moves.append(local(place_rows, r.mod_out.at[:, pl.ds(comp * width, width)]))
+    sum_out.forward(1)
     bias_chip.wait_recv()
     bias_full = r.bias_pair[...] + r.bias_chip[...]
 
@@ -1058,18 +1189,11 @@
     )
     for copy in qkv_moves:
         release(copy)
-    qkv_own, qkv_back = return_rows(sum_qkv.finish(), r.qkv_blocks, r.qkv_rows)
+    qkv_total = fc_rows.at[:, pl.ds(0, sz.joined)]
+    sum_qkv.finish(qkv_total)
+    qkv_own, qkv_back = return_rows(qkv_total[...], r.qkv_blocks, r.qkv_rows)
     sum_out.forward()
-    cond_total = r.cond_half[...]
-    for copy, step in zip(cond_z, range(1, line)):
-        copy.wait_recv()
-        cond_total = cond_total + r.cond_z[step]
-    r.cond_line[...] = cond_total
-    cond_core = send(r.cond_line, r.cond_core, device_seq(1))
-    r.out_out[...] = sum_out.finish()
-    cond_core.wait_recv()
-    r.cond_pair[...] = r.cond_line[...] + r.cond_core[...]
-    cond_chip = send(r.cond_pair, r.cond_chip, device_seq(2))
+    sum_out.finish(r.out_out)
     gather_grad.drain()
     gather_bias.drain()
     gather_cond.drain()
@@ -1207,6 +1331,8 @@
         cond_chip=full(8, width),
         send_sems=pltpu.SemaphoreType.DMA((200,)),
         recv_sems=pltpu.SemaphoreType.DMA((200,)),
+        free_x=pltpu.SemaphoreType.REGULAR,
+        free_z=pltpu.SemaphoreType.REGULAR,
         local_sems=pltpu.SemaphoreType.DMA((40,)),
     )
 

time: 338 us -> 265 us (0.78)
  Pallas kernels: 312 us -> 239 us
    pallas_call x1, Pallas kernels: 312 us -> 239 us  [run_kernel(): pl.pallas_call(partial(block_kernel, sz), out_shape=outputs, in_specs=[vm...]
where the time goes in v3:
time: 265 us; the launch traced here: 263 us
  Pallas kernels  239 us (90%)
  local copies, waits for them, and re-layouts  21.8 us (8%)
    pallas_call x1, Pallas kernels, run_kernel(): pl.pallas_call(partial(block_kernel, sz), out_shape=outputs, in_specs=[vm...  239 us

profile of v3, /device:TPU:4, one launch (start us, length us, event | category | flops | bytes accessed | tf_op | source)
XLA Modules:
  0.0 262.7 jit_solution(13103664270655146761)
XLA Ops:
  0.6 2.0 reshape.70
  2.6 0.1 copy.50
  2.7 0.0 copy-start.4
  2.7 0.7 reshape.71
  3.5 0.8 pad.13.refs_6_
  4.3 0.0 copy-done.4
  4.3 0.2 reshape.68
  4.5 0.0 copy-start.7
  4.5 0.2 copy.51
  4.7 0.0 copy-start.9
  4.7 0.0 copy-start.10
  4.8 0.0 copy-start.11
  4.8 0.0 copy-start.12
  4.8 0.0 copy-start.13
  4.8 0.3 reshape.69
  5.2 0.8 pad.12.refs_5_
  5.9 0.0 copy-done.7
  5.9 0.7 pad.14.refs_7_
  6.6 0.0 copy-done.9
  6.6 0.0 copy-done.10
  6.6 0.0 copy-done.11
  6.6 0.0 copy-done.12
  6.6 0.1 concatenate.3
  6.7 0.6 reshape.67.refs_3_
  7.3 238.7 %shard_map.228 = (bf16[2,128,1152]{2,1,0:T(8,128)(2,1)}, bf16[2,128,1152]{2,1,0:T(8,128)(2,1)}, bf16[2,1152]{1,0:T(2,128)(2,1)}, f32[40,6912]{1,0:T(8,128)}, f32...) custom-call(bf16[2,128,1152]{2,1,0:T(8,128)(2,1)} %refs_0_.1, ...), custom_call_target="tpu_custom_call" | custom-call | tf_op jit(solution)/shard_map/pallas_call | solution.py:1361
  246.1 1.3 slice_bitcast_fusion
  247.3 1.3 slice.28
  248.6 1.3 slice.34
  249.9 1.2 slice_bitcast_fusion.2
  251.0 1.0 slice_convert_fusion
  252.1 0.2 copy.47
  252.3 0.8 reshape.89
  253.1 0.5 copy.43
  253.6 2.0 reshape.83
  255.6 0.0 copy-done.5
  255.6 0.1 copy.46
  255.8 0.6 reshape.87
  256.3 0.2 copy.41
  256.5 0.0 copy-start.3
  256.5 0.0 copy-start.2
  256.5 1.2 reshape.81
  257.7 0.7 slice.31
  258.4 0.8 copy.57
  259.2 0.8 copy.58
  260.0 0.6 copy.59
  260.6 0.0 copy-done
  260.6 1.0 copy.60
  261.6 0.8 copy.61
  (14 shorter events, 0.1 us)
Async XLA Ops:
  2.7 1.6 copy-start.4
  4.5 1.4 copy-start.7
  4.7 1.9 copy-start.9
  4.7 1.9 copy-start.10
  4.8 1.8 copy-start.11
  4.8 1.8 copy-start.12
  4.8 1.8 copy-start.13
  253.6 2.0 copy-start.5
  256.3 1.4 copy-start.6
  256.5 1.9 copy-start.3
  256.5 2.7 %copy-start.2 = (bf16[2,128,1152]{2,1,0:T(8,128)(2,1)S(1)}, bf16[2,128,1152]{2,1,0:T(8,128)(2,1)}, u32[]{:S(2)}) copy-start(bf16[2,128,1152]{2,1,0:T(8,128)(2,1)} %get-tuple-element.47) | copy-start | bytes 1769476
  258.4 1.6 copy-start.8
  258.4 2.2 copy-start
  260.0 1.6 copy-start.1

commit v4 on v3

--- a/solution.py
+++ b/solution.py
@@ -164,6 +164,15 @@
     def rows_of(ref, start, size):
         return ref.at[pl.ds(start, size)]
 
+    raw_moves = [
+        local(source, target)
+        for source, target in (
+            (r.qkv_src, r.qkv_raw),
+            (r.fc1_src, r.fc1_raw),
+            (r.out_src, r.out_raw),
+        )
+    ]
+
     peers = [device_seq(mask) for mask in (1, 2, 3)]
     peers += [device_z(step) for step in range(1, line)] + [device_x]
     barrier = pltpu.get_barrier_semaphore()
@@ -381,15 +390,36 @@
     rows_of(r.cond_all, dp_me * 16, 16)[...] = low_rows.astype(BF16)
     gather_cond = GatherWeights(r.cond_all, 16)
     gather_cond.push()
+    for move in raw_moves:
+        move.wait()
+    own_out = jnp.concatenate(
+        [r.out_raw[...].astype(F32), jnp.zeros((pad - sz.rows, width), F32)], axis=0
+    )
+    rows_of(out_mine, dp_me * pad, pad)[...] = own_out.astype(BF16)
     gather_out = GatherWeights(out_mine, pad)
-    gather_out.push(r.out_src)
-    qkv_local = local(r.qkv_src.at[s_me], rows_of(qkv_blocks, s_me * pad, pad))
-    fc1_local = local(r.fc1_src.at[s_me], rows_of(fc1_blocks, s_me * pad, pad))
+    gather_out.push()
+    qkv_send, fc1_send = r.qkv_rows, r.fc1_rows
+    qkv_send[...] = jnp.zeros_like(qkv_send)
+    fc1_send[...] = jnp.zeros_like(fc1_send)
+    for position in range(seq):
+        here = slice(position * pad, position * pad + sz.rows)
+        pieces = [
+            r.qkv_raw[:, kind * width + position * sz.part :][:, : sz.part] for kind in range(3)
+        ]
+        qkv_send[here, : 3 * sz.part] = jnp.concatenate(pieces, axis=1)
+        pieces = [
+            r.fc1_raw[:, (group * seq + position) * sz.units :][:, : sz.units]
+            for group in range(sz.dp)
+        ]
+        fc1_send[here, :] = jnp.concatenate(pieces, axis=1)
+    qkv_local, fc1_local = [
+        local(rows_of(source, s_me * pad, pad), rows_of(target, s_me * pad, pad))
+        for source, target in ((qkv_send, qkv_blocks), (fc1_send, fc1_blocks))
+    ]
     lat_local, og_local = [
         [local(source.at[latent], token_rows(target, latent, s_me)) for latent in range(count)]
         for source, target in ((r.latents, r.lat_all), (r.out_grad, r.grad_branch))
     ]
-    out_local = local(r.out_src, rows_of(out_mine, dp_me * pad, pad))
     fc2_local = local(r.fc2_src, rows_of(r.fc2, dp_me * sz.units, sz.units))
 
     def place(values, start, size):
@@ -421,10 +451,12 @@
     bias_mine[...] = jnp.concatenate(bias_rows, axis=0).astype(BF16)
     bias_moves = exchange(lambda peer: bias_mine, lambda me: rows_of(r.bias_blocks, me * 16, 16))
     qkv_moves = exchange(
-        lambda peer: r.qkv_src.at[peer], lambda me: rows_of(qkv_blocks, me * pad, pad)
+        lambda peer: rows_of(qkv_send, peer * pad, pad),
+        lambda me: rows_of(qkv_blocks, me * pad, pad),
     )
     fc1_moves = exchange(
-        lambda peer: r.fc1_src.at[peer], lambda me: rows_of(fc1_blocks, me * pad, pad)
+        lambda peer: rows_of(fc1_send, peer * pad, pad),
+        lambda me: rows_of(fc1_blocks, me * pad, pad),
     )
     lat_moves = [GatherTokens(r.lat_all, 0, r.latents.at[0])]
 
@@ -498,7 +530,6 @@
     gather_qkv.forward()
     for move in lat_moves[1:]:
         move.forward()
-    out_local.wait()
     gather_out.finish()
     mod_total = r.mod_half[...]
     for copy, step in zip(mod_z, range(1, line)):
@@ -554,6 +585,10 @@
             ]
     pending.extend(mod_core + [mod_chip, mod_x] + mod_z + mod_moves)
     gather_fc1.forward(1)
+    for copy in qkv_moves + fc1_moves:
+        release(copy)
+    gather_bias.drain()
+    gather_cond.drain()
     fc2_local.wait()
     gather_fc2.push()
 
@@ -904,15 +939,7 @@
         lax.fori_loop(0, seq, unpack, 0)
         middle_head = latent * heads + heads // 2
         lax.fori_loop(latent * heads, middle_head, attend_back, 0)
-        if latent == 0:
-            sum_fc2.finish(fc_rows)
-            fc2_move = local(fc_rows, r.fc2_out)
-            pl.semaphore_signal(r.free_x, inc=1, device_id=device_x, device_id_type=MESH)
-            for step in range(1, line):
-                pl.semaphore_signal(
-                    r.free_z, inc=1, device_id=device_z(step), device_id_type=MESH
-                )
-        else:
+        if latent:
             token_moves[latent - 1].forward()
             sum_fc1.forward(1)
         lax.fori_loop(middle_head, (latent + 1) * heads, attend_back, 0)
@@ -948,11 +975,18 @@
         token_moves.append(SumTokens(r.part_a, 0, latent))
 
     token_moves[-1].forward()
+    sum_fc2.finish(fc_rows)
+    fc2_move = local(fc_rows, r.fc2_out)
+    pl.semaphore_signal(r.free_x, inc=1, device_id=device_x, device_id_type=MESH)
+    for step in range(1, line):
+        pl.semaphore_signal(
+            r.free_z, inc=1, device_id=device_z(step), device_id_type=MESH
+        )
     gather_qkv.drain()
     weight_grad(r.modded, grad_joined, r.qkv)
     sum_qkv = SumWeights(r.qkv, sz.chunk, r.across_b, r.along_b, sz.joined)
     pl.semaphore_wait(r.free_x, 1)
-    sum_qkv.push((3,))
+    sum_qkv.push()
     sum_fc1.forward()
 
 
@@ -1007,6 +1041,8 @@
         copy.wait_recv()
     other[...] = (other[...].astype(F32) + out_from_core(1 - y_me)).astype(BF16)
     out_second = [out_half(0)]
+    pl.semaphore_wait(r.free_z, line - 1)
+    sum_qkv.forward(1)
     for latent in range(count):
         token_moves[latent].finish()
 
@@ -1053,39 +1089,35 @@
     for position in range(seq):
         r.bias_sums[4 + position : 5 + position, :] = when(s_me == position, r.fc1_sums[...])
     bias_x = send(r.bias_sums, r.bias_x, device_x)
-    sum_qkv.push((2,))
     mod_core.wait_recv()
     r.grad_chip_send[...] = r.grad_core_send[...] + r.grad_core[...]
     mod_chip = send(r.grad_chip_send, r.grad_chip, device_seq(2))
     out_second.append(out_half(1))
-    for copy in fc1_moves:
-        release(copy)
     fc2_move.wait()
     sum_fc1.finish(fc_rows)
     fc1_own, fc1_back = return_rows(fc_rows[...], r.fc1_blocks, r.fc1_rows)
     bias_x.wait_recv()
     r.bias_half[...] = r.bias_sums[...] + r.bias_x[...]
     mod_chip.wait_recv()
-    rows_of(r.grad_all, dp_me * 16, 16)[...] = (r.grad_chip_send[...] + r.grad_chip[...]).astype(
+    rows_of(r.bias_all, dp_me * 16, 16)[...] = (r.grad_chip_send[...] + r.grad_chip[...]).astype(
         BF16
     )
-    gather_grad = GatherWeights(r.grad_all, 16)
+    gather_grad = GatherWeights(r.bias_all, 16)
     gather_grad.push()
-    bias_z = [send(r.bias_half, r.bias_z.at[step], device_z(step)) for step in range(1, line)]
-    pl.semaphore_wait(r.free_z, line - 1)
+    room_z = r.mod_z.at[:, :, pl.ds(0, width)]
+    bias_z = [send(r.bias_half, room_z.at[step], device_z(step)) for step in range(1, line)]
+    gather_grad.forward()
     sum_qkv.forward(1)
-    gather_grad.forward()
-    sum_qkv.push((1,))
     pending.extend([mod_core, bias_x, mod_chip] + bias_z)
     bias_total = r.bias_half[...]
     for copy, step in zip(bias_z, range(1, line)):
         copy.wait_recv()
-        bias_total = bias_total + r.bias_z[step]
+        bias_total = bias_total + room_z[step]
     r.bias_line[...] = bias_total
     bias_core = send(r.bias_line, r.bias_core, device_seq(1))
 
     gather_grad.finish()
-    all_grads = r.grad_all[...]
+    all_grads = r.bias_all[...]
     rows = sz.dp * 16
     comp_of = iota((rows, rows), 0) & 7
     source = (iota((rows, rows), 0) & ~15) + ((iota((rows, rows), 0) >> 3) & 1)
@@ -1124,7 +1156,6 @@
     r.cond_sides[0] = hits[0]
     r.cond_sides[1] = hits[1]
     cond_x = send(r.cond_sides.at[1 - x_me], r.cond_x, device_x)
-    sum_qkv.push((0,))
     bias_core.wait_recv()
     r.bias_pair[...] = r.bias_line[...] + r.bias_core[...]
     bias_chip = send(r.bias_pair, r.bias_chip, device_seq(2))
@@ -1187,16 +1218,14 @@
         ],
         axis=0,
     )
-    for copy in qkv_moves:
-        release(copy)
     qkv_total = fc_rows.at[:, pl.ds(0, sz.joined)]
     sum_qkv.finish(qkv_total)
     qkv_own, qkv_back = return_rows(qkv_total[...], r.qkv_blocks, r.qkv_rows)
     sum_out.forward()
-    sum_out.finish(r.out_out)
+    out_rows = rows_of(r.middle, 0, pad)
+    sum_out.finish(out_rows)
+    far_moves.append(local(out_rows, r.out_out))
     gather_grad.drain()
-    gather_bias.drain()
-    gather_cond.drain()
     cond_chip.wait_recv()
     cond_full = r.cond_pair[...] + r.cond_chip[...]
     picked = [
@@ -1272,6 +1301,9 @@
         sum_core=low(2, 2, count, tokens, width),
         sum_send=low(2, count, tokens, width),
         sum_chip=low(2, count, tokens, width),
+        qkv_raw=low(sz.rows, 3 * width),
+        fc1_raw=low(sz.rows, seq * sz.hidden),
+        out_raw=low(sz.rows, width),
         qkv_blocks=low(seq * pad, sz.joined),
         fc1_blocks=low(seq * pad, sz.hidden),
         qkv_rows=low(seq * pad, sz.joined),
@@ -1312,11 +1344,9 @@
         grad_core=full(16, width),
         grad_chip_send=full(16, width),
         grad_chip=full(16, width),
-        grad_all=low(sz.dp * 16, width),
         bias_sums=full(8, width),
         bias_x=full(8, width),
         bias_half=full(8, width),
-        bias_z=full(sz.line, 8, width),
         bias_line=full(8, width),
         bias_core=full(8, width),
         bias_pair=full(8, width),
@@ -1362,7 +1392,7 @@
         partial(block_kernel, sz),
         out_shape=outputs,
         in_specs=[vmem] * 5 + [far] * 4,
-        out_specs=[far, far, vmem, far, vmem, far, vmem, far, far],
+        out_specs=[far, far, vmem, far, vmem, far, far, far, far],
         scratch_shapes=list(kernel_scratch(sz).values()),
         compiler_params=pltpu.CompilerParams(
             collective_id=0, has_side_effects=True, vmem_limit_bytes=66584576
@@ -1502,10 +1532,6 @@
 
 
 def kernel_path(sz, latents, conditioning, w_mod, w_qkv, w_out, w_fc1, w_fc2, biases, out_grad):
-    more = sz.padded_rows - sz.rows
-    gap = sz.joined - 3 * sz.part
-    part, seq, pad, rows = sz.part, sz.seq, sz.padded_rows, sz.rows
-    qkv_blocks, fc1_blocks = column_blocks(seq, sz.dp, w_qkv, w_fc1, sz.units)
     output, grad_tokens, grad_cond, sums_mod, small, sums_qkv, sums_out, sums_fc1, sums_fc2 = (
         run_kernel(
             sz,
@@ -1514,32 +1540,85 @@
             conditioning,
             jnp.concatenate(biases).reshape(1, -1),
             w_mod,
-            jnp.pad(qkv_blocks, ((0, 0), (0, more), (0, gap))),
-            jnp.pad(fc1_blocks, ((0, 0), (0, more), (0, 0))),
-            jnp.pad(w_out, ((0, more), (0, 0))),
+            w_qkv,
+            w_fc1,
+            w_out,
             w_fc2,
         )
     )
 
-    def spread(sums, columns, groups):
-        sums = sums.reshape(seq, pad, -1)[:, :rows, :columns].astype(F32)
-        return sums.reshape(seq, rows, groups, -1).transpose(1, 2, 0, 3).reshape(rows, -1)
-
-    return (
-        output,
-        grad_tokens,
-        grad_cond,
-        sums_mod[:rows],
-        small[4, : 6 * rows],
-        spread(sums_qkv, 3 * part, 3),
-        small[2, : 2 * rows],
-        sums_out[:rows],
-        small[0, :rows],
-        spread(sums_fc1, sz.hidden, sz.dp),
-        small[3, : sz.units],
-        sums_fc2,
-        small[1, :rows],
-    )
+    return arrange(
+        sz, output, grad_tokens, sums_fc2, grad_cond, sums_mod, sums_qkv, sums_out, sums_fc1, small
+    )
+
+
+def arrange_kernel(sz, *refs):
+    output, grad_tokens, fc2, cond, mod, qkv, out, fc1, small = refs[:9]
+    (to_output, to_tokens, to_cond, to_mod, to_b_mod, to_qkv, to_b_qv) = refs[9:16]
+    (to_out, to_b_out, to_fc1, to_b_fc1, to_fc2, to_b_fc2, sems) = refs[16:23]
+    near = refs[23:]
+    pairs = list(zip((cond, mod, qkv, out, fc1, small), near))
+    pairs += [(output, to_output), (grad_tokens, to_tokens), (fc2, to_fc2)]
+    moves = [
+        pltpu.make_async_copy(source, target, sems.at[index])
+        for index, (source, target) in enumerate(pairs)
+    ]
+    for move in moves:
+        move.start()
+    for move in moves[: len(near)]:
+        move.wait()
+    cond, mod, qkv, out, fc1, small = near
+    rows, pad, seq = sz.rows, sz.padded_rows, sz.seq
+
+    def join(source, groups, size):
+        pieces = [
+            source[position * pad : (position + 1) * pad, group * size : (group + 1) * size]
+            for group in range(groups)
+            for position in range(seq)
+        ]
+        return jnp.concatenate([piece.astype(F32) for piece in pieces], axis=1)[:rows, :]
+
+    to_cond[...] = cond[...]
+    to_mod[...] = mod[:rows, :]
+    to_out[...] = out[:rows, :]
+    to_qkv[...] = join(qkv, 3, sz.part)
+    to_fc1[...] = join(fc1, sz.dp, sz.units)
+    for index, target in enumerate((to_b_out, to_b_fc2, to_b_qv, to_b_fc1, to_b_mod)):
+        target[...] = small[index : index + 1, : target.shape[1]]
+    for move in moves[len(near) :]:
+        move.wait()
+
+
+def arrange(sz, output, grad_tokens, fc2, cond, mod, qkv, out, fc1, small):
+    vmem = pl.BlockSpec(memory_space=pltpu.VMEM)
+    far = pl.BlockSpec(memory_space=pl.ANY)
+    low = lambda *shape: jax.ShapeDtypeStruct(shape, BF16)
+    full = lambda *shape: jax.ShapeDtypeStruct(shape, F32)
+    rows, width, hidden = sz.rows, sz.width, sz.hidden * sz.seq
+    results = pl.pallas_call(
+        partial(arrange_kernel, sz),
+        out_shape=[
+            low(*output.shape),
+            low(*output.shape),
+            low(sz.count, width),
+            full(rows, 6 * width),
+            full(1, 6 * rows),
+            full(rows, 3 * width),
+            full(1, 2 * rows),
+            full(rows, width),
+            full(1, rows),
+            full(rows, hidden),
+            full(1, sz.units),
+            full(sz.units, width),
+            full(1, rows),
+        ],
+        in_specs=[far] * 9,
+        out_specs=[far, far] + [vmem] * 9 + [far, vmem],
+        scratch_shapes=[pltpu.SemaphoreType.DMA((9,))]
+        + [pltpu.VMEM(item.shape, item.dtype) for item in (cond, mod, qkv, out, fc1, small)],
+        compiler_params=pltpu.CompilerParams(vmem_limit_bytes=33554432),
+    )(output, grad_tokens, fc2, cond, mod, qkv, out, fc1, small)
+    return tuple(item.reshape(-1) if item.shape[0] == 1 else item for item in results)
 
 
 def column_blocks(seq, dp, w_qkv, w_fc1, units):

time: 265 us -> 249 us (0.940)
  local copies, waits for them, and re-layouts: 21.8 us -> 12.8 us
  Pallas kernels: 239 us -> 234 us
    reshape x14 -> x0, local copies, waits for them, and re-layouts: 8.78 us -> none  [the longest x6 5.19 us: spread(): sums.reshape(seq, rows, groups, -1).transpose(1, 2, 0, 3).reshape(rows, -1)]
    pallas_call x1, Pallas kernels: 239 us -> 230 us  [run_kernel(): pl.pallas_call(partial(block_kernel, sz), out_shape=outputs, in_specs=[vm...]
    unnamed x35 -> x18, local copies, waits for them, and re-layouts: 4.43 us -> 8.76 us
    pallas_call x0 -> x1, Pallas kernels: none -> 3.63 us  [arrange(): pl.pallas_call(partial(arrange_kernel, sz), out_shape=[low(*output.shape)...]
    concatenate x1, local copies, waits for them, and re-layouts: 0.1 us -> 3.43 us  [kernel_path(): jnp.concatenate(biases).reshape(1, -1)]
    slice x3 -> x0, local copies, waits for them, and re-layouts: 3.21 us -> none  [the longest x1 1.26 us: kernel_path(): small[4, :6 * rows]]
where the time goes in v4:
time: 249 us; the launch traced here: 248 us
  Pallas kernels  234 us (94%)
  local copies, waits for them, and re-layouts  12.8 us (5%)
    pallas_call x1, Pallas kernels, run_kernel(): pl.pallas_call(partial(block_kernel, sz), out_shape=outputs, in_specs=[vm...  230 us
    unnamed x18, local copies, waits for them, and re-layouts  8.76 us

profile of v4, /device:TPU:4, one launch (start us, length us, event | category | flops | bytes accessed | tf_op | source)
XLA Modules:
  0.0 247.6 jit_solution(2214568846995838490)
XLA Ops:
  0.6 3.4 %concatenate.3 = bf16[504]{0:T(512)(128)(2,1)S(1)} concatenate(bf16[216]{0:T(256)(128)(2,1)} %param.16, bf16[72]{0:T(256)(128)(2,1)} %param.18, bf16[36]{0:T(256)(128)(2,1)} %param.20, bf16[144]{0:T(256)(128)(2,1)} %param.22, bf16[36]{0:T(256)(128)(2,1)} %param.24), dimensions={0} | concatenate | bytes 2016 | tf_op jit(solution)/shard_map/concatenate | solution.py:1541
  4.1 0.6 reshape.44.refs_3_
  4.7 230.3 %shard_map.228 = (bf16[2,128,1152]{2,1,0:T(8,128)(2,1)}, bf16[2,128,1152]{2,1,0:T(8,128)(2,1)}, bf16[2,1152]{1,0:T(2,128)(2,1)}, f32[40,6912]{1,0:T(8,128)}, f32...) custom-call(bf16[2,128,1152]{2,1,0:T(8,128)(2,1)} %refs_0_.1, ...), custom_call_target="tpu_custom_call" | custom-call | tf_op jit(solution)/shard_map/pallas_call | solution.py:1391
  235.0 0.0 copy-start
  235.0 1.2 copy-done
  236.2 0.0 copy-start.1
  236.2 1.1 copy-done.1
  237.3 0.0 copy-start.2
  237.3 1.1 copy-done.2
  238.4 0.0 copy-start.3
  238.4 1.1 copy-done.3
  239.5 0.0 copy-start.4
  239.5 1.0 copy-done.4
  240.5 0.0 copy-start.5
  240.5 1.0 copy-done.5
  241.4 0.0 copy-start.6
  241.4 0.9 copy-done.6
  242.4 0.0 copy-start.7
  242.4 0.7 copy-done.7
  243.1 0.0 copy-start.8
  243.1 0.7 copy-done.8
  243.8 3.6 %shard_map.229 = (bf16[2,128,1152]{2,1,0:T(8,128)(2,1)}, bf16[2,128,1152]{2,1,0:T(8,128)(2,1)}, bf16[2,1152]{1,0:T(2,128)(2,1)}, f32[36,6912]{1,0:T(8,128)}, f32...) custom-call(bf16[2,128,1152]{2,1,0:T(8,128)(2,1)S(1)} %copy-done.2, ...), custom_call_target="tpu_custom_call" | custom-call | tf_op jit(solution)/shard_map/pallas_call | solution.py:1598
Async XLA Ops:
  235.0 1.2 copy-start
  236.2 1.1 copy-start.1
  237.3 1.1 copy-start.2
  238.4 1.1 copy-start.3
  239.5 1.0 copy-start.4
  240.5 1.0 copy-start.5
  241.4 0.9 copy-start.6
  242.4 0.7 copy-start.7
  243.1 0.7 copy-start.8

commit v5 on v4

--- a/solution.py
+++ b/solution.py
@@ -255,8 +255,8 @@
         pending.extend(copies)
 
     class GatherWeights:
-        def __init__(self, ref, chunk):
-            self.ref, self.chunk = ref, chunk
+        def __init__(self, ref, chunk, direct=False):
+            self.ref, self.chunk, self.direct = ref, chunk, direct
 
         def slot(self, dp):
             return rows_of(self.ref, dp * self.chunk, self.chunk)
@@ -267,7 +267,10 @@
             self.along = [send(mine, own, device_flip(mask)) for mask in (2, 1)]
             self.arrival = r.recv_sems.at[used[0]]
             self.last = copy_to(mine, own, device_flip(3))
-            pl.when(inner)(self.last.start)
+            if self.direct:
+                self.last.start()
+            else:
+                pl.when(inner)(self.last.start)
             self.across, self.passed = [], 0
 
         def push_across(self, source=None):
@@ -284,7 +287,7 @@
                 (self.along + [self.last])[self.passed].wait_recv()
                 self.passed += 1
                 came = self.slot(z_flip(mask) * 2 + x_me)
-                if mask == 2:
+                if mask == 2 and not self.direct:
                     self.relay = copy_to(came, came, device_flip(1), self.arrival)
                     pl.when(inner)(self.relay.start)
                 self.across.append(send(came, came, device_x))
@@ -296,6 +299,9 @@
         def drain(self):
             for copy in self.along + self.across:
                 copy.wait_send()
+            if self.direct:
+                self.last.wait_send()
+                return
 
             @pl.when(inner)
             def _():
@@ -431,10 +437,8 @@
         return jnp.where(hit, values, jnp.zeros_like(values))
 
     me = dp_me * seq + s_me
-    lengths = (6 * sz.rows, 2 * sz.rows, sz.rows, sz.units, sz.rows)
-    starts = [sum(lengths[:index]) for index in range(len(lengths))]
     own_mod, own_qv, own_out, own_fc1, own_fc2 = [
-        r.bias[:, start : start + size] for start, size in zip(starts, lengths)
+        ref[...].astype(F32).reshape(1, -1) for ref in (r.b_mod, r.b_qv, r.b_out, r.b_fc1, r.b_fc2)
     ]
     devices = sz.dp * seq
     half_way = devices // 2
@@ -458,7 +462,6 @@
         lambda peer: rows_of(fc1_send, peer * pad, pad),
         lambda me: rows_of(fc1_blocks, me * pad, pad),
     )
-    lat_moves = [GatherTokens(r.lat_all, 0, r.latents.at[0])]
 
     tighten = one_hot(sz.chunk, seq * pad, sz.rows, pad, False)
     loosen = one_hot(sz.chunk, seq * pad, sz.rows, pad, True)
@@ -512,12 +515,12 @@
         copy.wait_recv()
     r.mod_send[...] = mod_part((1 - y_me) * 2 + c_me)[...] + r.mod_core[1 - y_me]
     mod_chip = send(r.mod_send, r.mod_chip, device_seq(2))
-    for latent in range(1, count):
-        lat_moves.append(GatherTokens(r.lat_all, latent, r.latents.at[latent]))
+    lat_moves = [
+        GatherTokens(r.lat_all, latent, r.latents.at[latent]) for latent in range(count)
+    ]
     mod_chip.wait_recv()
     r.mod_sum[...] = mod_part(s_me)[...] + r.mod_core[y_me] + r.mod_chip[...]
     mod_x = send(rows_of(r.mod_sum, (1 - x_me) * 8, 8), r.mod_x, device_x)
-    lat_moves[0].forward()
     gather_bias.forward(1)
     gather_qkv.forward(1)
     mod_x.wait_recv()
@@ -528,7 +531,7 @@
     og_moves = [GatherTokens(r.grad_branch, 0, r.out_grad.at[0])]
     gather_fc1.push_across()
     gather_qkv.forward()
-    for move in lat_moves[1:]:
+    for move in lat_moves:
         move.forward()
     gather_out.finish()
     mod_total = r.mod_half[...]
@@ -988,37 +991,8 @@
     pl.semaphore_wait(r.free_x, 1)
     sum_qkv.push()
     sum_fc1.forward()
-
-
-    weight_grad(r.mixed, r.grad_attended, r.out)
-
-    def loosen_out(step, carry):
-        start = pl.multiple_of(step * sz.chunk, 16)
-        spread = dot(loosen, r.out[pl.ds(start, sz.chunk), :]).astype(BF16)
-        for block in range(seq):
-            place = pl.multiple_of(block * out_wide + step * pad, 16)
-            r.out_blocks[pl.ds(place, pad), :] = spread[block * pad : (block + 1) * pad, :]
-        return carry
-
-    lax.fori_loop(0, sz.dp, loosen_out, 0)
-    out_first = [
-        send(
-            rows_of(r.out_blocks, (y * 2 + 1 - c_me) * out_wide, out_wide),
-            rows_of(r.grad_branch, y * out_wide, out_wide),
-            device_seq(1),
-        )
-        for y in range(2)
-    ]
-
-    def out_from_core(y):
-        return rows_of(r.grad_branch, y * out_wide, out_wide)[...].astype(F32)
-
-    other = rows_of(r.out_blocks, ((1 - y_me) * 2 + c_me) * out_wide, out_wide)
-    out_chip_sum = rows_of(r.modded_two, 2 * count * tokens, out_wide)
-
-    def out_half(index):
-        start, size = index * (out_wide // 2), out_wide // 2
-        return send(rows_of(other, start, size), rows_of(out_chip_sum, start, size), device_seq(2))
+    pl.semaphore_wait(r.free_z, line - 1)
+
 
     for latent in range(count):
         branch_moves[latent].finish()
@@ -1037,12 +1011,6 @@
         lax.fori_loop(0, tokens // ROWS, final_output, 0)
         slot = rows_of(r.modded_two, latent * tokens, tokens)
         far_moves.append(local(slot, r.output.at[latent]))
-    for copy in out_first:
-        copy.wait_recv()
-    other[...] = (other[...].astype(F32) + out_from_core(1 - y_me)).astype(BF16)
-    out_second = [out_half(0)]
-    pl.semaphore_wait(r.free_z, line - 1)
-    sum_qkv.forward(1)
     for latent in range(count):
         token_moves[latent].finish()
 
@@ -1092,29 +1060,58 @@
     mod_core.wait_recv()
     r.grad_chip_send[...] = r.grad_core_send[...] + r.grad_core[...]
     mod_chip = send(r.grad_chip_send, r.grad_chip, device_seq(2))
-    out_second.append(out_half(1))
+    weight_grad(r.mixed, r.grad_attended, r.out)
+
+    def loosen_out(step, carry):
+        start = pl.multiple_of(step * sz.chunk, 16)
+        spread = dot(loosen, r.out[pl.ds(start, sz.chunk), :]).astype(BF16)
+        for block in range(seq):
+            place = pl.multiple_of(block * out_wide + step * pad, 16)
+            r.out_blocks[pl.ds(place, pad), :] = spread[block * pad : (block + 1) * pad, :]
+        return carry
+
+    lax.fori_loop(0, sz.dp, loosen_out, 0)
+    out_first = [
+        send(
+            rows_of(r.out_blocks, (y * 2 + 1 - c_me) * out_wide, out_wide),
+            rows_of(r.grad_branch, y * out_wide, out_wide),
+            device_seq(1),
+        )
+        for y in range(2)
+    ]
+
+    def out_from_core(y):
+        return rows_of(r.grad_branch, y * out_wide, out_wide)[...].astype(F32)
+
+    other = rows_of(r.out_blocks, ((1 - y_me) * 2 + c_me) * out_wide, out_wide)
+    out_chip_sum = rows_of(r.modded_two, 2 * count * tokens, out_wide)
+
+    def out_half(index):
+        start, size = index * (out_wide // 2), out_wide // 2
+        return send(rows_of(other, start, size), rows_of(out_chip_sum, start, size), device_seq(2))
+
+    for copy in out_first:
+        copy.wait_recv()
+    other[...] = (other[...].astype(F32) + out_from_core(1 - y_me)).astype(BF16)
+    out_second = [out_half(0), out_half(1)]
+    mod_chip.wait_recv()
+    rows_of(r.bias_all, dp_me * 16, 16)[...] = (r.grad_chip_send[...] + r.grad_chip[...]).astype(
+        BF16
+    )
+    gather_grad = GatherWeights(r.bias_all, 16, direct=True)
+    gather_grad.push()
+    sum_qkv.forward(1)
     fc2_move.wait()
     sum_fc1.finish(fc_rows)
     fc1_own, fc1_back = return_rows(fc_rows[...], r.fc1_blocks, r.fc1_rows)
+    gather_grad.forward()
+    sum_qkv.forward(1)
     bias_x.wait_recv()
     r.bias_half[...] = r.bias_sums[...] + r.bias_x[...]
-    mod_chip.wait_recv()
-    rows_of(r.bias_all, dp_me * 16, 16)[...] = (r.grad_chip_send[...] + r.grad_chip[...]).astype(
-        BF16
-    )
-    gather_grad = GatherWeights(r.bias_all, 16)
-    gather_grad.push()
     room_z = r.mod_z.at[:, :, pl.ds(0, width)]
     bias_z = [send(r.bias_half, room_z.at[step], device_z(step)) for step in range(1, line)]
-    gather_grad.forward()
+    pending.extend([mod_core, bias_x, mod_chip] + bias_z)
     sum_qkv.forward(1)
-    pending.extend([mod_core, bias_x, mod_chip] + bias_z)
-    bias_total = r.bias_half[...]
-    for copy, step in zip(bias_z, range(1, line)):
-        copy.wait_recv()
-        bias_total = bias_total + room_z[step]
-    r.bias_line[...] = bias_total
-    bias_core = send(r.bias_line, r.bias_core, device_seq(1))
 
     gather_grad.finish()
     all_grads = r.bias_all[...]
@@ -1156,15 +1153,6 @@
     r.cond_sides[0] = hits[0]
     r.cond_sides[1] = hits[1]
     cond_x = send(r.cond_sides.at[1 - x_me], r.cond_x, device_x)
-    bias_core.wait_recv()
-    r.bias_pair[...] = r.bias_line[...] + r.bias_core[...]
-    bias_chip = send(r.bias_pair, r.bias_chip, device_seq(2))
-    comp_rows = iota((8, rows), 0) == (iota((8, rows), 1) & 7)
-    mod_bias = dot(jnp.where(comp_rows, 1.0, 0.0).astype(BF16), all_grads)
-    cond_x.wait_recv()
-    r.cond_half[...] = r.cond_sides[x_me] + r.cond_x[...]
-    cond_z = [send(r.cond_half, r.cond_z.at[step], device_z(step)) for step in range(1, line)]
-    sum_qkv.forward(1)
     for copy in out_second:
         copy.wait_recv()
     mine = out_mine[...].astype(F32) + out_from_core(y_me)
@@ -1172,16 +1160,26 @@
     pending.extend(out_first + out_second)
     sum_out = SumWeights(out_mine, pad, r.across_out, r.along_out, width)
     sum_out.push()
+    bias_total = r.bias_half[...]
+    for copy, step in zip(bias_z, range(1, line)):
+        copy.wait_recv()
+        bias_total = bias_total + room_z[step]
+    r.bias_line[...] = bias_total
+    bias_core = send(r.bias_line, r.bias_core, device_seq(1))
+    cond_x.wait_recv()
+    r.cond_half[...] = r.cond_sides[x_me] + r.cond_x[...]
+    cond_z = [send(r.cond_half, r.cond_z.at[step], device_z(step)) for step in range(1, line)]
+    bias_core.wait_recv()
+    r.bias_pair[...] = r.bias_line[...] + r.bias_core[...]
+    bias_chip = send(r.bias_pair, r.bias_chip, device_seq(2))
+    comp_rows = iota((8, rows), 0) == (iota((8, rows), 1) & 7)
+    mod_bias = dot(jnp.where(comp_rows, 1.0, 0.0).astype(BF16), all_grads)
     cond_total = r.cond_half[...]
     for copy, step in zip(cond_z, range(1, line)):
         copy.wait_recv()
         cond_total = cond_total + r.cond_z[step]
     r.cond_line[...] = cond_total
-    cond_core = send(r.cond_line, r.cond_core, device_seq(1))
-    sum_qkv.forward()
-    cond_core.wait_recv()
-    r.cond_pair[...] = r.cond_line[...] + r.cond_core[...]
-    cond_chip = send(r.cond_pair, r.cond_chip, device_seq(2))
+    cond_seq = exchange(lambda peer: r.cond_line, lambda me: r.cond_seq.at[me])
     for comp in range(6):
         chosen = jnp.where(comp_of == comp, cond_spread, 0.0).astype(BF16)
         place_rows = rows_of(r.grad_middle, comp * mod_rows, mod_rows)
@@ -1226,8 +1224,10 @@
     sum_out.finish(out_rows)
     far_moves.append(local(out_rows, r.out_out))
     gather_grad.drain()
-    cond_chip.wait_recv()
-    cond_full = r.cond_pair[...] + r.cond_chip[...]
+    cond_full = r.cond_line[...]
+    for copy, mask in zip(cond_seq, (1, 2, 3)):
+        copy.wait_recv()
+        cond_full = cond_full + r.cond_seq[seq_peer(mask)]
     picked = [
         jnp.sum(
             jnp.where(comp_row == z_me * count + latent, cond_full, 0.0), axis=0, keepdims=True
@@ -1236,7 +1236,7 @@
     ]
     slope = gate_cond * (1.0 + cond * (1.0 - gate_cond))
     r.cond_grad[...] = (jnp.concatenate(picked, axis=0) * slope).astype(BF16)
-    pending.extend([bias_core, bias_chip, cond_x, cond_core, cond_chip] + cond_z)
+    pending.extend([bias_core, bias_chip, cond_x] + cond_seq + cond_z)
     for own, moves in ((fc1_own, fc1_back), (qkv_own, qkv_back)):
         own.wait()
         settle(moves)
@@ -1252,7 +1252,11 @@
     latents: object
     out_grad: object
     conditioning: object
-    bias: object
+    b_mod: object
+    b_qv: object
+    b_out: object
+    b_fc1: object
+    b_fc2: object
     w_mod: object
     qkv_src: object
     fc1_src: object
@@ -1356,9 +1360,7 @@
         cond_half=full(8, width),
         cond_z=full(sz.line, 8, width),
         cond_line=full(8, width),
-        cond_core=full(8, width),
-        cond_pair=full(8, width),
-        cond_chip=full(8, width),
+        cond_seq=full(seq, 8, width),
         send_sems=pltpu.SemaphoreType.DMA((200,)),
         recv_sems=pltpu.SemaphoreType.DMA((200,)),
         free_x=pltpu.SemaphoreType.REGULAR,
@@ -1391,7 +1393,7 @@
     return pl.pallas_call(
         partial(block_kernel, sz),
         out_shape=outputs,
-        in_specs=[vmem] * 5 + [far] * 4,
+        in_specs=[vmem] * 9 + [far] * 4,
         out_specs=[far, far, vmem, far, vmem, far, far, far, far],
         scratch_shapes=list(kernel_scratch(sz).values()),
         compiler_params=pltpu.CompilerParams(
@@ -1538,7 +1540,7 @@
             latents,
             out_grad,
             conditioning,
-            jnp.concatenate(biases).reshape(1, -1),
+            *biases,
             w_mod,
             w_qkv,
             w_fc1,
@@ -1557,17 +1559,23 @@
     (to_output, to_tokens, to_cond, to_mod, to_b_mod, to_qkv, to_b_qv) = refs[9:16]
     (to_out, to_b_out, to_fc1, to_b_fc1, to_fc2, to_b_fc2, sems) = refs[16:23]
     near = refs[23:]
-    pairs = list(zip((cond, mod, qkv, out, fc1, small), near))
-    pairs += [(output, to_output), (grad_tokens, to_tokens), (fc2, to_fc2)]
     moves = [
         pltpu.make_async_copy(source, target, sems.at[index])
-        for index, (source, target) in enumerate(pairs)
+        for index, (source, target) in enumerate(zip(refs[:9], near))
     ]
     for move in moves:
         move.start()
-    for move in moves[: len(near)]:
+    for move in moves:
         move.wait()
-    cond, mod, qkv, out, fc1, small = near
+    output, grad_tokens, fc2, cond, mod, qkv, out, fc1, small = near
+    moves = [
+        pltpu.make_async_copy(source, target, sems.at[index])
+        for index, (source, target) in enumerate(
+            ((output, to_output), (grad_tokens, to_tokens), (fc2, to_fc2))
+        )
+    ]
+    for move in moves:
+        move.start()
     rows, pad, seq = sz.rows, sz.padded_rows, sz.seq
 
     def join(source, groups, size):
@@ -1585,7 +1593,7 @@
     to_fc1[...] = join(fc1, sz.dp, sz.units)
     for index, target in enumerate((to_b_out, to_b_fc2, to_b_qv, to_b_fc1, to_b_mod)):
         target[...] = small[index : index + 1, : target.shape[1]]
-    for move in moves[len(near) :]:
+    for move in moves:
         move.wait()
 
 
@@ -1615,8 +1623,11 @@
         in_specs=[far] * 9,
         out_specs=[far, far] + [vmem] * 9 + [far, vmem],
         scratch_shapes=[pltpu.SemaphoreType.DMA((9,))]
-        + [pltpu.VMEM(item.shape, item.dtype) for item in (cond, mod, qkv, out, fc1, small)],
-        compiler_params=pltpu.CompilerParams(vmem_limit_bytes=33554432),
+        + [
+            pltpu.VMEM(item.shape, item.dtype)
+            for item in (output, grad_tokens, fc2, cond, mod, qkv, out, fc1, small)
+        ],
+        compiler_params=pltpu.CompilerParams(vmem_limit_bytes=66584576),
     )(output, grad_tokens, fc2, cond, mod, qkv, out, fc1, small)
     return tuple(item.reshape(-1) if item.shape[0] == 1 else item for item in results)
 

time: 249 us -> 234 us (0.940)
  local copies, waits for them, and re-layouts: 12.8 us -> 0 us
  Pallas kernels: 234 us -> 230 us
    unnamed x18 -> x0, local copies, waits for them, and re-layouts: 8.76 us -> none
    pallas_call x1, Pallas kernels: 230 us -> 226 us  [run_kernel(): pl.pallas_call(partial(block_kernel, sz), out_shape=outputs, in_specs=[vm...]
    concatenate x1 -> x0, local copies, waits for them, and re-layouts: 3.43 us -> none  [kernel_path(): jnp.concatenate(biases).reshape(1, -1)]
where the time goes in v5:
time: 234 us; the launch traced here: 231 us
  Pallas kernels  230 us (98%)
    pallas_call x1, Pallas kernels, run_kernel(): pl.pallas_call(partial(block_kernel, sz), out_shape=outputs, in_specs=[vm...  226 us
    pallas_call x1, Pallas kernels, arrange(): pl.pallas_call(partial(arrange_kernel, sz), out_shape=[low(*output.shape)...  4.88 us

profile of v5, /device:TPU:4, one launch (start us, length us, event | category | flops | bytes accessed | tf_op | source)
XLA Modules:
  0.0 231.3 jit_solution(10443224194717467827)
XLA Ops:
  0.6 225.5 %shard_map.228 = (bf16[2,128,1152]{2,1,0:T(8,128)(2,1)}, bf16[2,128,1152]{2,1,0:T(8,128)(2,1)}, bf16[2,1152]{1,0:T(2,128)(2,1)}, f32[40,6912]{1,0:T(8,128)}, f32...) custom-call(bf16[2,128,1152]{2,1,0:T(8,128)(2,1)} %refs_0_.1, ...), custom_call_target="tpu_custom_call" | custom-call | tf_op jit(solution)/shard_map/pallas_call | solution.py:1393
  226.2 4.9 %shard_map.229 = (bf16[2,128,1152]{2,1,0:T(8,128)(2,1)}, bf16[2,128,1152]{2,1,0:T(8,128)(2,1)}, bf16[2,1152]{1,0:T(2,128)(2,1)}, f32[36,6912]{1,0:T(8,128)}, f32...) custom-call(bf16[2,128,1152]{2,1,0:T(8,128)(2,1)} %get-tuple-element, ...), custom_call_target="tpu_custom_call" | custom-call | tf_op jit(solution)/shard_map/pallas_call | solution.py:1606

commit v6 on v5

--- a/solution.py
+++ b/solution.py
@@ -45,7 +45,7 @@
 MESH = pl.DeviceIdType.MESH
 ROOT = HEAD_DIM ** (-0.5)
 LANES = 128
-ROWS = 32
+ROWS = 64
 
 
 class Sizes:
@@ -641,16 +641,14 @@
     def attend(index, carry):
         keys, values = r.k_heads[index], r.v_heads[index]
 
-        def rows(step, carry):
-            here = pl.ds(pl.multiple_of(step * half, half), half)
+        for row in range(0, length, half):
+            here = slice(row, row + half)
             scores = dot_right_t(r.q_heads[index, here, :], keys) * ROOT
             expon = jnp.exp(scores - jnp.max(scores, axis=-1, keepdims=True))
             soft = (expon * (1.0 / jnp.sum(expon, axis=-1, keepdims=True))).astype(BF16)
             r.soft[index, here, :] = soft
             r.o_heads[index, here, :] = dot(soft, values).astype(BF16)
-            return carry
-
-        return lax.fori_loop(0, 2, rows, carry)
+        return carry
 
     mixed_moves = []
     for latent in range(count):
@@ -837,6 +835,19 @@
     weight_grad(r.modded_two, r.grad_hidden, r.fc1)
     sum_fc1 = SumWeights(r.fc1, sz.chunk, r.across_a, r.along_a, sz.hidden)
     sum_fc1.push()
+
+    gather_fc2.drain()
+    branch_moves = []
+    for latent in range(count):
+
+        def branch_out(step, carry, latent=latent):
+            start = pl.multiple_of(latent * length + step * tile, tile)
+            sums = dot(r.lat_all[pl.ds(start, tile), :], r.fc2[...])
+            r.lat_all[pl.ds(start, tile), :] = sums.astype(BF16)
+            return carry
+
+        lax.fori_loop(0, per_latent, branch_out, 0)
+        branch_moves.append(SumTokens(r.lat_all, 1, latent))
 
     grad_mod = r.grad_mod
     grad_mod[...] = jnp.zeros_like(grad_mod)
@@ -886,19 +897,8 @@
             )
         )
 
-    gather_fc2.drain()
-    branch_moves = []
-    for latent in range(count):
-
-        def branch_out(step, carry, latent=latent):
-            start = pl.multiple_of(latent * length + step * tile, tile)
-            sums = dot(r.lat_all[pl.ds(start, tile), :], r.fc2[...])
-            r.lat_all[pl.ds(start, tile), :] = sums.astype(BF16)
-            return carry
-
-        lax.fori_loop(0, per_latent, branch_out, 0)
-        branch_moves.append(SumTokens(r.lat_all, 1, latent))
     sum_fc2.forward()
+    weight_grad(r.mixed, r.grad_attended, r.out)
 
     for move in branch_moves:
         move.forward()
@@ -908,15 +908,12 @@
         incoming = r.o_heads[index]
         r.v_heads[index] = dot_left_t(r.soft[index], incoming).astype(BF16)
 
-        def rows(step, carry):
-            here = pl.ds(pl.multiple_of(step * half, half), half)
+        for row in range(0, length, half):
+            here = slice(row, row + half)
             soft = r.soft[index, here, :].astype(F32)
             grad_soft = dot_right_t(r.o_heads[index, here, :], values)
             delta = jnp.sum(soft * grad_soft, axis=-1, keepdims=True)
             r.soft[index, here, :] = (soft * (grad_soft - delta)).astype(BF16)
-            return carry
-
-        lax.fori_loop(0, 2, rows, 0)
         r.q_heads[index] = (dot(r.soft[index], keys) * ROOT).astype(BF16)
         r.k_heads[index] = (dot_left_t(r.soft[index], queries) * ROOT).astype(BF16)
         return carry
@@ -1060,7 +1057,6 @@
     mod_core.wait_recv()
     r.grad_chip_send[...] = r.grad_core_send[...] + r.grad_core[...]
     mod_chip = send(r.grad_chip_send, r.grad_chip, device_seq(2))
-    weight_grad(r.mixed, r.grad_attended, r.out)
 
     def loosen_out(step, carry):
         start = pl.multiple_of(step * sz.chunk, 16)
@@ -1217,9 +1213,9 @@
         axis=0,
     )
     qkv_total = fc_rows.at[:, pl.ds(0, sz.joined)]
+    sum_out.forward()
     sum_qkv.finish(qkv_total)
     qkv_own, qkv_back = return_rows(qkv_total[...], r.qkv_blocks, r.qkv_rows)
-    sum_out.forward()
     out_rows = rows_of(r.middle, 0, pad)
     sum_out.finish(out_rows)
     far_moves.append(local(out_rows, r.out_out))

time: 234 us -> 233 us (level)
  no operation moved by 1% of the time
where the time goes in v6:
time: 233 us; the launch traced here: 232 us
  Pallas kernels  231 us (99%)
    pallas_call x1, Pallas kernels, run_kernel(): pl.pallas_call(partial(block_kernel, sz), out_shape=outputs, in_specs=[vm...  226 us
    pallas_call x1, Pallas kernels, arrange(): pl.pallas_call(partial(arrange_kernel, sz), out_shape=[low(*output.shape)...  4.88 us

profile of v6, /device:TPU:4, one launch (start us, length us, event | category | flops | bytes accessed | tf_op | source)
XLA Modules:
  0.0 231.6 jit_solution(1919883730354391283)
XLA Ops:
  0.6 225.9 %shard_map.228 = (bf16[2,128,1152]{2,1,0:T(8,128)(2,1)}, bf16[2,128,1152]{2,1,0:T(8,128)(2,1)}, bf16[2,1152]{1,0:T(2,128)(2,1)}, f32[40,6912]{1,0:T(8,128)}, f32...) custom-call(bf16[2,128,1152]{2,1,0:T(8,128)(2,1)} %refs_0_.1, ...), custom_call_target="tpu_custom_call" | custom-call | tf_op jit(solution)/shard_map/pallas_call | solution.py:1389
  226.6 4.9 %shard_map.229 = (bf16[2,128,1152]{2,1,0:T(8,128)(2,1)}, bf16[2,128,1152]{2,1,0:T(8,128)(2,1)}, bf16[2,1152]{1,0:T(2,128)(2,1)}, f32[36,6912]{1,0:T(8,128)}, f32...) custom-call(bf16[2,128,1152]{2,1,0:T(8,128)(2,1)} %get-tuple-element, ...), custom_call_target="tpu_custom_call" | custom-call | tf_op jit(solution)/shard_map/pallas_call | solution.py:1602
